TPU v7x, 128 devices: a whole 4x4x4 slice. The times are simulated.
128 devices in a mesh: wide: 32 (over z_hi, y, x), narrow: 4 (over z_lo, core).
Axes of the slice: x: 4, y: 4, z: 4 (z_hi: 2, z_lo: 2; z = z_hi * 2 + z_lo), core: 2. Of those that a mesh axis runs over, the one named last changes fastest.
Arguments:
- tokens: bfloat16 [32768, 768], P('wide'), may hold values from -6 to 6
- cotangent: bfloat16 [32768, 768], P('wide'), may hold values from -6 to 6
- seg_ids: int32 [32, 1024], P('wide'), may hold values from 0 to 23, never falling along the last dimension, each value on 1 to 256 neighbouring positions
- pad_len: int32 [32], P('wide'), may hold values from 0 to 255
- qkv_weight: bfloat16 [3, 768, 768], P(None, None, 'narrow'), may hold values from -0.21875 to 0.21875
- query_gain: float32 [768], P('narrow'), may hold values from 0.1 to 1.9
- key_gain: float32 [768], P('narrow'), may hold values from 0.1 to 1.9
- out_weight: bfloat16 [768, 768], P('narrow'), may hold values from -0.625 to 0.625
- up_weight: bfloat16 [768, 3072], P(None, 'narrow'), may hold values from -0.21875 to 0.21875
- down_weight: bfloat16 [3072, 768], P('narrow'), may hold values from -0.21875 to 0.21875
- attn_gain: float32 [768], replicated, may hold values from 0.1 to 1.9
- attn_shift: float32 [768], replicated, may hold values from -3 to 3
- mlp_gain: float32 [768], replicated, may hold values from 0.1 to 1.9
- mlp_shift: float32 [768], replicated, may hold values from -3 to 3
Outputs:
- layer_out: bfloat16 [32768, 768], P('wide')
- grad_tokens: bfloat16 [32768, 768], P('wide')
- grad_qkv: float32 [3, 768, 768], P(None, None, 'narrow')
- grad_query_gain: float32 [768], P('narrow')
- grad_key_gain: float32 [768], P('narrow')
- grad_out_weight: float32 [768, 768], P('narrow')
- grad_up: float32 [768, 3072], P(None, 'narrow')
- grad_down: float32 [3072, 768], P('narrow')
- grad_attn_gain: float32 [768], replicated
- grad_attn_shift: float32 [768], replicated
- grad_mlp_gain: float32 [768], replicated
- grad_mlp_shift: float32 [768], replicated
Inputs may be any that keep to these rules, and one draw needn't show every extreme that they name: `seg_ids`: within each sequence the image numbers never fall, each image has 1 to 256 patches and some image has exactly 256.
All inputs are finite; a program needn't handle non-finite values.
Results may differ from a plain program's by a relative error of at most 0.03.
Values may be sent and summed in bfloat16 or wider, within the bound.
A program may use at most 128 MiB of HBM per device.

v0:
```python
import jax
import jax.numpy as jnp
from jax import lax
from jax.sharding import PartitionSpec as P

HEAD_DIM = 64


masked_score = -1e30


def layer_norm(values, gain, shift):
    centre = values - jnp.mean(values, axis=-1, keepdims=True)
    spread = jnp.mean(centre * centre, axis=-1, keepdims=True)
    return centre * lax.rsqrt(spread + 1e-06) * gain + shift


def head_norm(values, gain, heads):
    count = values.shape[0]
    shaped = values.reshape(count, heads, -1)
    centre = shaped - jnp.mean(shaped, axis=-1, keepdims=True)
    spread = jnp.mean(centre * centre, axis=-1, keepdims=True)
    normed = centre * lax.rsqrt(spread + 1e-06) * gain.reshape(heads, -1)
    return normed.reshape(count, -1)


def allowed_keys(segment, valid, start, block):
    length = segment.shape[0]
    places = jnp.arange(length, dtype=jnp.int32)
    query_seg = lax.dynamic_slice_in_dim(segment, start, block)
    query_pos = start + jnp.arange(block, dtype=jnp.int32)
    same = (query_seg[:, None] == segment[None, :]) & valid[None, :]
    return same | (query_pos[:, None] == places[None, :])


def attend_forward(queries, keys, values, segment, valid, heads):
    length, width = queries.shape
    block = min(512, length)
    scale = (width // heads) ** (-0.5)
    key_heads = keys.reshape(length, heads, -1)
    value_heads = values.reshape(length, heads, -1)
    query_blocks = queries.reshape(length // block, block, heads, -1)
    starts = jnp.arange(length // block, dtype=jnp.int32) * block

    def one_block(pair):
        query_block, start = pair
        scores = (
            jnp.einsum("qhd,khd->hqk", query_block, key_heads, preferred_element_type=jnp.float32)
            * scale
        )
        scores = jnp.where(allowed_keys(segment, valid, start, block)[None], scores, masked_score)
        top = jnp.max(scores, axis=-1, keepdims=True)
        weights = jnp.exp(scores - top)
        total = jnp.sum(weights, axis=-1, keepdims=True)
        probs = (weights / total).astype(jnp.bfloat16)
        mixed = jnp.einsum("hqk,khd->qhd", probs, value_heads, preferred_element_type=jnp.float32)
        return (mixed.reshape(block, width), top[..., 0] + jnp.log(total[..., 0]))

    mixed, log_sums = lax.map(one_block, (query_blocks, starts))
    return (mixed.reshape(length, width), log_sums)


def attend_backward(queries, keys, values, grad_mixed, log_sums, segment, valid, heads):
    length, width = queries.shape
    block = min(512, length)
    scale = (width // heads) ** (-0.5)
    key_heads = keys.reshape(length, heads, -1)
    value_heads = values.reshape(length, heads, -1)
    query_blocks = queries.reshape(length // block, block, heads, -1)
    grad_blocks = grad_mixed.reshape(length // block, block, heads, -1)
    starts = jnp.arange(length // block, dtype=jnp.int32) * block

    def one_block(carry, item):
        grad_keys, grad_values = carry
        query_block, grad_block, log_sum, start = item
        scores = (
            jnp.einsum("qhd,khd->hqk", query_block, key_heads, preferred_element_type=jnp.float32)
            * scale
        )
        scores = jnp.where(allowed_keys(segment, valid, start, block)[None], scores, masked_score)
        probs = jnp.exp(scores - log_sum[..., None])
        grad_probs = jnp.einsum(
            "qhd,khd->hqk", grad_block, value_heads, preferred_element_type=jnp.float32
        )
        grad_scores = probs * (grad_probs - jnp.sum(grad_probs * probs, axis=-1, keepdims=True))
        rounded = grad_scores.astype(jnp.bfloat16)
        grad_query = (
            jnp.einsum("hqk,khd->qhd", rounded, key_heads, preferred_element_type=jnp.float32)
            * scale
        )
        grad_keys = (
            grad_keys
            + jnp.einsum("hqk,qhd->khd", rounded, query_block, preferred_element_type=jnp.float32)
            * scale
        )
        grad_values = grad_values + jnp.einsum(
            "hqk,qhd->khd",
            probs.astype(jnp.bfloat16),
            grad_block,
            preferred_element_type=jnp.float32,
        )
        return ((grad_keys, grad_values), grad_query.reshape(block, width))

    zeros = jnp.zeros((length, heads, width // heads), jnp.float32)
    (grad_keys, grad_values), grad_queries = lax.scan(
        one_block, (zeros, zeros), (query_blocks, grad_blocks, log_sums, starts)
    )
    return (
        grad_queries.reshape(length, width),
        grad_keys.reshape(length, width),
        grad_values.reshape(length, width),
    )


def attention_half(
    tokens_f, seg_ids, pad_len, qkv_weight, query_gain, key_gain, out_weight, attn_gain, attn_shift
):
    seqs, length = seg_ids.shape
    width = query_gain.shape[0]
    heads = width // HEAD_DIM
    normed = layer_norm(tokens_f, attn_gain, attn_shift).astype(jnp.bfloat16)
    projected = jnp.einsum("td,cde->cte", normed, qkv_weight, preferred_element_type=jnp.float32)
    queries = head_norm(projected[0], query_gain, heads).astype(jnp.bfloat16)
    keys = head_norm(projected[1], key_gain, heads).astype(jnp.bfloat16)
    values = projected[2].astype(jnp.bfloat16)
    valid = jnp.arange(length, dtype=jnp.int32)[None, :] < (length - pad_len)[:, None]

    def attention_per_sequence(item):
        query_seq, key_seq, value_seq, segment, valid_seq = item
        return attend_forward(query_seq, key_seq, value_seq, segment, valid_seq, heads)

    mixed, log_sums = lax.map(
        attention_per_sequence,
        (
            queries.reshape(seqs, length, width),
            keys.reshape(seqs, length, width),
            values.reshape(seqs, length, width),
            seg_ids,
            valid,
        ),
    )
    mixed_low = mixed.reshape(seqs * length, width).astype(jnp.bfloat16)
    partial_value = jnp.dot(mixed_low, out_weight, preferred_element_type=jnp.float32).astype(
        jnp.bfloat16
    )
    return (normed, projected, queries, keys, values, valid, mixed_low, log_sums, partial_value)


def body(
    tokens,
    cotangent,
    seg_ids,
    pad_len,
    qkv_weight,
    query_gain,
    key_gain,
    out_weight,
    up_weight,
    down_weight,
    attn_gain,
    attn_shift,
    mlp_gain,
    mlp_shift,
):
    seqs, length = seg_ids.shape
    width = query_gain.shape[0]
    heads = width // HEAD_DIM
    tokens_f = tokens.astype(jnp.float32)
    kept = attention_half(
        tokens_f,
        seg_ids,
        pad_len,
        qkv_weight,
        query_gain,
        key_gain,
        out_weight,
        attn_gain,
        attn_shift,
    )
    middle = tokens_f + lax.psum(kept[8], "narrow").astype(jnp.float32)
    normed_two = layer_norm(middle, mlp_gain, mlp_shift).astype(jnp.bfloat16)
    pre_act = jnp.dot(normed_two, up_weight, preferred_element_type=jnp.float32)
    active = jax.nn.gelu(pre_act).astype(jnp.bfloat16)
    mlp_partial = jnp.dot(active, down_weight, preferred_element_type=jnp.float32).astype(
        jnp.bfloat16
    )
    layer_out = (middle + lax.psum(mlp_partial, "narrow").astype(jnp.float32)).astype(jnp.bfloat16)
    normed, projected, queries, keys, values, valid, mixed_low, log_sums, partial_value = (
        attention_half(
            tokens_f,
            seg_ids,
            pad_len,
            qkv_weight,
            query_gain,
            key_gain,
            out_weight,
            attn_gain,
            attn_shift,
        )
    )
    middle = tokens_f + lax.psum(partial_value, "narrow").astype(jnp.float32)
    normed_two = layer_norm(middle, mlp_gain, mlp_shift).astype(jnp.bfloat16)
    pre_act = jnp.dot(normed_two, up_weight, preferred_element_type=jnp.float32)
    active = jax.nn.gelu(pre_act).astype(jnp.bfloat16)
    grad_out_f = cotangent.astype(jnp.float32)
    grad_down = jnp.einsum("tf,td->fd", active, cotangent, preferred_element_type=jnp.float32)
    grad_active = jnp.einsum(
        "td,fd->tf", cotangent, down_weight, preferred_element_type=jnp.float32
    )
    _, gelu_back = jax.vjp(jax.nn.gelu, pre_act)
    grad_pre = gelu_back(grad_active)[0].astype(jnp.bfloat16)
    grad_up = jnp.einsum("td,tf->df", normed_two, grad_pre, preferred_element_type=jnp.float32)
    grad_two_part = jnp.einsum(
        "tf,df->td", grad_pre, up_weight, preferred_element_type=jnp.float32
    ).astype(jnp.bfloat16)
    grad_normed_two = lax.psum(grad_two_part, "narrow").astype(jnp.float32)
    _, second_back = jax.vjp(layer_norm, middle, mlp_gain, mlp_shift)
    grad_middle_norm, grad_mlp_gain, grad_mlp_shift = second_back(grad_normed_two)
    grad_middle = grad_out_f + grad_middle_norm
    grad_attn = grad_middle.astype(jnp.bfloat16)
    grad_out_weight = jnp.einsum(
        "te,td->ed", mixed_low, grad_attn, preferred_element_type=jnp.float32
    )
    grad_mixed = jnp.einsum(
        "td,ed->te", grad_attn, out_weight, preferred_element_type=jnp.float32
    ).astype(jnp.bfloat16)

    def body_per_sequence(item):
        query_seq, key_seq, value_seq, grad_seq, log_seq, segment, valid_seq = item
        return attend_backward(
            query_seq, key_seq, value_seq, grad_seq, log_seq, segment, valid_seq, heads
        )

    grad_queries, grad_keys, grad_values = lax.map(
        body_per_sequence,
        (
            queries.reshape(seqs, length, width),
            keys.reshape(seqs, length, width),
            values.reshape(seqs, length, width),
            grad_mixed.reshape(seqs, length, width),
            log_sums,
            seg_ids,
            valid,
        ),
    )
    _, query_back = jax.vjp(
        lambda source, gain: head_norm(source, gain, heads), projected[0], query_gain
    )
    grad_query_raw, grad_query_gain = query_back(grad_queries.reshape(seqs * length, width))
    _, key_back = jax.vjp(
        lambda source, gain: head_norm(source, gain, heads), projected[1], key_gain
    )
    grad_key_raw, grad_key_gain = key_back(grad_keys.reshape(seqs * length, width))
    grad_proj = jnp.stack(
        [grad_query_raw, grad_key_raw, grad_values.reshape(seqs * length, width)]
    ).astype(jnp.bfloat16)
    grad_qkv = jnp.einsum("td,cte->cde", normed, grad_proj, preferred_element_type=jnp.float32)
    grad_first_part = jnp.einsum(
        "cte,cde->td", grad_proj, qkv_weight, preferred_element_type=jnp.float32
    ).astype(jnp.bfloat16)
    grad_normed = lax.psum(grad_first_part, "narrow").astype(jnp.float32)
    _, first_back = jax.vjp(layer_norm, tokens_f, attn_gain, attn_shift)
    grad_input_norm, grad_attn_gain, grad_attn_shift = first_back(grad_normed)
    grad_tokens = (grad_middle + grad_input_norm).astype(jnp.bfloat16)
    (
        grad_qkv,
        grad_query_gain,
        grad_key_gain,
        grad_out_weight,
        grad_up,
        grad_down,
        grad_attn_gain,
        grad_attn_shift,
        grad_mlp_gain,
        grad_mlp_shift,
    ) = (
        lax.psum(grad_qkv.astype(jnp.bfloat16), "wide").astype(jnp.float32),
        lax.psum(grad_query_gain.astype(jnp.bfloat16), "wide").astype(jnp.float32),
        lax.psum(grad_key_gain.astype(jnp.bfloat16), "wide").astype(jnp.float32),
        lax.psum(grad_out_weight.astype(jnp.bfloat16), "wide").astype(jnp.float32),
        lax.psum(grad_up.astype(jnp.bfloat16), "wide").astype(jnp.float32),
        lax.psum(grad_down.astype(jnp.bfloat16), "wide").astype(jnp.float32),
        lax.psum(grad_attn_gain.astype(jnp.bfloat16), "wide").astype(jnp.float32),
        lax.psum(grad_attn_shift.astype(jnp.bfloat16), "wide").astype(jnp.float32),
        lax.psum(grad_mlp_gain.astype(jnp.bfloat16), "wide").astype(jnp.float32),
        lax.psum(grad_mlp_shift.astype(jnp.bfloat16), "wide").astype(jnp.float32),
    )
    return (
        layer_out,
        grad_tokens,
        grad_qkv,
        grad_query_gain,
        grad_key_gain,
        grad_out_weight,
        grad_up,
        grad_down,
        grad_attn_gain,
        grad_attn_shift,
        grad_mlp_gain,
        grad_mlp_shift,
    )


def solution(mesh):
    placed = (
        P("wide", None),
        P("wide", None),
        P("wide", None),
        P("wide"),
        P(None, None, "narrow"),
        P("narrow"),
        P("narrow"),
        P("narrow", None),
        P(None, "narrow"),
        P("narrow", None),
        P(),
        P(),
        P(),
        P(),
    )
    return jax.shard_map(
        body,
        mesh=mesh,
        in_specs=placed,
        out_specs=(
            P("wide", None),
            P("wide", None),
            P(None, None, "narrow"),
            P("narrow"),
            P("narrow"),
            P("narrow", None),
            P(None, "narrow"),
            P("narrow", None),
            P(),
            P(),
            P(),
            P(),
        ),
        check_vma=False,
    )
```

profile of v0, /device:TPU:0, one launch (start us, length us, event | category | flops | bytes accessed | tf_op | source)
XLA Modules:
  0.0 778.0 jit_solution(5452048473937678723)
XLA Ops:
  26.9 29.9 %while.66 = (s32[]{:T(128)}, bf16[2,512,192]{1,2,0:T(8,128)(2,1)S(1)}, s32[2]{0:T(128)S(1)}, s32[1024]{0:T(1024)S(1)}, bf16[2,512,3,64]{1,3,2,0:T(8,128)(2,1)}, ...) while((s32[]{:T(128)}, ...), condition=%wide.region_9.10_spmd.clone, body=%wide.region_6.9_spmd.clone.sunk | while | flops 414190080 | bytes 15233207 | solution.py:59
  31.9 6.1 fusion.217
  38.1 3.9 fusion.218
  46.8 6.1 fusion.217
  52.9 3.9 fusion.218
  57.7 23.8 %while.67 = (s32[]{:T(128)}, bf16[2,512,192]{1,2,0:T(8,128)(2,1)S(1)}, f32[2,3,512]{2,1,0:T(4,128)}, s32[2]{0:T(128)S(1)}, s32[1024]{0:T(1024)S(1)}, /*index=5*/...) while((s32[]{:T(128)}, ...), condition=%wide.region_17.18_spmd.clone, body=%wide.region_14.17_spmd.clone.sunk | while | flops 423624704 | bytes 22714620 | solution.py:59
  87.0 4.8 fusion.156
  91.8 72.0 %all-reduce.15.cloned.1.call-done = (bf16[1024,768]{1,0:T(8,128)(2,1)}, bf16[1024,768]{1,0:T(8,128)(2,1)}) async-done(((bf16[1024,768]{1,0:T(8,128)(2,1)}, bf16[1024,768]{1,0:T(8,128)(2,1)}), (bf16[1024,768]{1,0:T(8,128)(2,1)}, bf16[1024,768]{1,0:T(8,128)(2,1)})) %all-reduce.15.cloned.1.call-update) | async-done | bytes 3145744 | tf_op jit(solution)/shard_map/psum | solution.py:180
  169.5 4.2 fusion.90
  177.7 49.8 %all-reduce.9.cloned.1.call-done = bf16[1024,768]{1,0:T(8,128)(2,1)} async-done(((bf16[1024,768]{1,0:T(8,128)(2,1)}), bf16[1024,768]{1,0:T(8,128)(2,1)}) %all-reduce.9.cloned.1.call-update) | async-done | bytes 1572880 | tf_op jit(solution)/shard_map/psum | solution.py:216
  227.5 5.0 fusion.82
  241.1 57.6 %while.68 = (s32[]{:T(128)}, f32[1024,3,64]{0,2,1:T(8,128)}, f32[1024,3,64]{0,2,1:T(8,128)}, f32[2,512,192]{1,0,2:T(2,128)}, bf16[2,512,3,64]{1,3,2,0:T(8,128)(2...) while((s32[]{:T(128)}, f32[1024,3,64]{0,2,1:T(8,128)}, ...), condition=%wide.region_26.27_spmd.clone, body=%wide.region_24.26_spmd.clone.sunk | while | flops 1033404416 | bytes 62712100 | solution.py:105
  248.3 3.8 fusion.237
  252.1 3.6 multiply_reduce_fusion.10
  261.6 8.0 %dynamic_update_slice.42 = f32[2,512,192]{1,0,2:T(2,128)} dynamic-update-slice(f32[2,512,192]{1,0,2:T(2,128)} %get-tuple-element.729, f32[1,512,192]{1,0,2:T(1,128)S(1)} %copy.75, s32[]{:T(128)S(6)} %copy.102, s32[]{:T(128)} %constant.156.clone.1..sunk.2, s32[]{:T(128)} %constant.156.clone.1..sunk.2) | dynamic-update-slice | bytes 786436 | tf_op jit(solution)/shard_map/while/body/eval_jaxpr/while/body/jit(dynamic_update_index_in_dim)/dynamic_update_slice | solution.py:59
  276.9 4.1 fusion.237
  281.0 3.6 multiply_reduce_fusion.10
  290.5 8.0 %dynamic_update_slice.42 = f32[2,512,192]{1,0,2:T(2,128)} dynamic-update-slice(f32[2,512,192]{1,0,2:T(2,128)} %get-tuple-element.729, f32[1,512,192]{1,0,2:T(1,128)S(1)} %copy.75, s32[]{:T(128)S(6)} %copy.102, s32[]{:T(128)} %constant.156.clone.1..sunk.2, s32[]{:T(128)} %constant.156.clone.1..sunk.2) | dynamic-update-slice | bytes 786436 | tf_op jit(solution)/shard_map/while/body/eval_jaxpr/while/body/jit(dynamic_update_index_in_dim)/dynamic_update_slice | solution.py:59
  304.1 6.0 convolution_convert_fusion.2
  319.0 4.5 convolution_convert_fusion.4
  344.9 49.7 %all-reduce.13.cloned.1.call-done = (bf16[1024,768]{1,0:T(8,128)(2,1)}, bf16[1024,768]{1,0:T(8,128)(2,1)}) async-done(((bf16[1024,768]{1,0:T(8,128)(2,1)}, bf16[1024,768]{1,0:T(8,128)(2,1)}), (bf16[1024,768]{1,0:T(8,128)(2,1)}, bf16[1024,768]{1,0:T(8,128)(2,1)})) %all-reduce.13.cloned.1.call-update) | async-done | bytes 3145744 | tf_op jit(solution)/shard_map/psum | solution.py:187
  400.7 98.7 %all-reduce = (bf16[192]{0:T(256)(128)(2,1)S(1)}, bf16[192]{0:T(256)(128)(2,1)S(1)}, bf16[768]{0:T(1024)(128)(2,1)S(1)}, bf16[768]{0:T(1024)(128)(2,1)S(1)}, bf1...) all-reduce(bf16[192]{0:T(256)(128)(2,1)S(1)} %multiply_reduce_fusio, ...), channel_id=1, replica_groups=mesh['wide'=32,'narrow'=4] {'wide'}, use_global_device_ids=true, to_apply=%region_36.37 | all-reduce | flops 3456 | bytes 13824 | tf_op jit(solution)/shard_map/psum | solution.py:278
  502.9 6.0 add_convert_fusion
  508.9 254.5 %all-reduce.11.cloned.1.call-done = (bf16[3,768,192]{1,2,0:T(8,128)(2,1)}, bf16[192,768]{1,0:T(8,128)(2,1)}, bf16[768,768]{1,0:T(8,128)(2,1)}, bf16[768,768]{1,0:T(8,128)(2,1)}) async-done(((bf16[3,768,192]{1,2,0:T(8,128)(2,1)}, bf16[192,768]{1,0:T(8,128)(2,1)}, bf16[768,768]{1,0:T(8,128)(2,1)}, bf16[768,768]{1,0:T(8,128)(2,1)}), (bf16[3,768,192]{1,2,0:T(8,128)(2,1)}, bf16[192,768]{1,0:T(8,128)(2,1)}, ...) | async-done | bytes 3538960 | tf_op jit(solution)/shard_map/psum | solution.py:277
  (309 shorter events, 143.3 us)
Async XLA Ops:
  7.2 161.3 %copy-start = (bf16[768,768]{1,0:T(8,128)(2,1)S(1)}, bf16[768,768]{1,0:T(8,128)(2,1)}, u32[]{:S(2)}) copy-start(bf16[768,768]{1,0:T(8,128)(2,1)} %param.28) | copy-start | bytes 3538948
  7.2 156.6 %all-reduce.15.cloned.1.call-start = ((), (), s32[]{:S(2)}) async-start(), calls=%async_computation.3 | async-start | bytes 6291456 | tf_op jit(solution)/shard_map/psum | solution.py:180
  16.2 10.7 %copy-start.51 = (f32[3,64]{1,0:T(4,128)}, f32[3,64]{1,0:T(4,128)S(1)}, u32[]{:S(2)}) copy-start(f32[3,64]{1,0:T(4,128)S(1)} %mul.452) | copy-start | bytes 2308
  16.3 10.6 %copy-start.60 = (f32[3,64]{1,0:T(4,128)}, f32[3,64]{1,0:T(4,128)S(1)}, u32[]{:S(2)}) copy-start(f32[3,64]{1,0:T(4,128)S(1)} %mul.446) | copy-start | bytes 2308
  19.0 8.0 %copy-start.23 = (s32[1,1024]{1,0:T(1,128)S(1)}, s32[1,1024]{1,0:T(1,128)}, u32[]{:S(2)}) copy-start(s32[1,1024]{1,0:T(1,128)} %param.22) | copy-start | bytes 12292
  20.2 6.7 copy-start.29
  21.4 4.5 copy-start.22
  21.4 5.4 copy-start.31
  81.5 4.9 copy-start.73
  86.4 141.1 %all-reduce.9.cloned.1.call-start = ((), (), s32[]{:S(2)}) async-start(), calls=%async_computation | async-start | bytes 3145728 | tf_op jit(solution)/shard_map/psum | solution.py:216
  177.4 217.1 %all-reduce.13.cloned.1.call-start = ((), (), s32[]{:S(2)}) async-start(), calls=%async_computation.2 | async-start | bytes 6291456 | tf_op jit(solution)/shard_map/psum | solution.py:187
  227.5 5.6 copy-start.6
  227.5 5.6 copy-start.11
  298.7 5.4 copy-start.66
  298.7 5.4 copy-start.67
  304.1 7.4 copy-start.32
  304.1 7.4 copy-start.52
  304.1 9.2 %copy-start.46 = (f32[1024,3]{0,1:T(4,128)S(1)}, f32[1024,3]{0,1:T(4,128)}, u32[]{:S(2)}) copy-start(f32[1024,3]{0,1:T(4,128)} %copy-done.45) | copy-start | bytes 36868
  304.1 9.2 %copy-start.42 = (f32[1024,3]{0,1:T(4,128)S(1)}, f32[1024,3]{0,1:T(4,128)}, u32[]{:S(2)}) copy-start(f32[1024,3]{0,1:T(4,128)} %copy-done.41) | copy-start | bytes 36868
  311.5 4.6 copy-start.39
  318.7 444.7 %all-reduce.11.cloned.1.call-start = ((), (), s32[]{:S(2)}) async-start(), calls=%async_computation.1 | async-start | bytes 7077888 | tf_op jit(solution)/shard_map/psum | solution.py:277
  319.0 4.5 copy-start.17
  344.9 53.8 %copy-start.55 = (f32[1024]{0:T(1024)S(1)}, f32[1024]{0:T(1024)}, u32[]{:S(2)}) copy-start(f32[1024]{0:T(1024)} %copy-done.54) | copy-start | bytes 12292
  763.3 4.5 copy-start.28
  (61 other events, 167.3 us)
Sparse Core Ops, SparseCore 0:
  86.5 77.2 all-reduce.14
  177.6 49.8 all-reduce.8
  318.8 75.7 all-reduce.12
  397.8 365.5 all-reduce.10
where the time goes:
time: 784 us; the launch traced here: 778 us
  waiting for transfers between devices  426 us (54%)
  blocking collectives  98.7 us (13%)
  matrix products  94.2 us (12%)
  other arithmetic  73.2 us (9%)
  local copies, waits for them, and re-layouts  56.4 us (7%)
  between operations  15.9 us (2%)
  loops' own time  12.5 us (2%)
    psum x1, waiting for transfers between devices, body(): lax.psum(grad_qkv.astype(jnp.bfloat16), 'wide').astype(jnp.float32)  254 us
    psum x1, blocking collectives, body(): lax.psum(grad_query_gain.astype(jnp.bfloat16), 'wide').astype(jnp.float32)  98.7 us
    psum x1, waiting for transfers between devices, body(): middle = tokens_f + lax.psum(kept[8], 'narrow').astype(jnp.float32)  72 us
    psum x1, waiting for transfers between devices, body(): grad_normed_two = lax.psum(grad_two_part, 'narrow').astype(jnp.float32)  49.8 us
    psum x1, waiting for transfers between devices, body(): lax.psum(mlp_partial, 'narrow').astype(jnp.float32)  49.7 us
    dynamic_update_slice x8, local copies, waits for them, and re-layouts, attend_forward(): mixed, log_sums = lax.map(one_block, (query_blocks, starts))  16.9 us
  transfers between devices with their start and end apart: 4, of which 4 were waited for; matrix products, arithmetic and copies ran while one was open for 6% of the time, Pallas kernels for 0%

commit v1 on v0

v1 whole, which is shorter than its diff:
```python
import functools

import jax
import jax.numpy as jnp
from jax import lax
from jax.experimental import pallas as pl
from jax.experimental.pallas import tpu as pltpu
from jax.sharding import PartitionSpec as P

T = 1024
D = 768
HEADS = 3
HD = 64
W = HEADS * HD
F = 768
BLK = 256
CH = T // BLK
HALF = BLK // 2
BIG = 2048.0
SC = 0.125 * 1.4426950408889634
EPS = 1e-06
GELU_A = 0.7978845608028654
GELU_B = 0.044715 * GELU_A

BF = jnp.bfloat16
F32 = jnp.float32
MESH = pl.DeviceIdType.MESH


def nn(a, b):
    return lax.dot_general(a, b, (((1,), (0,)), ((), ())), preferred_element_type=F32)


def nt(a, b):
    return lax.dot_general(a, b, (((1,), (1,)), ((), ())), preferred_element_type=F32)


def tn(a, b):
    return lax.dot_general(a, b, (((0,), (0,)), ((), ())), preferred_element_type=F32)


def at(start, size, unit):
    return pl.ds(pl.multiple_of(start, unit), size)


def chunk(b):
    return at(b * BLK, BLK, BLK)


def moments(values):
    centre = values - jnp.mean(values, axis=-1, keepdims=True)
    rstd = lax.rsqrt(jnp.mean(centre * centre, axis=-1, keepdims=True) + EPS)
    return centre * rstd, rstd


def norm_back(grad, hat, rstd):
    return rstd * (
        grad
        - jnp.mean(grad, axis=-1, keepdims=True)
        - hat * jnp.mean(grad * hat, axis=-1, keepdims=True)
    )


SCRATCH = dict(
    x=((T, D), BF),
    dy=((T, D), BF),
    wraw=((3, D, W), BF),
    wt=((3 * W, D), BF),
    wo=((4 * W, D), BF),
    up=((D, F), BF),
    dn=((F, D), BF),
    normed=((T, D), BF),
    qta=((HEADS, 2 * HD, T), BF),
    kta=((HEADS, 2 * HD, T), BF),
    vt=((W, T), BF),
    qn=((HEADS, T, 2 * HD), BF),
    kn=((HEADS, T, 2 * HD), BF),
    vn=((HEADS, T, 2 * HD), BF),
    hat=((2 * W, T), F32),
    rstd=((6, 1, T), F32),
    lse=((HEADS, 1, T), F32),
    gcol=((2 * W, 128), F32),
    mixed=((4 * W, T), BF),
    mixf=((W, T), F32),
    mid=((T, D), F32),
    normed2=((T, D), BF),
    active=((T, F), BF),
    gpre=((T, F), BF),
    big0=((BLK, D), F32),
    big1=((BLK, D), F32),
    p2=((T, D), BF),
    p3=((T, D), BF),
    p4=((T, D), BF),
    r12=((CH, HALF, D), BF),
    r13=((CH, HALF, D), BF),
    r14=((CH, HALF, D), BF),
    c2=((CH, HALF, D), BF),
    c3=((CH, HALF, D), BF),
    c4=((CH, HALF, D), BF),
    r22=((CH, HALF, D), BF),
    r23=((CH, HALF, D), BF),
    r24=((CH, HALF, D), BF),
    lo=((CH, HALF, D), BF),
    gt=((CH, HALF, D), BF),
    gm=((CH, HALF, D), F32),
    gattn=((T, D), BF),
    gmt=((W, BLK), F32),
    dk=((HEADS, T, 2 * HD), F32),
    dv=((HEADS, T, 2 * HD), F32),
    dkx=((W, T), F32),
    dvx=((W, T), F32),
    gproj=((3 * W, T), BF),
    gacc=((2 * W, BLK), F32),
    m0=((D, F), BF),
    m1=((F, D), BF),
    m2=((4 * W, D), BF),
    vec=((8, D), F32),
    vecs=((8, D), F32),
    rvx=((4, 8, D), F32),
    rvy=((4, 8, D), F32),
    rvz=((3, 8, D), F32),
    v1=((8, D), F32),
    v2=((8, D), F32),
    v3=((8, D), F32),
    v4=((8, D), F32),
)
for _s, _w in (("a", D), ("b", D), ("c", D // 2), ("d", D // 2)):
    SCRATCH["rs1" + _s] = ((3, 192, _w), BF)
    SCRATCH["s1" + _s] = ((192, _w), BF)
    SCRATCH["rs2" + _s] = ((3, 48, _w), BF)
    SCRATCH["s2" + _s] = ((48, _w), BF)
    SCRATCH["rz" + _s] = ((48, _w), BF)
    SCRATCH["rr" + _s] = ((192, _w), BF)

NSEM = 192
NLOC = 40


class Wide:
    def __init__(self, k, name, mat, cols, out, first, second):
        self.k, self.s, self.mat, self.cols, self.out = k, k.s, mat, cols, out
        self.name = name
        self.first, self.second = first, second
        self.u, self.t = k.coord(first), k.coord(second)
        self.base = k.sems(3 + 3 + 1 + 3 + 3)
        self.local = k.locals(1)

    def ref(self, what):
        return getattr(self.s, what + self.name)

    def rs1(self, d):
        k = self.k
        q = lax.rem(self.u + d, 4)
        return k.remote(
            self.mat.at[at(q * 192, 192, 192), self.cols],
            self.ref("rs1").at[d - 1],
            self.base + d - 1,
            k.along(self.first, d),
        )

    def rs2(self, d):
        k = self.k
        q = lax.rem(self.t + d, 4)
        return k.remote(
            self.ref("s1").at[at(q * 48, 48, 48)],
            self.ref("rs2").at[d - 1],
            self.base + 3 + d - 1,
            k.along(self.second, d),
        )

    def zz(self):
        return self.k.remote(self.ref("s2"), self.ref("rz"), self.base + 6, self.k.zhi)

    def ag2(self, d):
        piece = self.ref("rr").at[at(self.t * 48, 48, 48)]
        return self.k.remote(piece, piece, self.base + 7 + d - 1, self.k.along(self.second, d))

    def ag1(self, d):
        return self.k.remote(
            self.ref("rr"),
            self.out.at[at(self.u * 192, 192, 192), self.cols],
            self.base + 10 + d - 1,
            self.k.along(self.first, d),
        )

    def own(self):
        return self.k.copy(
            self.ref("rr"), self.out.at[at(self.u * 192, 192, 192), self.cols], self.local
        )

    def step1(self):
        for d in (2, 1, 3):
            self.rs1(d).start()

    def step2(self):
        for d in (1, 2, 3):
            self.rs1(d).wait_recv()
        rs1, s1 = self.ref("rs1"), self.ref("s1")

        def strip(i, c):
            rows = at(i * 48, 48, 48)
            total = self.mat[at(self.u * 192 + i * 48, 48, 48), self.cols].astype(F32)
            for d in range(3):
                total = total + rs1[d, rows, :].astype(F32)
            s1[rows, :] = total.astype(BF)
            return c

        lax.fori_loop(0, 4, strip, 0)
        for d in (2, 1, 3):
            self.rs2(d).start()

    def step3(self):
        for d in (1, 2, 3):
            self.rs2(d).wait_recv()
        total = self.ref("s1")[at(self.t * 48, 48, 48), :].astype(F32)
        for d in range(3):
            total = total + self.ref("rs2")[d].astype(F32)
        self.ref("s2")[...] = total.astype(BF)
        self.zz().start()

    def step4(self):
        self.zz().wait_recv()
        total = self.ref("s2")[...].astype(F32) + self.ref("rz")[...].astype(F32)
        self.ref("rr")[at(self.t * 48, 48, 48), :] = total.astype(BF)
        for d in (2, 1, 3):
            self.ag2(d).start()

    def step5(self):
        for d in (1, 2, 3):
            self.ag2(d).wait_recv()
        for d in (2, 1, 3):
            self.ag1(d).start()
        self.own().start()

    def finish(self):
        for d in (1, 2, 3):
            self.ag1(d).wait_recv()
        self.own().wait()
        for d in (1, 2, 3):
            self.rs1(d).wait_send()
            self.rs2(d).wait_send()
            self.ag2(d).wait_send()
            self.ag1(d).wait_send()
        self.zz().wait_send()


class Narrow:
    def __init__(self, k, part, r1, c, r2, result):
        self.k, self.part, self.r1, self.c, self.r2, self.result = k, part, r1, c, r2, result
        self.base = k.sems(3 * CH)

    def mine(self, b):
        return at(b * BLK + self.k.core * HALF, HALF, HALF)

    def theirs(self, b):
        return at(b * BLK + (1 - self.k.core) * HALF, HALF, HALF)

    def d1(self, b):
        return self.k.remote(
            self.part.at[self.theirs(b)], self.r1.at[b], self.base + b, self.k.mate
        )

    def d2(self, b):
        return self.k.remote(self.c.at[b], self.r2.at[b], self.base + CH + b, self.k.zlo)

    def d3(self, b):
        src, dst = self.result(b, self.mine(b))
        return self.k.remote(src, dst, self.base + 2 * CH + b, self.k.mate)

    def s1(self, b):
        self.d1(b).start()

    def s2(self, b):
        self.d1(b).wait_recv()
        total = self.part[self.mine(b), :].astype(F32) + self.r1[b].astype(F32)
        self.c[b] = total.astype(BF)
        self.d2(b).start()

    def total(self, b):
        return self.c[b].astype(F32) + self.r2[b].astype(F32)

    def finish(self, last=True):
        for b in range(CH):
            self.d1(b).wait_send()
            self.d2(b).wait_send()
            self.d3(b).wait_send()


class Names:
    pass


class Kernel:
    def __init__(self, s, send, recv, loc):
        self.s, self.send, self.recv, self.loc = s, send, recv, loc
        self.nsem = self.nloc = 0
        w = lax.axis_index("wide")
        n = lax.axis_index("narrow")
        self.w, self.n = w, n
        self.x = lax.rem(w, 4)
        self.y = lax.rem(lax.div(w, 4), 4)
        self.z = lax.div(w, 16)
        self.core = lax.rem(n, 2)
        self.n1 = n + 1 - 2 * self.core
        self.n2 = lax.rem(n + 2, 4)
        self.mate = (w, self.n1)
        self.zlo = (w, self.n2)
        self.zhi = (lax.rem(w + 16, 32), n)
        self.side = (lax.rem(w + 16, 32), self.n2)

    def coord(self, axis):
        return self.x if axis == "x" else self.y

    def along(self, axis, d):
        if axis == "x":
            return (self.w - self.x + lax.rem(self.x + d, 4), self.n)
        return (self.w - 4 * self.y + 4 * lax.rem(self.y + d, 4), self.n)

    def sems(self, count):
        self.nsem += count
        assert self.nsem <= NSEM
        return self.nsem - count

    def locals(self, count):
        self.nloc += count
        assert self.nloc <= NLOC
        return self.nloc - count

    def remote(self, src, dst, sem, device):
        return pltpu.make_async_remote_copy(
            src_ref=src,
            dst_ref=dst,
            send_sem=self.send.at[sem],
            recv_sem=self.recv.at[sem],
            device_id=device,
            device_id_type=MESH,
        )

    def copy(self, src, dst, sem):
        return pltpu.make_async_copy(src, dst, self.loc.at[sem])


def kernel(
    x_in,
    dy_in,
    seg_in,
    pad_in,
    wqkv_in,
    qg_in,
    kg_in,
    wo_in,
    up_in,
    dn_in,
    ag_in,
    as_in,
    mg_in,
    ms_in,
    lo_out,
    gt_out,
    gup_out,
    gdn_out,
    g2_out,
    vec_out,
    *scratch,
):
    s = Names()
    for name, ref in zip(SCRATCH, scratch):
        setattr(s, name, ref)
    k = Kernel(s, *scratch[len(SCRATCH) :])
    n, core = k.n, k.core

    own_wo = s.wo.at[at(n * W, W, W)]
    loads = [
        (x_in, s.x),
        (wqkv_in, s.wraw),
        (wo_in, own_wo),
        (up_in, s.up),
        (dn_in, s.dn),
        (dy_in, s.dy),
    ]
    load_sem = k.locals(len(loads))
    loads = [k.copy(src, dst, load_sem + i) for i, (src, dst) in enumerate(loads)]
    for load in loads:
        load.start()
    load_x, load_w, load_wo, load_up, load_dn, load_dy = loads

    barrier = pltpu.get_barrier_semaphore()
    peers = [k.mate, k.zlo, k.zhi, k.side]
    peers += [k.along(axis, d) for axis in "xy" for d in (1, 2, 3)]
    for peer in peers:
        pl.semaphore_signal(barrier, inc=1, device_id=peer, device_id_type=MESH)

    sem = k.sems(3)
    wo_mate = k.remote(own_wo, own_wo, sem, k.mate)
    wo_side = k.remote(own_wo, own_wo, sem + 1, k.side)
    other_wo = s.wo.at[at(k.n2 * W, W, W)]
    wo_pass = k.remote(other_wo, other_wo, sem + 2, k.mate)
    mix_sem = k.sems(3 * CH)

    def mix_mate(b):
        ref = s.mixed.at[at(n * W, W, W), chunk(b)]
        return k.remote(ref, ref, mix_sem + b, k.mate)

    def mix_z(b):
        ref = s.mixed.at[at(n * W, W, W), chunk(b)]
        return k.remote(ref, ref, mix_sem + CH + b, k.zlo)

    def mix_pass(b):
        ref = s.mixed.at[at(k.n2 * W, W, W), chunk(b)]
        return k.remote(ref, ref, mix_sem + 2 * CH + b, k.mate)

    ar2 = Narrow(k, s.p2, s.r12, s.c2, s.r22, lambda b, rows: (s.lo.at[b], lo_out.at[rows]))
    ar3 = Narrow(k, s.p3, s.r13, s.c3, s.r23, lambda b, rows: (s.gattn.at[rows], s.gattn.at[rows]))
    ar4 = Narrow(k, s.p4, s.r14, s.c4, s.r24, lambda b, rows: (s.gt.at[b], gt_out.at[rows]))
    full = pl.ds(0, D)
    wide_a = Wide(k, "a", s.m0, full, gup_out, "x", "y")
    wide_b = Wide(k, "b", s.m1, full, gdn_out, "y", "x")
    wide_c = Wide(k, "c", s.m2, pl.ds(0, D // 2), g2_out, "x", "y")
    wide_d = Wide(k, "d", s.m2, pl.ds(D // 2, D // 2), g2_out, "y", "x")
    vec_sem = k.sems(3 + 3 + 3)
    vec_x = [
        k.remote(s.vecs, s.rvx.at[k.x], vec_sem + d - 1, k.along("x", d)) for d in (1, 2, 3)
    ]
    vec_y = [
        k.remote(s.v1, s.rvy.at[k.y], vec_sem + 3 + d - 1, k.along("y", d)) for d in (1, 2, 3)
    ]
    vec_z = k.remote(s.v2, s.rvz.at[0], vec_sem + 6, k.zhi)
    vec_c = k.remote(s.v3, s.rvz.at[1], vec_sem + 7, k.mate)
    vec_l = k.remote(s.v4, s.rvz.at[2], vec_sem + 8, k.zlo)
    out_sem = k.locals(2 * CH)

    def lo_copy(b):
        return k.copy(s.lo.at[b], lo_out.at[ar2.mine(b)], out_sem + b)

    def gt_copy(b):
        return k.copy(s.gt.at[b], gt_out.at[ar4.mine(b)], out_sem + CH + b)

    s.vec[...] = jnp.zeros_like(s.vec)
    s.gacc[...] = jnp.zeros_like(s.gacc)

    def clear(b, c):
        for h in range(HEADS):
            s.dk[h, chunk(b), :] = jnp.zeros((BLK, 2 * HD), F32)
            s.dv[h, chunk(b), :] = jnp.zeros((BLK, 2 * HD), F32)
        return c

    lax.fori_loop(0, CH, clear, 0)
    s.gcol[0:W, :] = jnp.transpose(jnp.broadcast_to(qg_in[...].reshape(1, W), (128, W)))
    s.gcol[W:, :] = jnp.transpose(jnp.broadcast_to(kg_in[...].reshape(1, W), (128, W)))
    ag = ag_in[...].reshape(1, D)
    ash = as_in[...].reshape(1, D)
    mg = mg_in[...].reshape(1, D)
    msh = ms_in[...].reshape(1, D)
    limit = T - pad_in[0]

    pl.semaphore_wait(barrier, len(peers))
    load_wo.wait()
    wo_side.start()
    wo_mate.start()

    load_w.wait()
    for c in range(3):
        s.wt[c * W : (c + 1) * W, :] = jnp.transpose(s.wraw[c].astype(F32)).astype(BF)
    load_x.wait()

    def gain_col(c, h):
        col = s.gcol[c * W + h * HD : c * W + (h + 1) * HD, :]
        return jnp.concatenate([col, col], axis=1)

    lanes = lax.broadcasted_iota(jnp.int32, (1, BLK), 1)
    subs = lax.broadcasted_iota(jnp.int32, (HD, BLK), 0)

    def padded(b):
        return jnp.where(lanes + b * BLK >= limit, 1.0, 0.0)

    def project(b, c):
        def strip(i, c):
            rows = at(b * BLK + i * HALF, HALF, HALF)
            hat, _ = moments(s.x[rows, :].astype(F32))
            s.normed[rows, :] = (hat * ag + ash).astype(BF)
            return c

        lax.fori_loop(0, 2, strip, 0)
        raw = nt(s.wt[...], s.normed[chunk(b), :])
        s.big0[0 : 3 * W // 3, 0:BLK] = raw[0:W]
        s.big0[0:W, BLK : 2 * BLK] = raw[W : 2 * W]
        s.big0[0:W, 2 * BLK :] = raw[2 * W :]
        seg = seg_in[:, chunk(b)]
        same = jnp.where(subs == seg, 1.0, 0.0)
        same_valid = same * (1.0 - padded(b))
        ones = jnp.where(subs < 2, 1.0, 0.0)
        for h in range(HEADS):
            rows = slice(h * HD, (h + 1) * HD)
            for which in range(2):
                value = s.big0[rows, which * BLK : (which + 1) * BLK]
                centre = value - jnp.mean(value, axis=0, keepdims=True)
                rstd = lax.rsqrt(jnp.mean(centre * centre, axis=0, keepdims=True) + EPS)
                hat = centre * rstd
                s.hat[which * W + h * HD : which * W + (h + 1) * HD, chunk(b)] = hat
                s.rstd[which * HEADS + h, :, chunk(b)] = rstd
                extra = same * BIG if which == 0 else same_valid
                both = jnp.concatenate([hat * gain_col(which, h), extra], axis=0)
                wide_ref, tall_ref = ((s.qta, s.qn), (s.kta, s.kn))[which]
                wide_ref[h, :, chunk(b)] = both.astype(BF)
                tall_ref[h, chunk(b), :] = jnp.transpose(both).astype(BF)
            value = s.big0[rows, 2 * BLK :]
            s.vt[rows, chunk(b)] = value.astype(BF)
            s.vn[h, chunk(b), :] = jnp.transpose(jnp.concatenate([value, ones], axis=0)).astype(BF)
        return c

    lax.fori_loop(0, CH, project, 0)

    wo_side.wait_recv()
    wo_pass.start()

    def window(b):
        return jnp.minimum(jnp.maximum(b - 1, 0), 1) * BLK

    def self_score(b, h):
        query = s.qta[h, 0:HD, chunk(b)].astype(F32)
        key = s.kta[h, 0:HD, chunk(b)].astype(F32)
        return query, key, jnp.sum(query * key, axis=0, keepdims=True) * SC

    def attend(b, c):
        first = window(b)
        pad_row = padded(b)
        for h in range(HEADS):
            rows = slice(h * HD, (h + 1) * HD)
            _, _, own = self_score(b, h)
            total = jnp.exp2(own) * pad_row
            out = s.vt[rows, chunk(b)].astype(F32) * total
            query = s.qta[h, :, chunk(b)]
            for i in range(3):
                keys = at(first + i * BLK, BLK, BLK)
                score = nn(s.kn[h, keys, :], query)
                weight = jnp.exp2(score * SC - SC * BIG)
                total = total + jnp.sum(weight, axis=0, keepdims=True)
                out = out + nn(s.vt[rows, keys], weight.astype(BF))
            out = out / total
            s.lse[h, :, chunk(b)] = jnp.log(total) * 1.4426950408889634
            s.mixf[rows, chunk(b)] = out
            s.mixed[at(n * W + h * HD, HD, HD), chunk(b)] = out.astype(BF)
        mix_z(b).start()
        mix_mate(b).start()
        return c

    lax.fori_loop(0, CH, attend, 0)

    wo_mate.wait_recv()
    wo_pass.wait_recv()
    mix_z(0).wait_recv()
    mix_pass(0).start()
    load_up.wait()
    load_dn.wait()
    load_dy.wait()

    def mlp(b, c):
        mix_mate(b).wait_recv()
        mix_pass(b).wait_recv()
        s.big0[...] = tn(s.mixed[:, chunk(b)], s.wo[...])

        @pl.when(b < CH - 1)
        def _():
            mix_z(b + 1).wait_recv()
            mix_pass(b + 1).start()

        @pl.when(b > 0)
        def _():
            ar3.s2(b - 1)

        def strip(i, c):
            rows = at(b * BLK + i * HALF, HALF, HALF)
            middle = s.x[rows, :].astype(F32) + s.big0[at(i * HALF, HALF, HALF), :]
            s.mid[rows, :] = middle
            hat, _ = moments(middle)
            s.normed2[rows, :] = (hat * mg + msh).astype(BF)
            return c

        lax.fori_loop(0, 2, strip, 0)
        s.big0[...] = nn(s.normed2[chunk(b), :], s.up[...])
        s.big1[...] = nt(s.dy[chunk(b), :], s.dn[...])

        def gelu(i, c):
            rows = at(i * 32, 32, 32)
            pre = s.big0[rows, :]
            square = pre * pre
            tanh = jnp.tanh(pre * (GELU_A + GELU_B * square))
            half = 0.5 + 0.5 * tanh
            slope = half + (0.5 * pre) * (1.0 - tanh * tanh) * (GELU_A + 3.0 * GELU_B * square)
            out = at(b * BLK + i * 32, 32, 32)
            s.active[out, :] = (pre * half).astype(BF)
            s.gpre[out, :] = (s.big1[rows, :] * slope).astype(BF)
            return c

        lax.fori_loop(0, BLK // 32, gelu, 0)
        s.p3[chunk(b), :] = nt(s.gpre[chunk(b), :], s.up[...]).astype(BF)
        ar3.s1(b)
        s.p2[chunk(b), :] = nn(s.active[chunk(b), :], s.dn[...]).astype(BF)
        ar2.s1(b)
        return c

    lax.fori_loop(0, CH, mlp, 0)
    ar3.s2(CH - 1)

    def grad_cols(i, c):
        cols = at(i * 256, 256, 256)
        s.m0[cols, :] = tn(s.normed2[:, cols], s.gpre[...]).astype(BF)
        s.m1[cols, :] = tn(s.active[:, cols], s.dy[...]).astype(BF)
        return c

    lax.fori_loop(0, 3, grad_cols, 0)
    wide_a.step1()
    wide_b.step1()

    def second_back(b):
        ar3.d2(b).wait_recv()
        total = ar3.total(b)
        hat, rstd = moments(s.mid[ar3.mine(b), :])
        s.vec[2:3, :] += 0.5 * jnp.sum(total * hat, axis=0, keepdims=True)
        s.vec[3:4, :] += 0.5 * jnp.sum(total, axis=0, keepdims=True)
        grad = s.dy[ar3.mine(b), :].astype(F32) + norm_back(total * mg, hat, rstd)
        s.gm[b] = grad
        s.gattn[ar3.mine(b), :] = grad.astype(BF)
        ar3.d3(b).start()

    def head_back(grad, which, h, b):
        rows = slice(which * W + h * HD, which * W + (h + 1) * HD)
        hat = s.hat[rows, chunk(b)]
        s.gacc[rows, :] += grad * hat
        grad = grad * gain_col(which, h)
        grad = (
            grad
            - jnp.mean(grad, axis=0, keepdims=True)
            - hat * jnp.mean(grad * hat, axis=0, keepdims=True)
        )
        s.gproj[rows, chunk(b)] = (grad * s.rstd[which * HEADS + h, :, chunk(b)]).astype(BF)

    def attend_back(b):
        ar3.d3(b).wait_recv()
        s.gmt[...] = nt(s.wo[at(n * W, W, W), :], s.gattn[chunk(b), :])
        first = window(b)
        pad_row = padded(b)
        for h in range(HEADS):
            rows = slice(h * HD, (h + 1) * HD)
            grad_out = s.gmt[rows, :].astype(BF).astype(F32)
            delta = jnp.sum(grad_out * s.mixf[rows, chunk(b)], axis=0, keepdims=True)
            high = delta.astype(BF).astype(F32)
            extra = jnp.where(subs == 0, -high, jnp.where(subs == 1, high - delta, 0.0))
            both = jnp.concatenate([grad_out, extra], axis=0)
            grad_wide = both.astype(BF)
            grad_tall = jnp.transpose(both).astype(BF)
            lse = s.lse[h, :, chunk(b)]
            query = s.qta[h, :, chunk(b)]
            query_tall = s.qn[h, chunk(b), :]
            shift = lse + SC * BIG
            qf, kf, own = self_score(b, h)
            own_prob = jnp.exp2(own - lse) * pad_row
            own_grad = jnp.sum(grad_out * s.vt[rows, chunk(b)].astype(F32), axis=0, keepdims=True)
            own_score = own_prob * (own_grad - delta)
            s.dkx[rows, chunk(b)] = qf * own_score
            s.dvx[rows, chunk(b)] = grad_out * own_prob
            grad_query = kf * own_score
            for i in range(3):
                keys = at(first + i * BLK, BLK, BLK)
                score = nn(s.kn[h, keys, :], query)
                prob = jnp.exp2(score * SC - shift)
                grad_score = (prob * nn(s.vn[h, keys, :], grad_wide)).astype(BF)
                s.dv[h, keys, :] += nn(prob.astype(BF), grad_tall)
                s.dk[h, keys, :] += nn(grad_score, query_tall)
                grad_query = grad_query + nn(s.kta[h, 0:HD, keys], grad_score)
            head_back(grad_query * 0.125, 0, h, b)

    def first_part(b):
        for h in range(HEADS):
            rows = slice(h * HD, (h + 1) * HD)
            grad_key = jnp.transpose(s.dk[h, chunk(b), :])[0:HD, :] + s.dkx[rows, chunk(b)]
            head_back(grad_key * 0.125, 1, h, b)
            grad_value = jnp.transpose(s.dv[h, chunk(b), :])[0:HD, :] + s.dvx[rows, chunk(b)]
            s.gproj[2 * W + h * HD : 2 * W + (h + 1) * HD, chunk(b)] = grad_value.astype(BF)
        s.big0[...] = tn(s.gproj[:, chunk(b)], s.wt[...])

        def strip(i, c):
            rows = at(b * BLK + i * HALF, HALF, HALF)
            part = s.big0[at(i * HALF, HALF, HALF), :]
            s.p4[rows, :] = part.astype(BF)
            hat, _ = moments(s.x[rows, :].astype(F32))
            s.vec[0:1, :] += jnp.sum(part * hat, axis=0, keepdims=True)
            s.vec[1:2, :] += jnp.sum(part, axis=0, keepdims=True)
            return c

        lax.fori_loop(0, 2, strip, 0)
        ar4.s1(b)

    def back(b, c):
        @pl.when(b < CH)
        def _():
            second_back(b)

        @pl.when(b >= 1)
        def _():
            ar2.s2(b - 1)

        @pl.when(b >= 2)
        def _():
            ar4.s2(b - 2)

        @pl.when(b < CH)
        def _():
            attend_back(b)

        @pl.when(b >= 1)
        def _():
            first_part(b - 1)

        return c

    lax.fori_loop(0, CH + 1, back, 0)
    wide_a.step2()
    wide_b.step2()
    ar4.s2(CH - 1)

    def grad_rows(i, c):
        rows = at(i * 192, 192, 192)
        s.m2[rows, :] = nn(s.gproj[rows, :], s.normed[...]).astype(BF)
        return c

    lax.fori_loop(0, 3, grad_rows, 0)
    s.m2[3 * W :, :] = nn(s.mixed[at(n * W, W, W), :], s.gattn[...]).astype(BF)
    wide_c.step1()
    wide_d.step1()
    for which in range(2):
        rows = slice(which * W, (which + 1) * W)
        both = s.gacc[rows, 0:128] + s.gacc[rows, 128:256]
        s.vec[4 + which : 5 + which, 0:W] = jnp.sum(jnp.transpose(both), axis=0, keepdims=True)
    s.vecs[...] = s.vec[...]
    s.rvx[k.x] = s.vec[...]
    for copy in vec_x:
        copy.start()

    def layer_out(b):
        ar2.d2(b).wait_recv()
        s.lo[b] = (s.mid[ar2.mine(b), :] + ar2.total(b)).astype(BF)
        ar2.d3(b).start()
        lo_copy(b).start()

    def grad_tokens(b):
        ar4.d2(b).wait_recv()
        hat, rstd = moments(s.x[ar4.mine(b), :].astype(F32))
        s.gt[b] = (s.gm[b] + norm_back(ar4.total(b) * ag, hat, rstd)).astype(BF)
        ar4.d3(b).start()
        gt_copy(b).start()

    layer_out(0)
    wide_a.step3()
    wide_b.step3()
    layer_out(1)
    wide_a.step4()
    wide_b.step4()
    layer_out(2)
    wide_a.step5()
    wide_b.step5()
    layer_out(3)
    grad_tokens(0)
    wide_c.step2()
    wide_d.step2()
    for copy in vec_x:
        copy.wait_recv()
    s.v1[...] = (s.rvx[0] + s.rvx[1]) + (s.rvx[2] + s.rvx[3])
    s.rvy[k.y] = s.v1[...]
    for copy in vec_y:
        copy.start()
    grad_tokens(1)
    wide_c.step3()
    wide_d.step3()
    for copy in vec_y:
        copy.wait_recv()
    s.v2[...] = (s.rvy[0] + s.rvy[1]) + (s.rvy[2] + s.rvy[3])
    vec_z.start()
    grad_tokens(2)
    wide_c.step4()
    wide_d.step4()
    vec_z.wait_recv()
    s.v3[...] = s.v2[...] + s.rvz[0]
    vec_c.start()
    grad_tokens(3)
    wide_c.step5()
    wide_d.step5()
    upper = lax.broadcasted_iota(jnp.int32, (8, D), 0) < 4
    vec_c.wait_recv()
    s.v4[...] = s.v3[...] + jnp.where(upper, s.rvz[1], 0.0)
    vec_l.start()
    vec_l.wait_recv()
    vec_out[...] = s.v4[...] + jnp.where(upper, s.rvz[2], 0.0)

    for b in range(CH):
        ar2.d3(b).wait_recv()
        ar4.d3(b).wait_recv()
        lo_copy(b).wait()
        gt_copy(b).wait()
        mix_mate(b).wait_send()
        mix_z(b).wait_send()
        mix_pass(b).wait_send()
    for item in (ar2, ar3, ar4, wide_a, wide_b, wide_c, wide_d):
        item.finish()
    for copy in [wo_mate, wo_side, wo_pass, *vec_x, *vec_y, vec_z, vec_c, vec_l]:
        copy.wait_send()


def body(*args):
    any_spec = pl.BlockSpec(memory_space=pl.ANY)
    vmem = pl.BlockSpec(memory_space=pltpu.VMEM)
    smem = pl.BlockSpec(memory_space=pltpu.SMEM)
    out = pl.pallas_call(
        kernel,
        out_shape=(
            jax.ShapeDtypeStruct((T, D), BF),
            jax.ShapeDtypeStruct((T, D), BF),
            jax.ShapeDtypeStruct((D, F), BF),
            jax.ShapeDtypeStruct((F, D), BF),
            jax.ShapeDtypeStruct((4 * W, D), BF),
            jax.ShapeDtypeStruct((8, D), F32),
        ),
        in_specs=[
            any_spec,
            any_spec,
            vmem,
            smem,
            any_spec,
            vmem,
            vmem,
            any_spec,
            any_spec,
            any_spec,
            vmem,
            vmem,
            vmem,
            vmem,
        ],
        out_specs=(any_spec, any_spec, any_spec, any_spec, any_spec, vmem),
        scratch_shapes=[pltpu.VMEM(shape, dtype) for shape, dtype in SCRATCH.values()]
        + [
            pltpu.SemaphoreType.DMA((NSEM,)),
            pltpu.SemaphoreType.DMA((NSEM,)),
            pltpu.SemaphoreType.DMA((NLOC,)),
        ],
        compiler_params=pltpu.CompilerParams(
            collective_id=0, has_side_effects=True, vmem_limit_bytes=60 * 1024 * 1024
        ),
        cost_estimate=pl.CostEstimate(
            flops=14 * 10**9, bytes_accessed=20 * 2**20, transcendentals=8 * 2**20
        ),
    )(*args)
    layer, grad_tokens, grad_up, grad_down, rest, vec = out
    grad_qkv = jnp.swapaxes(rest[: 3 * W].reshape(3, W, D), 1, 2).astype(F32)
    return (
        layer,
        grad_tokens,
        grad_qkv,
        vec[4, :W],
        vec[5, :W],
        rest[3 * W :].astype(F32),
        grad_up.astype(F32),
        grad_down.astype(F32),
        vec[0],
        vec[1],
        vec[2],
        vec[3],
    )


def solution(mesh):
    placed = (
        P("wide", None),
        P("wide", None),
        P("wide", None),
        P("wide"),
        P(None, None, "narrow"),
        P("narrow"),
        P("narrow"),
        P("narrow", None),
        P(None, "narrow"),
        P("narrow", None),
        P(),
        P(),
        P(),
        P(),
    )
    return jax.shard_map(
        body,
        mesh=mesh,
        in_specs=placed,
        out_specs=(
            P("wide", None),
            P("wide", None),
            P(None, None, "narrow"),
            P("narrow"),
            P("narrow"),
            P("narrow", None),
            P(None, "narrow"),
            P("narrow", None),
            P(),
            P(),
            P(),
            P(),
        ),
        check_vma=False,
    )
```

time: 784 us -> 147 us (0.19)
  waiting for transfers between devices: 426 us -> 0 us
  Pallas kernels: 0 us -> 129 us
  blocking collectives: 98.7 us -> 0 us
  matrix products: 94.2 us -> 0 us
  other arithmetic: 73.2 us -> 6.32 us
  local copies, waits for them, and re-layouts: 56.4 us -> 10.5 us
  between operations: 15.9 us -> 1.32 us
  loops' own time: 12.5 us -> 0 us
    psum x4 -> x0, waiting for transfers between devices: 426 us -> none  [the longest x1 254 us: body(): lax.psum(grad_qkv.astype(jnp.bfloat16), 'wide').astype(jnp.float32)]
    pallas_call x0 -> x1, Pallas kernels: none -> 129 us  [body(): pl.pallas_call(kernel, out_shape=(jax.ShapeDtypeStruct((T, D), BF), jax.S...]
    psum x1 -> x0, blocking collectives: 98.7 us -> none  [body(): lax.psum(grad_query_gain.astype(jnp.bfloat16), 'wide').astype(jnp.float32)]
    dot_general x28 -> x0, matrix products: 80.6 us -> none  [the longest x4 14.3 us: one_block(): jnp.einsum('hqk,khd->qhd', probs, value_heads, preferred_element_type=jnp...]
    reduce_sum x21 -> x0, other arithmetic: 35.9 us -> none  [the longest x5 12.8 us: layer_norm(): return centre * lax.rsqrt(spread + 1e-06) * gain + shift]
    convert_element_type x17 -> x4, other arithmetic: 24.2 us -> 6.32 us  [the longest x1 1.81 us: body(): rest[3 * W:].astype(F32)]
    dynamic_update_slice x8 -> x0, local copies, waits for them, and re-layouts: 16.9 us -> none  [attend_forward(): mixed, log_sums = lax.map(one_block, (query_blocks, starts))]
    another operation x3 -> x0, loops' own time: 12.5 us -> none  [the longest x2 8.31 us: attend_forward(): mixed, log_sums = lax.map(one_block, (query_blocks, starts))]
  transfers between devices with their start and end apart: 4 -> 0, of which waited for: 4 -> 0; matrix products, arithmetic and copies ran while one was open for 6% -> 0% of each run, Pallas kernels for 0% -> 0%
where the time goes in v1:
time: 147 us
  Pallas kernels  129 us (88%)
  local copies, waits for them, and re-layouts  10.5 us (7%)
  other arithmetic  6.32 us (4%)
    pallas_call x1, Pallas kernels, body(): pl.pallas_call(kernel, out_shape=(jax.ShapeDtypeStruct((T, D), BF), jax.S...  129 us
    unnamed x11, local copies, waits for them, and re-layouts  6.44 us

profile of v1, /device:TPU:0, one launch (start us, length us, event | category | flops | bytes accessed | tf_op | source)
XLA Modules:
  0.0 146.8 jit_solution(14990103793958855773)
XLA Ops:
  1.3 2.3 %copy.26.wqkv_in = bf16[3,768,192]{2,1,0:T(8,128)(2,1)} copy(bf16[3,768,192]{1,2,0:T(8,128)(2,1)} %param.18) | data formatting | bytes 1769472 | tf_op args[4]
  3.6 128.6 %shard_map.229 = (bf16[1024,768]{1,0:T(8,128)(2,1)}, bf16[1024,768]{1,0:T(8,128)(2,1)}, bf16[768,768]{1,0:T(8,128)(2,1)}, bf16[768,768]{1,0:T(8,128)(2,1)}, bf16[768,768]{1,0:T(8,128)(2,1)}, /*index=5*/f32[8,768]{1,0:T(8,128)}) custom-call(bf16[1024,768]{1,0:T(8,128)(2,1)} %x_in.1, bf16[1024,768]{1,0:T(8,128)(2,1)} %dy_in.1, s32[1,1024]{1,0:T(1,128)} %seg_in.1, ...), custom_call_target="tpu_custom_call" | custom-call | flops 14000000000 | bytes 20971520 | tf_op jit(solution)/shard_map/pallas_call | solution.py:813
  132.2 1.3 fusion
  133.6 1.5 %slice_reduce_fusion = (f32[768]{0:T(1024)}, f32[768]{0:T(1024)}, f32[768]{0:T(1024)}, f32[768]{0:T(1024)}) fusion(f32[8,768]{1,0:T(8,128)} %get-tuple-element.21), kind=kLoop, calls=%fused_computation.2 | loop fusion | bytes 24576 | tf_op jit(solution)/shard_map/slice | solution.py:867
  135.1 1.8 %slice_convert_fusion = f32[192,768]{1,0:T(8,128)} fusion(bf16[768,768]{1,0:T(8,128)(2,1)} %get-tuple-element.20), kind=kLoop, calls=%fused_computation.1 | loop fusion | flops 147456 | bytes 884736 | tf_op jit(solution)/shard_map/convert_element_type | solution.py:861
  136.9 1.2 slice.24
  138.1 0.0 copy-start.3
  138.2 1.4 convert_bitcast_fusion
  139.5 0.4 copy-done.3
  139.9 0.0 copy-start.2
  139.9 1.6 %convert_element_type.22 = f32[768,768]{1,0:T(8,128)} convert(bf16[768,768]{1,0:T(8,128)(2,1)S(1)} %copy-done.3) | non-fusion elementwise | flops 589824 | bytes 3538944 | tf_op jit(solution)/shard_map/convert_element_type | solution.py:862
  141.4 0.1 copy-done.2
  141.5 0.0 copy-start.1
  141.5 1.6 %convert_element_type.23 = f32[768,768]{1,0:T(8,128)} convert(bf16[768,768]{1,0:T(8,128)(2,1)S(1)} %copy-done.2) | non-fusion elementwise | flops 589824 | bytes 3538944 | tf_op jit(solution)/shard_map/convert_element_type | solution.py:863
  143.1 0.5 copy-done.1
  143.7 0.0 copy-start
  143.7 1.1 copy.30
  144.8 0.8 copy-done
  145.6 1.1 copy.31
Async XLA Ops:
  138.1 1.7 %copy-start.3 = (bf16[768,768]{1,0:T(8,128)(2,1)S(1)}, bf16[768,768]{1,0:T(8,128)(2,1)}, u32[]{:S(2)}) copy-start(bf16[768,768]{1,0:T(8,128)(2,1)} %get-tuple-element.22) | copy-start | bytes 3538948
  139.9 1.7 %copy-start.2 = (bf16[768,768]{1,0:T(8,128)(2,1)S(1)}, bf16[768,768]{1,0:T(8,128)(2,1)}, u32[]{:S(2)}) copy-start(bf16[768,768]{1,0:T(8,128)(2,1)} %get-tuple-element.23) | copy-start | bytes 3538948
  141.5 2.1 %copy-start.1 = (bf16[1024,768]{1,0:T(8,128)(2,1)S(1)}, bf16[1024,768]{1,0:T(8,128)(2,1)}, u32[]{:S(2)}) copy-start(bf16[1024,768]{1,0:T(8,128)(2,1)} %get-tuple-element.42) | copy-start | bytes 4718596
  143.7 2.0 %copy-start = (bf16[1024,768]{1,0:T(8,128)(2,1)S(1)}, bf16[1024,768]{1,0:T(8,128)(2,1)}, u32[]{:S(2)}) copy-start(bf16[1024,768]{1,0:T(8,128)(2,1)} %get-tuple-element.43) | copy-start | bytes 4718596

commit v2 on v1

--- a/solution.py
+++ b/solution.py
@@ -1,5 +1,3 @@
-import functools
-
 import jax
 import jax.numpy as jnp
 from jax import lax
@@ -16,8 +14,10 @@
 BLK = 256
 CH = T // BLK
 HALF = BLK // 2
-BIG = 2048.0
-SC = 0.125 * 1.4426950408889634
+BIG = 512.0
+MINUS, LSE = 31, 28
+LOG2E = 1.4426950408889634
+SC = 0.125 * LOG2E
 EPS = 1e-06
 GELU_A = 0.7978845608028654
 GELU_B = 0.044715 * GELU_A
@@ -64,7 +64,6 @@
 SCRATCH = dict(
     x=((T, D), BF),
     dy=((T, D), BF),
-    wraw=((3, D, W), BF),
     wt=((3 * W, D), BF),
     wo=((4 * W, D), BF),
     up=((D, F), BF),
@@ -78,7 +77,6 @@
     vn=((HEADS, T, 2 * HD), BF),
     hat=((2 * W, T), F32),
     rstd=((6, 1, T), F32),
-    lse=((HEADS, 1, T), F32),
     gcol=((2 * W, 128), F32),
     mixed=((4 * W, T), BF),
     mixf=((W, T), F32),
@@ -87,6 +85,7 @@
     active=((T, F), BF),
     gpre=((T, F), BF),
     big0=((BLK, D), F32),
+    gact=((T, F), F32),
     big1=((BLK, D), F32),
     p2=((T, D), BF),
     p3=((T, D), BF),
@@ -345,7 +344,7 @@
     dy_in,
     seg_in,
     pad_in,
-    wqkv_in,
+    wt_in,
     qg_in,
     kg_in,
     wo_in,
@@ -372,7 +371,7 @@
     own_wo = s.wo.at[at(n * W, W, W)]
     loads = [
         (x_in, s.x),
-        (wqkv_in, s.wraw),
+        (wt_in, s.wt),
         (wo_in, own_wo),
         (up_in, s.up),
         (dn_in, s.dn),
@@ -390,11 +389,16 @@
     for peer in peers:
         pl.semaphore_signal(barrier, inc=1, device_id=peer, device_id_type=MESH)
 
-    sem = k.sems(3)
-    wo_mate = k.remote(own_wo, own_wo, sem, k.mate)
-    wo_side = k.remote(own_wo, own_wo, sem + 1, k.side)
+    sem = k.sems(4)
+    own_low = s.wo.at[at(n * W, W // 2, W // 2)]
+    own_high = s.wo.at[at(n * W + W // 2, W // 2, W // 2)]
     other_wo = s.wo.at[at(k.n2 * W, W, W)]
-    wo_pass = k.remote(other_wo, other_wo, sem + 2, k.mate)
+    wo_sends = [
+        k.remote(own_wo, own_wo, sem, k.mate),
+        k.remote(own_low, own_low, sem + 1, k.zlo),
+        k.remote(own_high, own_high, sem + 2, k.side),
+    ]
+    wo_pass = k.remote(other_wo, other_wo, sem + 3, k.mate)
     mix_sem = k.sems(3 * CH)
 
     def mix_mate(b):
@@ -453,15 +457,8 @@
     msh = ms_in[...].reshape(1, D)
     limit = T - pad_in[0]
 
-    pl.semaphore_wait(barrier, len(peers))
-    load_wo.wait()
-    wo_side.start()
-    wo_mate.start()
-
+    load_x.wait()
     load_w.wait()
-    for c in range(3):
-        s.wt[c * W : (c + 1) * W, :] = jnp.transpose(s.wraw[c].astype(F32)).astype(BF)
-    load_x.wait()
 
     def gain_col(c, h):
         col = s.gcol[c * W + h * HD : c * W + (h + 1) * HD, :]
@@ -482,12 +479,12 @@
 
         lax.fori_loop(0, 2, strip, 0)
         raw = nt(s.wt[...], s.normed[chunk(b), :])
-        s.big0[0 : 3 * W // 3, 0:BLK] = raw[0:W]
-        s.big0[0:W, BLK : 2 * BLK] = raw[W : 2 * W]
-        s.big0[0:W, 2 * BLK :] = raw[2 * W :]
-        seg = seg_in[:, chunk(b)]
-        same = jnp.where(subs == seg, 1.0, 0.0)
+        for which in range(3):
+            s.big0[0:W, which * BLK : (which + 1) * BLK] = raw[which * W : (which + 1) * W]
+        same = jnp.where(subs == seg_in[:, chunk(b)], 1.0, 0.0)
         same_valid = same * (1.0 - padded(b))
+        query_rows = jnp.where(subs == MINUS, -BIG, BIG * same)
+        key_rows = jnp.where((subs >= LSE) & (subs <= MINUS), 1.0, same_valid)
         ones = jnp.where(subs < 2, 1.0, 0.0)
         for h in range(HEADS):
             rows = slice(h * HD, (h + 1) * HD)
@@ -498,8 +495,9 @@
                 hat = centre * rstd
                 s.hat[which * W + h * HD : which * W + (h + 1) * HD, chunk(b)] = hat
                 s.rstd[which * HEADS + h, :, chunk(b)] = rstd
-                extra = same * BIG if which == 0 else same_valid
-                both = jnp.concatenate([hat * gain_col(which, h), extra], axis=0)
+                extra = (query_rows, key_rows)[which]
+                value = hat * gain_col(which, h) * (1.0, SC)[which]
+                both = jnp.concatenate([value, extra], axis=0)
                 wide_ref, tall_ref = ((s.qta, s.qn), (s.kta, s.kn))[which]
                 wide_ref[h, :, chunk(b)] = both.astype(BF)
                 tall_ref[h, chunk(b), :] = jnp.transpose(both).astype(BF)
@@ -510,107 +508,125 @@
 
     lax.fori_loop(0, CH, project, 0)
 
-    wo_side.wait_recv()
-    wo_pass.start()
-
     def window(b):
-        return jnp.minimum(jnp.maximum(b - 1, 0), 1) * BLK
+        if isinstance(b, int):
+            return range(max(b - 1, 0), min(b + 2, CH))
+        return [b - 1, b, b + 1]
 
     def self_score(b, h):
         query = s.qta[h, 0:HD, chunk(b)].astype(F32)
         key = s.kta[h, 0:HD, chunk(b)].astype(F32)
-        return query, key, jnp.sum(query * key, axis=0, keepdims=True) * SC
-
-    def attend(b, c):
-        first = window(b)
+        return query, key, jnp.sum(query * key, axis=0, keepdims=True)
+
+    def attend(b):
         pad_row = padded(b)
+        same = jnp.where(subs == MINUS, -BIG, jnp.where(subs == seg_in[:, chunk(b)], BIG, 0.0))
         for h in range(HEADS):
             rows = slice(h * HD, (h + 1) * HD)
             _, _, own = self_score(b, h)
             total = jnp.exp2(own) * pad_row
             out = s.vt[rows, chunk(b)].astype(F32) * total
             query = s.qta[h, :, chunk(b)]
-            for i in range(3):
-                keys = at(first + i * BLK, BLK, BLK)
-                score = nn(s.kn[h, keys, :], query)
-                weight = jnp.exp2(score * SC - SC * BIG)
+            for i in window(b):
+                weight = jnp.exp2(nn(s.kn[h, chunk(i), :], query))
                 total = total + jnp.sum(weight, axis=0, keepdims=True)
-                out = out + nn(s.vt[rows, keys], weight.astype(BF))
+                out = out + nn(s.vt[rows, chunk(i)], weight.astype(BF))
             out = out / total
-            s.lse[h, :, chunk(b)] = jnp.log(total) * 1.4426950408889634
             s.mixf[rows, chunk(b)] = out
             s.mixed[at(n * W + h * HD, HD, HD), chunk(b)] = out.astype(BF)
+            lse = jnp.log(total) * -LOG2E
+            for i in range(3):
+                term = lse.astype(BF).astype(F32)
+                same = jnp.where(subs == LSE + i, term, same)
+                lse = lse - term
+            s.qta[h, HD : 2 * HD, chunk(b)] = same.astype(BF)
+
+    def send_mixed(b):
         mix_z(b).start()
         mix_mate(b).start()
+
+    attend(0)
+    pl.semaphore_wait(barrier, len(peers))
+    load_wo.wait()
+    for copy in wo_sends:
+        copy.start()
+    send_mixed(0)
+
+    def attend_inner(b, c):
+        attend(b)
+        send_mixed(b)
         return c
 
-    lax.fori_loop(0, CH, attend, 0)
-
-    wo_mate.wait_recv()
-    wo_pass.wait_recv()
+    lax.fori_loop(1, CH - 1, attend_inner, 0)
+    attend(CH - 1)
+    send_mixed(CH - 1)
+
+    load_dy.wait()
+    load_dn.wait()
+    s.gact[...] = nt(s.dy[...], s.dn[...])
+    load_up.wait()
+    for copy in wo_sends[1:]:
+        copy.wait_recv()
+    wo_pass.start()
     mix_z(0).wait_recv()
     mix_pass(0).start()
-    load_up.wait()
-    load_dn.wait()
-    load_dy.wait()
-
-    def mlp(b, c):
+    wo_sends[0].wait_recv()
+    wo_pass.wait_recv()
+
+    def out_product(b):
         mix_mate(b).wait_recv()
         mix_pass(b).wait_recv()
         s.big0[...] = tn(s.mixed[:, chunk(b)], s.wo[...])
 
-        @pl.when(b < CH - 1)
-        def _():
-            mix_z(b + 1).wait_recv()
-            mix_pass(b + 1).start()
-
-        @pl.when(b > 0)
-        def _():
-            ar3.s2(b - 1)
-
-        def strip(i, c):
-            rows = at(b * BLK + i * HALF, HALF, HALF)
-            middle = s.x[rows, :].astype(F32) + s.big0[at(i * HALF, HALF, HALF), :]
+    def pass_mixed(b):
+        mix_z(b).wait_recv()
+        mix_pass(b).start()
+
+    def second_norm(b):
+        for i in range(2):
+            rows = slice(b * BLK + i * HALF, b * BLK + (i + 1) * HALF)
+            middle = s.x[rows, :].astype(F32) + s.big0[i * HALF : (i + 1) * HALF, :]
             s.mid[rows, :] = middle
             hat, _ = moments(middle)
             s.normed2[rows, :] = (hat * mg + msh).astype(BF)
-            return c
-
-        lax.fori_loop(0, 2, strip, 0)
-        s.big0[...] = nn(s.normed2[chunk(b), :], s.up[...])
-        s.big1[...] = nt(s.dy[chunk(b), :], s.dn[...])
-
-        def gelu(i, c):
-            rows = at(i * 32, 32, 32)
-            pre = s.big0[rows, :]
+
+    def gelu(b):
+        for i in range(BLK // 32):
+            out = slice(b * BLK + i * 32, b * BLK + (i + 1) * 32)
+            pre = s.big1[i * 32 : (i + 1) * 32, :]
             square = pre * pre
             tanh = jnp.tanh(pre * (GELU_A + GELU_B * square))
             half = 0.5 + 0.5 * tanh
             slope = half + (0.5 * pre) * (1.0 - tanh * tanh) * (GELU_A + 3.0 * GELU_B * square)
-            out = at(b * BLK + i * 32, 32, 32)
             s.active[out, :] = (pre * half).astype(BF)
-            s.gpre[out, :] = (s.big1[rows, :] * slope).astype(BF)
-            return c
-
-        lax.fori_loop(0, BLK // 32, gelu, 0)
-        s.p3[chunk(b), :] = nt(s.gpre[chunk(b), :], s.up[...]).astype(BF)
+            s.gpre[out, :] = (s.gact[out, :] * slope).astype(BF)
+
+    out_product(0)
+    pass_mixed(1)
+    second_norm(0)
+    s.big1[...] = nn(s.normed2[0:BLK, :], s.up[...])
+    for b in range(CH):
+        rows = slice(b * BLK, (b + 1) * BLK)
+        if b + 1 < CH:
+            out_product(b + 1)
+        gelu(b)
+        if b + 2 < CH:
+            pass_mixed(b + 2)
+        s.p3[rows, :] = nt(s.gpre[rows, :], s.up[...]).astype(BF)
+        s.p2[rows, :] = nn(s.active[rows, :], s.dn[...]).astype(BF)
+        if b + 1 < CH:
+            second_norm(b + 1)
         ar3.s1(b)
-        s.p2[chunk(b), :] = nn(s.active[chunk(b), :], s.dn[...]).astype(BF)
         ar2.s1(b)
-        return c
-
-    lax.fori_loop(0, CH, mlp, 0)
-    ar3.s2(CH - 1)
-
-    def grad_cols(i, c):
-        cols = at(i * 256, 256, 256)
-        s.m0[cols, :] = tn(s.normed2[:, cols], s.gpre[...]).astype(BF)
-        s.m1[cols, :] = tn(s.active[:, cols], s.dy[...]).astype(BF)
-        return c
-
-    lax.fori_loop(0, 3, grad_cols, 0)
+        if b + 1 < CH:
+            after = slice((b + 1) * BLK, (b + 2) * BLK)
+            s.big1[...] = nn(s.normed2[after, :], s.up[...])
+        ar3.s2(b)
+
+    s.m1[...] = tn(s.active[...], s.dy[...]).astype(BF)
+    wide_b.step1()
+    s.m0[...] = tn(s.normed2[...], s.gpre[...]).astype(BF)
     wide_a.step1()
-    wide_b.step1()
 
     def second_back(b):
         ar3.d2(b).wait_recv()
@@ -638,7 +654,6 @@
     def attend_back(b):
         ar3.d3(b).wait_recv()
         s.gmt[...] = nt(s.wo[at(n * W, W, W), :], s.gattn[chunk(b), :])
-        first = window(b)
         pad_row = padded(b)
         for h in range(HEADS):
             rows = slice(h * HD, (h + 1) * HD)
@@ -649,26 +664,23 @@
             both = jnp.concatenate([grad_out, extra], axis=0)
             grad_wide = both.astype(BF)
             grad_tall = jnp.transpose(both).astype(BF)
-            lse = s.lse[h, :, chunk(b)]
             query = s.qta[h, :, chunk(b)]
             query_tall = s.qn[h, chunk(b), :]
-            shift = lse + SC * BIG
             qf, kf, own = self_score(b, h)
-            own_prob = jnp.exp2(own - lse) * pad_row
+            shift = jnp.sum(s.qta[h, HD + LSE : HD + MINUS, chunk(b)].astype(F32), axis=0, keepdims=True)
+            own_prob = jnp.exp2(own + shift) * pad_row
             own_grad = jnp.sum(grad_out * s.vt[rows, chunk(b)].astype(F32), axis=0, keepdims=True)
             own_score = own_prob * (own_grad - delta)
             s.dkx[rows, chunk(b)] = qf * own_score
             s.dvx[rows, chunk(b)] = grad_out * own_prob
             grad_query = kf * own_score
-            for i in range(3):
-                keys = at(first + i * BLK, BLK, BLK)
-                score = nn(s.kn[h, keys, :], query)
-                prob = jnp.exp2(score * SC - shift)
-                grad_score = (prob * nn(s.vn[h, keys, :], grad_wide)).astype(BF)
-                s.dv[h, keys, :] += nn(prob.astype(BF), grad_tall)
-                s.dk[h, keys, :] += nn(grad_score, query_tall)
-                grad_query = grad_query + nn(s.kta[h, 0:HD, keys], grad_score)
-            head_back(grad_query * 0.125, 0, h, b)
+            for i in window(b):
+                prob = jnp.exp2(nn(s.kn[h, chunk(i), :], query))
+                grad_score = (prob * nn(s.vn[h, chunk(i), :], grad_wide)).astype(BF)
+                s.dv[h, chunk(i), :] += nn(prob.astype(BF), grad_tall)
+                s.dk[h, chunk(i), :] += nn(grad_score, query_tall)
+                grad_query = grad_query + nn(s.kta[h, 0:HD, chunk(i)], grad_score)
+            head_back(grad_query * (0.125 / SC), 0, h, b)
 
     def first_part(b):
         for h in range(HEADS):
@@ -691,40 +703,20 @@
         lax.fori_loop(0, 2, strip, 0)
         ar4.s1(b)
 
-    def back(b, c):
-        @pl.when(b < CH)
-        def _():
-            second_back(b)
-
-        @pl.when(b >= 1)
-        def _():
+    for b in range(CH):
+        second_back(b)
+        if b >= 1:
             ar2.s2(b - 1)
-
-        @pl.when(b >= 2)
-        def _():
+        if b >= 2:
             ar4.s2(b - 2)
-
-        @pl.when(b < CH)
-        def _():
-            attend_back(b)
-
-        @pl.when(b >= 1)
-        def _():
+        if b == 3:
+            wide_a.step2()
+            wide_b.step2()
+        attend_back(b)
+        if b >= 1:
             first_part(b - 1)
-
-        return c
-
-    lax.fori_loop(0, CH + 1, back, 0)
-    wide_a.step2()
-    wide_b.step2()
-    ar4.s2(CH - 1)
-
-    def grad_rows(i, c):
-        rows = at(i * 192, 192, 192)
-        s.m2[rows, :] = nn(s.gproj[rows, :], s.normed[...]).astype(BF)
-        return c
-
-    lax.fori_loop(0, 3, grad_rows, 0)
+    first_part(CH - 1)
+    s.m2[0 : 3 * W, :] = nn(s.gproj[...], s.normed[...]).astype(BF)
     s.m2[3 * W :, :] = nn(s.mixed[at(n * W, W, W), :], s.gattn[...]).astype(BF)
     wide_c.step1()
     wide_d.step1()
@@ -750,17 +742,18 @@
         ar4.d3(b).start()
         gt_copy(b).start()
 
-    layer_out(0)
     wide_a.step3()
     wide_b.step3()
+    ar4.s2(CH - 2)
+    layer_out(0)
     layer_out(1)
     wide_a.step4()
     wide_b.step4()
+    ar4.s2(CH - 1)
     layer_out(2)
+    grad_tokens(0)
     wide_a.step5()
     wide_b.step5()
-    layer_out(3)
-    grad_tokens(0)
     wide_c.step2()
     wide_d.step2()
     for copy in vec_x:
@@ -776,6 +769,7 @@
         copy.wait_recv()
     s.v2[...] = (s.rvy[0] + s.rvy[1]) + (s.rvy[2] + s.rvy[3])
     vec_z.start()
+    ar2.s2(CH - 1)
     grad_tokens(2)
     wide_c.step4()
     wide_d.step4()
@@ -789,6 +783,7 @@
     vec_c.wait_recv()
     s.v4[...] = s.v3[...] + jnp.where(upper, s.rvz[1], 0.0)
     vec_l.start()
+    layer_out(3)
     vec_l.wait_recv()
     vec_out[...] = s.v4[...] + jnp.where(upper, s.rvz[2], 0.0)
 
@@ -802,14 +797,60 @@
         mix_pass(b).wait_send()
     for item in (ar2, ar3, ar4, wide_a, wide_b, wide_c, wide_d):
         item.finish()
-    for copy in [wo_mate, wo_side, wo_pass, *vec_x, *vec_y, vec_z, vec_c, vec_l]:
+    for copy in [*wo_sends, wo_pass, *vec_x, *vec_y, vec_z, vec_c, vec_l]:
         copy.wait_send()
+
+
+PARTS = 4
+
+
+def finish(lo, gt, gup, gdn, g2, vec, lo_o, gt_o, qkv_o, qg_o, kg_o, out_o, gup_o, gdn_o, ag_o, as_o, mg_o, ms_o, low, high, sem_in, sem_out):
+    through = []
+    for i, (src, dst) in enumerate(((lo, lo_o), (gt, gt_o))):
+        for p in range(PARTS):
+            rows = pl.ds(p * (T // PARTS), T // PARTS)
+            through.append(pltpu.make_async_copy(src.at[rows], dst.at[rows], sem_out.at[3 + i, p]))
+    size = D // PARTS
+    loads = {}
+    for i, src in enumerate((gup, gdn, g2)):
+        for p in range(PARTS):
+            rows = pl.ds(p * size, size)
+            loads[i, p] = pltpu.make_async_copy(src.at[rows], low.at[i, rows], sem_in.at[i, p])
+    for copy in loads.values():
+        copy.start()
+    for copy in through:
+        copy.start()
+    for ref, row, count in (
+        (ag_o, 0, D),
+        (as_o, 1, D),
+        (mg_o, 2, D),
+        (ms_o, 3, D),
+        (qg_o, 4, W),
+        (kg_o, 5, W),
+    ):
+        ref[...] = vec[row : row + 1, 0:count].reshape(count)
+    for i in range(3):
+        for p in range(PARTS):
+            rows = pl.ds(p * size, size)
+            loads[i, p].wait()
+            high[i, rows, :] = low[i, rows, :].astype(F32)
+            if i < 2:
+                dst = (gup_o, gdn_o)[i].at[rows]
+            else:
+                dst = qkv_o.at[p] if p < 3 else out_o
+            copy = pltpu.make_async_copy(high.at[i, rows], dst, sem_out.at[i, p])
+            copy.start()
+            through.append(copy)
+    for copy in through:
+        copy.wait()
 
 
 def body(*args):
     any_spec = pl.BlockSpec(memory_space=pl.ANY)
     vmem = pl.BlockSpec(memory_space=pltpu.VMEM)
     smem = pl.BlockSpec(memory_space=pltpu.SMEM)
+    args = list(args)
+    args[4] = jnp.swapaxes(args[4], 1, 2).reshape(3 * W, D)
     out = pl.pallas_call(
         kernel,
         out_shape=(
@@ -820,22 +861,9 @@
             jax.ShapeDtypeStruct((4 * W, D), BF),
             jax.ShapeDtypeStruct((8, D), F32),
         ),
-        in_specs=[
-            any_spec,
-            any_spec,
-            vmem,
-            smem,
-            any_spec,
-            vmem,
-            vmem,
-            any_spec,
-            any_spec,
-            any_spec,
-            vmem,
-            vmem,
-            vmem,
-            vmem,
-        ],
+        in_specs=[any_spec, any_spec, vmem, smem, any_spec, vmem, vmem]
+        + [any_spec] * 3
+        + [vmem] * 4,
         out_specs=(any_spec, any_spec, any_spec, any_spec, any_spec, vmem),
         scratch_shapes=[pltpu.VMEM(shape, dtype) for shape, dtype in SCRATCH.values()]
         + [
@@ -850,22 +878,35 @@
             flops=14 * 10**9, bytes_accessed=20 * 2**20, transcendentals=8 * 2**20
         ),
     )(*args)
-    layer, grad_tokens, grad_up, grad_down, rest, vec = out
-    grad_qkv = jnp.swapaxes(rest[: 3 * W].reshape(3, W, D), 1, 2).astype(F32)
-    return (
-        layer,
-        grad_tokens,
-        grad_qkv,
-        vec[4, :W],
-        vec[5, :W],
-        rest[3 * W :].astype(F32),
-        grad_up.astype(F32),
-        grad_down.astype(F32),
-        vec[0],
-        vec[1],
-        vec[2],
-        vec[3],
-    )
+    layer, tokens, qkv, *rest = pl.pallas_call(
+        finish,
+        out_shape=(
+            jax.ShapeDtypeStruct((T, D), BF),
+            jax.ShapeDtypeStruct((T, D), BF),
+            jax.ShapeDtypeStruct((3, W, D), F32),
+            jax.ShapeDtypeStruct((W,), F32),
+            jax.ShapeDtypeStruct((W,), F32),
+            jax.ShapeDtypeStruct((W, D), F32),
+            jax.ShapeDtypeStruct((D, F), F32),
+            jax.ShapeDtypeStruct((F, D), F32),
+            jax.ShapeDtypeStruct((D,), F32),
+            jax.ShapeDtypeStruct((D,), F32),
+            jax.ShapeDtypeStruct((D,), F32),
+            jax.ShapeDtypeStruct((D,), F32),
+        ),
+        in_specs=[any_spec] * 5 + [vmem],
+        out_specs=(any_spec, any_spec, any_spec, vmem, vmem, any_spec, any_spec, any_spec)
+        + (vmem,) * 4,
+        scratch_shapes=[
+            pltpu.VMEM((3, D, D), BF),
+            pltpu.VMEM((3, D, D), F32),
+            pltpu.SemaphoreType.DMA((3, PARTS)),
+            pltpu.SemaphoreType.DMA((5, PARTS)),
+        ],
+        compiler_params=pltpu.CompilerParams(vmem_limit_bytes=32 * 1024 * 1024),
+        cost_estimate=pl.CostEstimate(flops=0, bytes_accessed=17 * 2**20, transcendentals=0),
+    )(*out)
+    return (layer, tokens, jnp.swapaxes(qkv, 1, 2), *rest)
 
 
 def solution(mesh):

time: 147 us -> 126 us (0.86)
  Pallas kernels: 129 us -> 117 us
  other arithmetic: 6.32 us -> 0 us
  local copies, waits for them, and re-layouts: 10.5 us -> 7.36 us
    pallas_call x1, Pallas kernels: 129 us -> 111 us  [body(): pl.pallas_call(kernel, out_shape=(jax.ShapeDtypeStruct((T, D), BF), jax.S...]
    convert_element_type x4 -> x0, other arithmetic: 6.32 us -> none  [the longest x1 1.81 us: body(): rest[3 * W:].astype(F32)]
    pallas_call x0 -> x1, Pallas kernels: none -> 5.43 us  [body(): pl.pallas_call(finish, out_shape=(jax.ShapeDtypeStruct((T, D), BF), jax.S...]
    slice x3 -> x0, local copies, waits for them, and re-layouts: 4.09 us -> none  [the longest x1 1.52 us: body(): vec[3]]
    unnamed x11 -> x12, local copies, waits for them, and re-layouts: 6.44 us -> 7.36 us
where the time goes in v2:
time: 126 us
  Pallas kernels  117 us (93%)
  local copies, waits for them, and re-layouts  7.36 us (6%)
  between operations  1.52 us (1%)
    pallas_call x1, Pallas kernels, body(): pl.pallas_call(kernel, out_shape=(jax.ShapeDtypeStruct((T, D), BF), jax.S...  111 us
    unnamed x12, local copies, waits for them, and re-layouts  7.36 us
    pallas_call x1, Pallas kernels, body(): pl.pallas_call(finish, out_shape=(jax.ShapeDtypeStruct((T, D), BF), jax.S...  5.43 us

profile of v2, /device:TPU:0, one launch (start us, length us, event | category | flops | bytes accessed | tf_op | source)
XLA Modules:
  0.0 125.7 jit_solution(6736018596043331212)
XLA Ops:
  1.3 111.4 %shard_map.229 = (bf16[1024,768]{1,0:T(8,128)(2,1)}, bf16[1024,768]{1,0:T(8,128)(2,1)}, bf16[768,768]{1,0:T(8,128)(2,1)}, bf16[768,768]{1,0:T(8,128)(2,1)}, bf16[768,768]{1,0:T(8,128)(2,1)}, /*index=5*/f32[8,768]{1,0:T(8,128)}) custom-call(bf16[1024,768]{1,0:T(8,128)(2,1)} %x_in.1, bf16[1024,768]{1,0:T(8,128)(2,1)} %dy_in.1, s32[1,1024]{1,0:T(1,128)} %seg_in.1, ...), custom_call_target="tpu_custom_call" | custom-call | flops 14000000000 | bytes 20971520 | tf_op jit(solution)/shard_map/pallas_call | solution.py:854
  112.7 0.0 copy-start
  112.7 1.4 %copy-done = bf16[1024,768]{1,0:T(8,128)(2,1)S(1)} copy-done((bf16[1024,768]{1,0:T(8,128)(2,1)S(1)}, bf16[1024,768]{1,0:T(8,128)(2,1)}, u32[]{:S(2)}) %copy-start) | copy-done | bytes 1572888
  114.1 0.0 copy-start.1
  114.1 1.4 %copy-done.1 = bf16[1024,768]{1,0:T(8,128)(2,1)S(1)} copy-done((bf16[1024,768]{1,0:T(8,128)(2,1)S(1)}, bf16[1024,768]{1,0:T(8,128)(2,1)}, u32[]{:S(2)}) %copy-start.1) | copy-done | bytes 1572888
  115.5 0.0 copy-start.2
  115.5 1.3 %copy-done.2 = bf16[768,768]{1,0:T(8,128)(2,1)S(1)} copy-done((bf16[768,768]{1,0:T(8,128)(2,1)S(1)}, bf16[768,768]{1,0:T(8,128)(2,1)}, u32[]{:S(2)}) %copy-start.2) | copy-done | bytes 1179672
  116.8 0.0 copy-start.3
  116.8 1.3 %copy-done.3 = bf16[768,768]{1,0:T(8,128)(2,1)S(1)} copy-done((bf16[768,768]{1,0:T(8,128)(2,1)S(1)}, bf16[768,768]{1,0:T(8,128)(2,1)}, u32[]{:S(2)}) %copy-start.3) | copy-done | bytes 1179672
  118.0 0.0 copy-start.4
  118.0 1.3 %copy-done.4 = bf16[768,768]{1,0:T(8,128)(2,1)S(1)} copy-done((bf16[768,768]{1,0:T(8,128)(2,1)S(1)}, bf16[768,768]{1,0:T(8,128)(2,1)}, u32[]{:S(2)}) %copy-start.4) | copy-done | bytes 1179672
  119.3 0.0 copy-start.5
  119.3 0.7 copy-done.5
  120.0 5.4 %shard_map.230 = (bf16[1024,768]{1,0:T(8,128)(2,1)}, bf16[1024,768]{1,0:T(8,128)(2,1)}, f32[3,192,768]{2,1,0:T(8,128)}, f32[192]{0:T(256)}, f32[192]{0:T(256)}, ...) custom-call(bf16[1024,768]{1,0:T(8,128)(2,1)S(1)} %copy-done, ...), custom_call_target="tpu_custom_call" | custom-call | bytes 17825792 | tf_op jit(solution)/shard_map/pallas_call | solution.py:881
Async XLA Ops:
  112.7 1.4 %copy-start = (bf16[1024,768]{1,0:T(8,128)(2,1)S(1)}, bf16[1024,768]{1,0:T(8,128)(2,1)}, u32[]{:S(2)}) copy-start(bf16[1024,768]{1,0:T(8,128)(2,1)} %get-tuple-element.30.lo) | copy-start | bytes 4718596
  114.1 1.4 %copy-start.1 = (bf16[1024,768]{1,0:T(8,128)(2,1)S(1)}, bf16[1024,768]{1,0:T(8,128)(2,1)}, u32[]{:S(2)}) copy-start(bf16[1024,768]{1,0:T(8,128)(2,1)} %get-tuple-element.31.gt) | copy-start | bytes 4718596
  115.5 1.3 %copy-start.2 = (bf16[768,768]{1,0:T(8,128)(2,1)S(1)}, bf16[768,768]{1,0:T(8,128)(2,1)}, u32[]{:S(2)}) copy-start(bf16[768,768]{1,0:T(8,128)(2,1)} %get-tuple-element.32.gup) | copy-start | bytes 3538948
  116.8 1.3 %copy-start.3 = (bf16[768,768]{1,0:T(8,128)(2,1)S(1)}, bf16[768,768]{1,0:T(8,128)(2,1)}, u32[]{:S(2)}) copy-start(bf16[768,768]{1,0:T(8,128)(2,1)} %get-tuple-element.33.gdn) | copy-start | bytes 3538948
  118.0 1.3 %copy-start.4 = (bf16[768,768]{1,0:T(8,128)(2,1)S(1)}, bf16[768,768]{1,0:T(8,128)(2,1)}, u32[]{:S(2)}) copy-start(bf16[768,768]{1,0:T(8,128)(2,1)} %get-tuple-element.34.g2) | copy-start | bytes 3538948
  119.3 0.7 copy-start.5

commit v3 on v2

v3 whole, which is shorter than its diff:
```python
import jax
import jax.numpy as jnp
from jax import lax
from jax.experimental import pallas as pl
from jax.experimental.pallas import tpu as pltpu
from jax.sharding import PartitionSpec as P

T = 1024
D = 768
HEADS = 3
HD = 64
W = HEADS * HD
F = 768
BLK = 256
CH = T // BLK
HALF = BLK // 2
BIG = 512.0
MINUS = 31
LOG2E = 1.4426950408889634
SC = 0.125 * LOG2E
EPS = 1e-06
GELU_A = 0.7978845608028654
GELU_B = 0.044715 * GELU_A

BF = jnp.bfloat16
F32 = jnp.float32
MESH = pl.DeviceIdType.MESH


def nn(a, b):
    return lax.dot_general(a, b, (((1,), (0,)), ((), ())), preferred_element_type=F32)


def nt(a, b):
    return lax.dot_general(a, b, (((1,), (1,)), ((), ())), preferred_element_type=F32)


def tn(a, b):
    return lax.dot_general(a, b, (((0,), (0,)), ((), ())), preferred_element_type=F32)


def at(start, size, unit):
    return pl.ds(pl.multiple_of(start, unit), size)


def chunk(b):
    return at(b * BLK, BLK, BLK)


def moments(values):
    centre = values - jnp.mean(values, axis=-1, keepdims=True)
    rstd = lax.rsqrt(jnp.mean(centre * centre, axis=-1, keepdims=True) + EPS)
    return centre * rstd, rstd


def norm_back(grad, hat, rstd):
    return rstd * (
        grad
        - jnp.mean(grad, axis=-1, keepdims=True)
        - hat * jnp.mean(grad * hat, axis=-1, keepdims=True)
    )


SCRATCH = dict(
    x=((T, D), BF),
    dy=((T, D), BF),
    wt=((3 * W, D), BF),
    wo=((4 * W, D), BF),
    up=((D, F), BF),
    dn=((F, D), BF),
    normed=((T, D), BF),
    hat1=((T, D), BF),
    qta=((HEADS, 2 * HD, T), BF),
    kta=((HEADS, 2 * HD, T), BF),
    vt=((W, T), BF),
    qn=((HEADS, T, 2 * HD), BF),
    kn=((HEADS, T, 2 * HD), BF),
    vn=((HEADS, T, 2 * HD), BF),
    hat=((2 * W, T), F32),
    rstd=((6, 1, T), F32),
    gcol=((2 * W, 128), F32),
    mixed=((4 * W, T), BF),
    mixf=((W, T), F32),
    mid=((CH, HALF, D), F32),
    wgt=((HEADS, 10, BLK, BLK), BF),
    inv=((HEADS, 1, T), F32),
    normed2=((T, D), BF),
    active=((T, F), BF),
    gpre=((T, F), BF),
    big0=((BLK, D), F32),
    gact=((T, F), F32),
    big1=((BLK, D), F32),
    p2=((T, D), BF),
    p3=((T, D), BF),
    p4=((T, D), BF),
    r12=((CH, HALF, D), BF),
    r13=((CH, HALF, D), BF),
    r14=((CH, HALF, D), BF),
    r22=((CH, HALF, D), BF),
    r23=((CH, HALF, D), BF),
    r24=((CH, HALF, D), BF),
    gm=((CH, HALF, D), F32),
    gattn=((T, D), BF),
    dkv=((HEADS, T, 2 * HD), F32),
    dkx=((W, T), F32),
    dvx=((W, T), F32),
    gproj=((3 * W, T), BF),
    gacc=((2 * W, BLK), F32),
    m0=((D, F), BF),
    m1=((F, D), BF),
    m2=((4 * W, D), BF),
    vec=((8, D), F32),
    vecs=((8, D), F32),
    rvx=((4, 8, D), F32),
    rvy=((4, 8, D), F32),
    rvz=((3, 8, D), F32),
    v1=((8, D), F32),
    v2=((8, D), F32),
    v3=((8, D), F32),
    v4=((8, D), F32),
)
RELAYED = "abcd"
for _s, _w in ((_c, D // 2) for _c in "abcdef"):
    SCRATCH["rs1" + _s] = ((3, 192, _w), BF)
    SCRATCH["s1" + _s] = ((192, _w), BF)
    SCRATCH["rs2" + _s] = ((3, 48, _w), BF)
    SCRATCH["s2" + _s] = ((48, _w), BF)
    SCRATCH["rz" + _s] = ((48, _w), BF)
    SCRATCH["rr" + _s] = ((192, _w), BF)
    if _s in RELAYED:
        SCRATCH["nb" + _s] = ((2, 192, _w), BF)

NSEM = 192
NLOC = 48


class Wide:
    def __init__(self, k, name, mat, cols, out, first, second):
        self.k, self.s, self.mat, self.cols, self.out = k, k.s, mat, cols, out
        self.name = name
        self.first, self.second = first, second
        self.u, self.t = k.coord(first), k.coord(second)
        self.base = k.sems(3 + 3 + 1 + 3 + 3 + 2)
        self.local = k.locals(3)
        self.relayed = name in RELAYED

    def ref(self, what):
        return getattr(self.s, what + self.name)

    def rs1(self, d):
        k = self.k
        q = lax.rem(self.u + d, 4)
        return k.remote(
            self.mat.at[at(q * 192, 192, 192), self.cols],
            self.ref("rs1").at[d - 1],
            self.base + d - 1,
            k.along(self.first, d),
        )

    def rs2(self, d):
        k = self.k
        q = lax.rem(self.t + d, 4)
        return k.remote(
            self.ref("s1").at[at(q * 48, 48, 48)],
            self.ref("rs2").at[d - 1],
            self.base + 3 + d - 1,
            k.along(self.second, d),
        )

    def zz(self):
        return self.k.remote(self.ref("s2"), self.ref("rz"), self.base + 6, self.k.zhi)

    def ag2(self, d):
        piece = self.ref("rr").at[at(self.t * 48, 48, 48)]
        return self.k.remote(piece, piece, self.base + 7 + d - 1, self.k.along(self.second, d))

    def rows_out(self, u, start=0, size=192):
        return self.out.at[at(lax.rem(u + 4, 4) * 192 + start, size, 96), self.cols]

    def ag1(self, d):
        if self.relayed:
            dst = self.ref("nb").at[0 if d == 1 else 1]
        else:
            dst = self.rows_out(self.u)
        return self.k.remote(self.ref("rr"), dst, self.base + 10 + d - 1, self.k.along(self.first, d))

    def forward(self, d):
        u, start = (self.u - 1, 0) if d == 1 else (self.u + 1, 96)
        src = self.ref("nb").at[0 if d == 1 else 1, pl.ds(start, 96)]
        return self.k.remote(
            src, self.rows_out(u, start, 96), self.base + 13 + d // 2, self.k.along(self.first, d)
        )

    def own(self, i=0):
        if i == 0:
            return self.k.copy(self.ref("rr"), self.rows_out(self.u), self.local)
        u = self.u - 1 if i == 1 else self.u + 1
        return self.k.copy(self.ref("nb").at[i - 1], self.rows_out(u), self.local + i)

    def step1(self, which=(2, 1, 3)):
        for d in which:
            self.rs1(d).start()

    def step2(self):
        for d in (1, 2, 3):
            self.rs1(d).wait_recv()
        rs1, s1 = self.ref("rs1"), self.ref("s1")

        def strip(i, c):
            rows = at(i * 48, 48, 48)
            total = self.mat[at(self.u * 192 + i * 48, 48, 48), self.cols].astype(F32)
            for d in range(3):
                total = total + rs1[d, rows, :].astype(F32)
            s1[rows, :] = total.astype(BF)
            return c

        lax.fori_loop(0, 4, strip, 0)
        for d in (2, 1, 3):
            self.rs2(d).start()

    def step3(self):
        for d in (1, 2, 3):
            self.rs2(d).wait_recv()
        total = self.ref("s1")[at(self.t * 48, 48, 48), :].astype(F32)
        for d in range(3):
            total = total + self.ref("rs2")[d].astype(F32)
        self.ref("s2")[...] = total.astype(BF)
        self.zz().start()

    def step4(self):
        self.zz().wait_recv()
        total = self.ref("s2")[...].astype(F32) + self.ref("rz")[...].astype(F32)
        self.ref("rr")[at(self.t * 48, 48, 48), :] = total.astype(BF)
        for d in (2, 1, 3):
            self.ag2(d).start()

    def step5(self):
        for d in (1, 2, 3):
            self.ag2(d).wait_recv()
        self.own().start()

    def step6(self, d):
        self.ag1(d).start()

    def step7(self):
        for d in (1, 3):
            self.ag1(d).wait_recv()
            self.forward(d).start()
        for i in (1, 2):
            self.own(i).start()

    def finish(self):
        self.own().wait()
        if self.relayed:
            for d in (1, 3):
                self.forward(d).wait_recv()
                self.forward(d).wait_send()
                self.ag1(d).wait_send()
                self.own(1 + d // 2).wait()
        else:
            for d in (1, 2, 3):
                self.ag1(d).wait_recv()
                self.ag1(d).wait_send()
        for d in (1, 2, 3):
            self.rs1(d).wait_send()
            self.rs2(d).wait_send()
            self.ag2(d).wait_send()
        self.zz().wait_send()


class Narrow:
    def __init__(self, k, part, r1, r2, result):
        self.k, self.part, self.r1, self.r2, self.result = k, part, r1, r2, result
        self.base = k.sems(3 * CH)

    def mine(self, b):
        return at(b * BLK + self.k.core * HALF, HALF, HALF)

    def theirs(self, b):
        return at(b * BLK + (1 - self.k.core) * HALF, HALF, HALF)

    def d1(self, b):
        return self.k.remote(
            self.part.at[self.theirs(b)], self.r1.at[b], self.base + b, self.k.mate
        )

    def d2(self, b):
        return self.k.remote(
            self.part.at[self.mine(b)], self.r2.at[b], self.base + CH + b, self.k.zlo
        )

    def d3(self, b):
        src, dst = self.result(b, self.mine(b))
        return self.k.remote(src, dst, self.base + 2 * CH + b, self.k.mate)

    def s1(self, b):
        self.d1(b).start()

    def s2(self, b):
        self.d1(b).wait_recv()
        total = self.part[self.mine(b), :].astype(F32) + self.r1[b].astype(F32)
        self.part[self.mine(b), :] = total.astype(BF)
        self.d2(b).start()

    def total(self, b):
        return self.part[self.mine(b), :].astype(F32) + self.r2[b].astype(F32)

    def finish(self, last=True):
        for b in range(CH):
            self.d1(b).wait_send()
            self.d2(b).wait_send()
            self.d3(b).wait_send()


class Names:
    pass


class Kernel:
    def __init__(self, s, send, recv, loc):
        self.s, self.send, self.recv, self.loc = s, send, recv, loc
        self.nsem = self.nloc = 0
        w = lax.axis_index("wide")
        n = lax.axis_index("narrow")
        self.w, self.n = w, n
        self.x = lax.rem(w, 4)
        self.y = lax.rem(lax.div(w, 4), 4)
        self.z = lax.div(w, 16)
        self.core = lax.rem(n, 2)
        self.n1 = n + 1 - 2 * self.core
        self.n2 = lax.rem(n + 2, 4)
        self.mate = (w, self.n1)
        self.zlo = (w, self.n2)
        self.zhi = (lax.rem(w + 16, 32), n)
        self.side = (lax.rem(w + 16, 32), self.n2)

    def coord(self, axis):
        return self.x if axis == "x" else self.y

    def along(self, axis, d):
        if axis == "x":
            return (self.w - self.x + lax.rem(self.x + d, 4), self.n)
        return (self.w - 4 * self.y + 4 * lax.rem(self.y + d, 4), self.n)

    def sems(self, count):
        self.nsem += count
        assert self.nsem <= NSEM
        return self.nsem - count

    def locals(self, count):
        self.nloc += count
        assert self.nloc <= NLOC
        return self.nloc - count

    def remote(self, src, dst, sem, device):
        return pltpu.make_async_remote_copy(
            src_ref=src,
            dst_ref=dst,
            send_sem=self.send.at[sem],
            recv_sem=self.recv.at[sem],
            device_id=device,
            device_id_type=MESH,
        )

    def copy(self, src, dst, sem):
        return pltpu.make_async_copy(src, dst, self.loc.at[sem])


def kernel(
    x_in,
    dy_in,
    seg_in,
    pad_in,
    wt_in,
    qg_in,
    kg_in,
    wo_in,
    up_in,
    dn_in,
    ag_in,
    as_in,
    mg_in,
    ms_in,
    lo_out,
    gt_out,
    gup_out,
    gdn_out,
    g2_out,
    vec_out,
    *scratch,
):
    s = Names()
    for name, ref in zip(SCRATCH, scratch):
        setattr(s, name, ref)
    k = Kernel(s, *scratch[len(SCRATCH) :])
    n, core = k.n, k.core

    own_wo = s.wo.at[at(n * W, W, W)]
    pieces = [pl.ds(b * BLK, BLK) for b in range(CH)]
    loads = [
        (x_in.at[pieces[0]], s.x.at[pieces[0]]),
        (wt_in, s.wt),
        (wo_in, own_wo),
        *[(x_in.at[rows], s.x.at[rows]) for rows in pieces[1:]],
        (up_in, s.up),
        (dn_in, s.dn),
        (dy_in, s.dy),
    ]
    load_sem = k.locals(len(loads))
    loads = [k.copy(src, dst, load_sem + i) for i, (src, dst) in enumerate(loads)]
    for load in loads[:6]:
        load.start()
    load_x, load_w, load_wo, *load_rest, load_up, load_dn, load_dy = loads

    barrier = pltpu.get_barrier_semaphore()
    peers = [k.mate, k.zlo, k.zhi, k.side]
    peers += [k.along(axis, d) for axis in "xy" for d in (1, 2, 3)]
    for peer in peers:
        pl.semaphore_signal(barrier, inc=1, device_id=peer, device_id_type=MESH)

    sem = k.sems(4)
    own_low = s.wo.at[at(n * W, W // 3, W // 3)]
    own_high = s.wo.at[at(n * W + W // 3, 2 * W // 3, W // 3)]
    other_wo = s.wo.at[at(k.n2 * W, W, W)]
    wo_sends = [
        k.remote(own_wo, own_wo, sem, k.mate),
        k.remote(own_low, own_low, sem + 1, k.zlo),
        k.remote(own_high, own_high, sem + 2, k.side),
    ]
    wo_pass = k.remote(other_wo, other_wo, sem + 3, k.mate)
    mix_sem = k.sems(3 * CH)

    def mix_mate(b):
        ref = s.mixed.at[at(n * W, W, W), chunk(b)]
        return k.remote(ref, ref, mix_sem + b, k.mate)

    def mix_z(b):
        ref = s.mixed.at[at(n * W, W, W), chunk(b)]
        return k.remote(ref, ref, mix_sem + CH + b, k.zlo)

    def mix_pass(b):
        ref = s.mixed.at[at(k.n2 * W, W, W), chunk(b)]
        return k.remote(ref, ref, mix_sem + 2 * CH + b, k.mate)

    ar2 = Narrow(k, s.p2, s.r12, s.r22, lambda b, rows: (s.r22.at[b], lo_out.at[rows]))
    ar3 = Narrow(k, s.p3, s.r13, s.r23, lambda b, rows: (s.gattn.at[rows], s.gattn.at[rows]))
    ar4 = Narrow(k, s.p4, s.r14, s.r24, lambda b, rows: (s.r24.at[b], gt_out.at[rows]))
    low_cols, high_cols = pl.ds(0, D // 2), pl.ds(D // 2, D // 2)
    wide_1 = Wide(k, "a", s.m1, low_cols, gdn_out, "x", "y"), Wide(k, "b", s.m1, high_cols, gdn_out, "y", "x")
    wide_2 = Wide(k, "c", s.m0, low_cols, gup_out, "x", "y"), Wide(k, "d", s.m0, high_cols, gup_out, "y", "x")
    wide_3 = Wide(k, "e", s.m2, low_cols, g2_out, "x", "y"), Wide(k, "f", s.m2, high_cols, g2_out, "y", "x")

    def wide(pair, step, *args):
        for item in pair:
            getattr(item, step)(*args)

    vec_sem = k.sems(3 + 3 + 3)
    vec_c = k.remote(s.vecs, s.rvz.at[0], vec_sem, k.mate)
    vec_x = [k.remote(s.v1, s.rvx.at[k.x], vec_sem + d, k.along("x", d)) for d in (1, 2, 3)]
    vec_y = [k.remote(s.v2, s.rvy.at[k.y], vec_sem + 3 + d, k.along("y", d)) for d in (1, 2, 3)]
    vec_z = k.remote(s.v3, s.rvz.at[1], vec_sem + 7, k.zhi)
    vec_l = k.remote(s.v4, s.rvz.at[2], vec_sem + 8, k.zlo)
    out_sem = k.locals(2 * CH)

    def lo_copy(b):
        return k.copy(s.r22.at[b], lo_out.at[ar2.mine(b)], out_sem + b)

    def gt_copy(b):
        return k.copy(s.r24.at[b], gt_out.at[ar4.mine(b)], out_sem + CH + b)


    ag = ag_in[...].reshape(1, D)
    ash = as_in[...].reshape(1, D)
    mg = mg_in[...].reshape(1, D)
    msh = ms_in[...].reshape(1, D)
    limit = T - pad_in[0]

    load_x.wait()

    def gain_col(c, h):
        col = s.gcol[c * W + h * HD : c * W + (h + 1) * HD, :]
        return jnp.concatenate([col, col], axis=1)

    lanes = lax.broadcasted_iota(jnp.int32, (1, BLK), 1)
    subs = lax.broadcasted_iota(jnp.int32, (HD, BLK), 0)

    def padded(b):
        return jnp.where(lanes + b * BLK >= limit, 1.0, 0.0)

    def first_norm(b):
        for i in range(2):
            rows = slice(b * BLK + i * HALF, b * BLK + (i + 1) * HALF)
            hat, _ = moments(s.x[rows, :].astype(F32))
            s.hat1[rows, :] = hat.astype(BF)
            s.normed[rows, :] = (hat * ag + ash).astype(BF)

    def project(b):
        raw = nt(s.wt[...], s.normed[chunk(b), :])
        if b + 1 < CH:
            first_norm(b + 1)
        same = jnp.where(subs == seg_in[:, chunk(b)], 1.0, 0.0)
        same_valid = same * (1.0 - padded(b))
        query_rows = jnp.where(subs == MINUS, -BIG, BIG * same)
        key_rows = jnp.where(subs == MINUS, 1.0, same_valid)
        ones = jnp.where(subs < 2, 1.0, 0.0)
        for h in range(HEADS):
            for which in range(2):
                rows = slice(which * W + h * HD, which * W + (h + 1) * HD)
                value = raw[rows]
                centre = value - jnp.mean(value, axis=0, keepdims=True)
                rstd = lax.rsqrt(jnp.mean(centre * centre, axis=0, keepdims=True) + EPS)
                hat = centre * rstd
                s.hat[rows, chunk(b)] = hat
                s.rstd[which * HEADS + h, :, chunk(b)] = rstd
                value = hat * gain_col(which, h) * (1.0, SC)[which]
                both = jnp.concatenate([value, (query_rows, key_rows)[which]], axis=0)
                if which == 0:
                    s.qta[h, :, chunk(b)] = both.astype(BF)
                    tall = jnp.concatenate([value, jnp.zeros_like(value)], axis=0)
                    s.qn[h, chunk(b), :] = jnp.transpose(tall).astype(BF)
                else:
                    s.kta[h, :, chunk(b)] = both.astype(BF)
                    s.kn[h, chunk(b), :] = jnp.transpose(both).astype(BF)
            value = raw[2 * W + h * HD : 2 * W + (h + 1) * HD]
            s.vt[h * HD : (h + 1) * HD, chunk(b)] = value.astype(BF)
            s.vn[h, chunk(b), :] = jnp.transpose(jnp.concatenate([value, ones], axis=0)).astype(BF)

    first_norm(0)
    s.vec[...] = jnp.zeros_like(s.vec)
    s.gacc[...] = jnp.zeros_like(s.gacc)
    s.gcol[0:W, :] = jnp.transpose(jnp.broadcast_to(qg_in[...].reshape(1, W), (128, W)))
    s.gcol[W:, :] = jnp.transpose(jnp.broadcast_to(kg_in[...].reshape(1, W), (128, W)))
    load_w.wait()
    load_wo.wait()
    for load in loads[3:6]:
        load.wait()
    for load in loads[6:]:
        load.start()
    pl.semaphore_wait(barrier, len(peers))
    for copy in wo_sends:
        copy.start()
    for b in range(CH):
        project(b)

    def window(b):
        return range(max(b - 1, 0), min(b + 2, CH))

    def self_score(b, h):
        query = s.qta[h, 0:HD, chunk(b)].astype(F32)
        key = s.kta[h, 0:HD, chunk(b)].astype(F32)
        return query, key, jnp.sum(query * key, axis=0, keepdims=True)

    units = [(b, i) for b in range(CH) for i in window(b)]

    def attend(b):
        pad_row = padded(b)
        pairs = [(h, i) for h in range(HEADS) for i in window(b)]
        scores = [nn(s.kn[h, chunk(i), :], s.qta[h, :, chunk(b)]) for h, i in pairs]
        totals, outs = [], []
        for h in range(HEADS):
            own = jnp.exp2(self_score(b, h)[2]) * pad_row
            totals.append(own)
            outs.append(s.vt[h * HD : (h + 1) * HD, chunk(b)].astype(F32) * own)
        for (h, i), score in zip(pairs, scores):
            weight = jnp.exp2(score)
            totals[h] = totals[h] + jnp.sum(weight, axis=0, keepdims=True)
            weight = weight.astype(BF)
            s.wgt[h, units.index((b, i))] = weight
            outs[h] = outs[h] + nn(s.vt[h * HD : (h + 1) * HD, chunk(i)], weight)
        for h in range(HEADS):
            inv = 1.0 / totals[h]
            s.inv[h, :, chunk(b)] = inv
            out = outs[h] * inv
            s.mixf[h * HD : (h + 1) * HD, chunk(b)] = out
            s.mixed[at(n * W + h * HD, HD, HD), chunk(b)] = out.astype(BF)

    def send_mixed(b):
        mix_z(b).start()
        mix_mate(b).start()

    for b in range(CH):
        attend(b)
        send_mixed(b)

    load_dy.wait()
    load_dn.wait()
    s.gact[0 : T // 2, :] = nt(s.dy[0 : T // 2, :], s.dn[...])
    for copy in wo_sends[1:]:
        copy.wait_recv()
    wo_pass.start()
    s.gact[T // 2 :, :] = nt(s.dy[T // 2 :, :], s.dn[...])
    load_up.wait()
    mix_z(0).wait_recv()
    mix_pass(0).start()
    wo_sends[0].wait_recv()
    wo_pass.wait_recv()

    def wait_mixed(b):
        mix_mate(b).wait_recv()
        mix_pass(b).wait_recv()

    def out_product(b):
        s.big0[...] = tn(s.mixed[:, chunk(b)], s.wo[...])

    def pass_mixed(b):
        mix_z(b).wait_recv()
        mix_pass(b).start()

    def second_norm(b):
        for i in range(2):
            rows = slice(b * BLK + i * HALF, b * BLK + (i + 1) * HALF)
            hat, _ = moments(s.x[rows, :].astype(F32) + s.big0[i * HALF : (i + 1) * HALF, :])
            s.normed2[rows, :] = (hat * mg + msh).astype(BF)
        own = s.x[ar3.mine(b), :].astype(F32)
        s.mid[b] = own + s.big0[at(core * HALF, HALF, HALF), :]

    def gelu(b):
        for i in range(BLK // 8):
            out = slice(b * BLK + i * 8, b * BLK + (i + 1) * 8)
            pre = s.big1[i * 8 : (i + 1) * 8, :]
            square = pre * pre
            tanh = jnp.tanh(pre * (GELU_A + GELU_B * square))
            half = 0.5 + 0.5 * tanh
            slope = half + (0.5 * pre) * (1.0 - tanh * tanh) * (GELU_A + 3.0 * GELU_B * square)
            s.active[out, :] = (pre * half).astype(BF)
            s.gpre[out, :] = (s.gact[out, :] * slope).astype(BF)

    def mlp_part(b):
        rows = slice(b * BLK, (b + 1) * BLK)
        s.p2[rows, :] = nn(s.active[rows, :], s.dn[...]).astype(BF)

    wait_mixed(0)
    out_product(0)
    pass_mixed(1)
    second_norm(0)
    s.big1[...] = nn(s.normed2[0:BLK, :], s.up[...])
    for b in range(CH):
        rows = slice(b * BLK, (b + 1) * BLK)
        if b + 1 < CH:
            wait_mixed(b + 1)
        gelu(b)
        if b + 1 < CH:
            out_product(b + 1)
        if b >= 1:
            ar3.s2(b - 1)
            ar2.s1(b - 1)
        if b + 2 < CH:
            pass_mixed(b + 2)
        s.p3[rows, :] = nt(s.gpre[rows, :], s.up[...]).astype(BF)
        if b + 1 < CH:
            second_norm(b + 1)
        ar3.s1(b)
        if b + 1 < CH:
            after = slice((b + 1) * BLK, (b + 2) * BLK)
            s.big1[...] = nn(s.normed2[after, :], s.up[...])
            mlp_part(b)

    left, right = slice(0, D // 2), slice(D // 2, D)
    s.m1[:, left] = tn(s.active[...], s.dy[:, left]).astype(BF)
    ar3.s2(CH - 1)
    wide(wide_1[:1], "step1")
    s.m1[:, right] = tn(s.active[...], s.dy[:, right]).astype(BF)
    wide(wide_1[1:], "step1")

    def second_back(b):
        ar3.d2(b).wait_recv()
        total = ar3.total(b)
        hat, rstd = moments(s.mid[b])
        s.vec[2:3, :] += 0.5 * jnp.sum(total * hat, axis=0, keepdims=True)
        s.vec[3:4, :] += 0.5 * jnp.sum(total, axis=0, keepdims=True)
        grad = s.dy[ar3.mine(b), :].astype(F32) + norm_back(total * mg, hat, rstd)
        s.gm[b] = grad
        s.gattn[ar3.mine(b), :] = grad.astype(BF)
        ar3.d3(b).start()

    def head_back(grad, which, h, b):
        rows = slice(which * W + h * HD, which * W + (h + 1) * HD)
        hat = s.hat[rows, chunk(b)]
        s.gacc[rows, :] += grad * hat
        grad = grad * gain_col(which, h)
        grad = (
            grad
            - jnp.mean(grad, axis=0, keepdims=True)
            - hat * jnp.mean(grad * hat, axis=0, keepdims=True)
        )
        s.gproj[rows, chunk(b)] = (grad * s.rstd[which * HEADS + h, :, chunk(b)]).astype(BF)

    def attend_back(b):
        ar3.d3(b).wait_recv()
        grad_mixed = nt(s.wo[at(n * W, W, W), :], s.gattn[chunk(b), :])
        if b == CH - 1:
            s.m2[3 * W :, :] = nn(s.mixed[at(n * W, W, W), :], s.gattn[...]).astype(BF)
        pad_row = padded(b)
        wides, pairs, grad_queries = [], [], []
        for h in range(HEADS):
            rows = slice(h * HD, (h + 1) * HD)
            grad_out = grad_mixed[rows].astype(BF).astype(F32)
            inv = s.inv[h, :, chunk(b)]
            delta = jnp.sum(grad_out * s.mixf[rows, chunk(b)], axis=0, keepdims=True)
            scaled = grad_out * inv
            low = delta * inv
            high = low.astype(BF).astype(F32)
            extra = jnp.where(subs == 0, -high, jnp.where(subs == 1, high - low, 0.0))
            wides.append(jnp.concatenate([scaled, extra], axis=0).astype(BF))
            tall = jnp.concatenate([jnp.zeros_like(scaled), scaled], axis=0)
            tall = jnp.transpose(tall).astype(BF)
            pairs.append(jnp.concatenate([s.qn[h, chunk(b), :], tall], axis=0))
            qf, kf, own = self_score(b, h)
            own_prob = jnp.exp2(own) * inv * pad_row
            own_grad = jnp.sum(grad_out * s.vt[rows, chunk(b)].astype(F32), axis=0, keepdims=True)
            own_score = own_prob * (own_grad - delta)
            s.dkx[rows, chunk(b)] = qf * own_score
            s.dvx[rows, chunk(b)] = grad_out * own_prob
            grad_queries.append(kf * own_score)
        tasks = [(h, i) for h in range(HEADS) for i in window(b)]
        products, ahead = {}, 3
        grad_scores = [[] for _ in range(HEADS)]
        for t in range(len(tasks) + ahead):
            if t < len(tasks):
                h, i = tasks[t]
                products[t] = nn(s.vn[h, chunk(i), :], wides[h])
            if t < ahead:
                continue
            h, i = tasks[t - ahead]
            weight = s.wgt[h, units.index((b, i))]
            grad_score = (weight.astype(F32) * products.pop(t - ahead)).astype(BF)
            grad_scores[h].append(grad_score)
            both = nn(jnp.concatenate([grad_score, weight], axis=1), pairs[h])
            if b == max(i - 1, 0):
                s.dkv[h, chunk(i), :] = both
            else:
                s.dkv[h, chunk(i), :] += both
            if i == window(b)[-1]:
                keys = s.kta[h, 0:HD, window(b)[0] * BLK : (i + 1) * BLK]
                grad_queries[h] = grad_queries[h] + nn(
                    keys, jnp.concatenate(grad_scores[h], axis=0)
                )
        for h in range(HEADS):
            head_back(grad_queries[h] * (0.125 / SC), 0, h, b)

    def keys_back(b):
        for h in range(HEADS):
            rows = slice(h * HD, (h + 1) * HD)
            both = jnp.transpose(s.dkv[h, chunk(b), :])
            head_back((both[0:HD] + s.dkx[rows, chunk(b)]) * 0.125, 1, h, b)
            grad_value = both[HD:] + s.dvx[rows, chunk(b)]
            s.gproj[2 * W + h * HD : 2 * W + (h + 1) * HD, chunk(b)] = grad_value.astype(BF)

    def first_part(b):
        s.big0[...] = tn(s.gproj[:, chunk(b)], s.wt[...])
        for i in range(2):
            rows = slice(b * BLK + i * HALF, b * BLK + (i + 1) * HALF)
            part = s.big0[i * HALF : (i + 1) * HALF, :]
            s.p4[rows, :] = part.astype(BF)
            s.vec[0:1, :] += jnp.sum(part * s.hat1[rows, :].astype(F32), axis=0, keepdims=True)
            s.vec[1:2, :] += jnp.sum(part, axis=0, keepdims=True)
        ar4.s1(b)

    second_back(0)
    s.m0[...] = tn(s.normed2[...], s.gpre[...]).astype(BF)
    wide(wide_2, "step1", (2,))
    attend_back(0)
    second_back(1)
    mlp_part(CH - 1)
    ar2.s1(CH - 1)
    ar2.s2(0)
    attend_back(1)
    keys_back(0)
    second_back(2)
    first_part(0)
    wide(wide_1, "step2")
    wide(wide_2, "step1", (1, 3))
    attend_back(2)
    keys_back(1)
    second_back(3)
    first_part(1)
    wide(wide_1, "step3")
    ar2.s2(1)
    attend_back(3)
    keys_back(2)
    keys_back(3)
    wide(wide_2, "step2")
    s.m2[0 : 3 * W, left] = nn(s.gproj[...], s.normed[:, left]).astype(BF)
    wide(wide_3[:1], "step1")
    s.m2[0 : 3 * W, right] = nn(s.gproj[...], s.normed[:, right]).astype(BF)
    wide(wide_3[1:], "step1")
    ar4.s2(0)
    wide(wide_1, "step4")
    first_part(2)
    first_part(3)
    for which in range(2):
        rows = slice(which * W, (which + 1) * W)
        both = s.gacc[rows, 0:128] + s.gacc[rows, 128:256]
        s.vec[4 + which : 5 + which, 0:W] = jnp.sum(jnp.transpose(both), axis=0, keepdims=True)
    s.vecs[...] = s.vec[...]
    vec_c.start()

    def layer_out(b):
        ar2.d2(b).wait_recv()
        s.r22[b] = (s.mid[b] + ar2.total(b)).astype(BF)
        ar2.d3(b).start()
        lo_copy(b).start()

    def grad_tokens(b):
        ar4.d2(b).wait_recv()
        hat, rstd = moments(s.x[ar4.mine(b), :].astype(F32))
        s.r24[b] = (s.gm[b] + norm_back(ar4.total(b) * ag, hat, rstd)).astype(BF)
        ar4.d3(b).start()
        gt_copy(b).start()

    wide(wide_2, "step3")
    ar2.s2(2)
    ar4.s2(1)
    upper = lax.broadcasted_iota(jnp.int32, (8, D), 0) < 4
    vec_c.wait_recv()
    s.v1[...] = s.vec[...] + jnp.where(upper, s.rvz[0], 0.0)
    s.rvx[k.x] = s.v1[...]
    for copy in vec_x:
        copy.start()
    layer_out(0)
    wide(wide_3, "step2")
    wide(wide_2, "step4")
    wide(wide_1, "step5")
    for d in (1, 3):
        wide(wide_1, "step6", d)
    for copy in vec_x:
        copy.wait_recv()
    s.v2[...] = (s.rvx[0] + s.rvx[1]) + (s.rvx[2] + s.rvx[3])
    s.rvy[k.y] = s.v2[...]
    for copy in vec_y:
        copy.start()
    layer_out(1)
    wide(wide_3, "step3")
    ar4.s2(2)
    wide(wide_2, "step5")
    for copy in vec_y:
        copy.wait_recv()
    s.v3[...] = (s.rvy[0] + s.rvy[1]) + (s.rvy[2] + s.rvy[3])
    vec_z.start()
    ar2.s2(3)
    grad_tokens(0)
    wide(wide_3, "step4")
    wide(wide_1, "step7")
    for d in (1, 3):
        wide(wide_2, "step6", d)
    vec_z.wait_recv()
    s.v4[...] = s.v3[...] + s.rvz[1]
    vec_l.start()
    ar4.s2(3)
    layer_out(2)
    grad_tokens(1)
    wide(wide_3, "step5")
    for d in (2, 1, 3):
        wide(wide_3, "step6", d)
    wide(wide_2, "step7")
    vec_l.wait_recv()
    vec_out[...] = s.v4[...] + jnp.where(upper, s.rvz[2], 0.0)
    grad_tokens(2)
    layer_out(3)
    grad_tokens(3)

    for b in range(CH):
        ar2.d3(b).wait_recv()
        ar4.d3(b).wait_recv()
        lo_copy(b).wait()
        gt_copy(b).wait()
        mix_mate(b).wait_send()
        mix_z(b).wait_send()
        mix_pass(b).wait_send()
    for item in (ar2, ar3, ar4, *wide_1, *wide_2, *wide_3):
        item.finish()
    for copy in [*wo_sends, wo_pass, *vec_x, *vec_y, vec_z, vec_c, vec_l]:
        copy.wait_send()


PARTS = 4


def finish(lo, gt, gup, gdn, g2, vec, lo_o, gt_o, qkv_o, qg_o, kg_o, out_o, gup_o, gdn_o, ag_o, as_o, mg_o, ms_o, low, high, same, sem_in, sem_out):
    size = D // PARTS
    pieces = []
    for i, (src, dst) in enumerate(((gup, gup_o), (gdn, gdn_o), (g2, None))):
        for p in range(PARTS):
            rows = pl.ds(p * size, size)
            if dst is None:
                to = qkv_o.at[p] if p < 3 else out_o
            else:
                to = dst.at[rows]
            load = pltpu.make_async_copy(src.at[rows], low.at[i, rows], sem_in.at[i, p])
            pieces.append((load, (i, rows), pltpu.make_async_copy(high.at[i, rows], to, sem_out.at[i, p])))
    size = T // PARTS
    for i, (src, dst) in enumerate(((lo, lo_o), (gt, gt_o))):
        for p in range(PARTS):
            rows = pl.ds(p * size, size)
            load = pltpu.make_async_copy(src.at[rows], same.at[i, rows], sem_in.at[3 + i, p])
            pieces.append((load, None, pltpu.make_async_copy(same.at[i, rows], dst.at[rows], sem_out.at[3 + i, p])))
    for load, _, _ in pieces:
        load.start()
    for ref, row, count in (
        (ag_o, 0, D),
        (as_o, 1, D),
        (mg_o, 2, D),
        (ms_o, 3, D),
        (qg_o, 4, W),
        (kg_o, 5, W),
    ):
        ref[...] = vec[row : row + 1, 0:count].reshape(count)
    for load, cast, store in pieces:
        load.wait()
        if cast is not None:
            high[cast] = low[cast].astype(F32)
        store.start()
    for _, _, store in pieces:
        store.wait()


def body(*args):
    any_spec = pl.BlockSpec(memory_space=pl.ANY)
    vmem = pl.BlockSpec(memory_space=pltpu.VMEM)
    smem = pl.BlockSpec(memory_space=pltpu.SMEM)
    args = list(args)
    args[4] = jnp.swapaxes(args[4], 1, 2).reshape(3 * W, D)
    out = pl.pallas_call(
        kernel,
        out_shape=(
            jax.ShapeDtypeStruct((T, D), BF),
            jax.ShapeDtypeStruct((T, D), BF),
            jax.ShapeDtypeStruct((D, F), BF),
            jax.ShapeDtypeStruct((F, D), BF),
            jax.ShapeDtypeStruct((4 * W, D), BF),
            jax.ShapeDtypeStruct((8, D), F32),
        ),
        in_specs=[any_spec, any_spec, vmem, smem, any_spec, vmem, vmem]
        + [any_spec] * 3
        + [vmem] * 4,
        out_specs=(any_spec, any_spec, any_spec, any_spec, any_spec, vmem),
        scratch_shapes=[pltpu.VMEM(shape, dtype) for shape, dtype in SCRATCH.values()]
        + [
            pltpu.SemaphoreType.DMA((NSEM,)),
            pltpu.SemaphoreType.DMA((NSEM,)),
            pltpu.SemaphoreType.DMA((NLOC,)),
        ],
        compiler_params=pltpu.CompilerParams(
            collective_id=0, has_side_effects=True, vmem_limit_bytes=60 * 1024 * 1024
        ),
        cost_estimate=pl.CostEstimate(
            flops=14 * 10**9, bytes_accessed=20 * 2**20, transcendentals=8 * 2**20
        ),
    )(*args)
    layer, tokens, qkv, *rest = pl.pallas_call(
        finish,
        out_shape=(
            jax.ShapeDtypeStruct((T, D), BF),
            jax.ShapeDtypeStruct((T, D), BF),
            jax.ShapeDtypeStruct((3, W, D), F32),
            jax.ShapeDtypeStruct((W,), F32),
            jax.ShapeDtypeStruct((W,), F32),
            jax.ShapeDtypeStruct((W, D), F32),
            jax.ShapeDtypeStruct((D, F), F32),
            jax.ShapeDtypeStruct((F, D), F32),
            jax.ShapeDtypeStruct((D,), F32),
            jax.ShapeDtypeStruct((D,), F32),
            jax.ShapeDtypeStruct((D,), F32),
            jax.ShapeDtypeStruct((D,), F32),
        ),
        in_specs=[any_spec] * 5 + [vmem],
        out_specs=(any_spec, any_spec, any_spec, vmem, vmem, any_spec, any_spec, any_spec)
        + (vmem,) * 4,
        scratch_shapes=[
            pltpu.VMEM((3, D, D), BF),
            pltpu.VMEM((3, D, D), F32),
            pltpu.VMEM((2, T, D), BF),
            pltpu.SemaphoreType.DMA((5, PARTS)),
            pltpu.SemaphoreType.DMA((5, PARTS)),
        ],
        compiler_params=pltpu.CompilerParams(vmem_limit_bytes=60 * 1024 * 1024),
        cost_estimate=pl.CostEstimate(flops=0, bytes_accessed=17 * 2**20, transcendentals=0),
    )(*out)
    return (layer, tokens, jnp.swapaxes(qkv, 1, 2), *rest)


def solution(mesh):
    placed = (
        P("wide", None),
        P("wide", None),
        P("wide", None),
        P("wide"),
        P(None, None, "narrow"),
        P("narrow"),
        P("narrow"),
        P("narrow", None),
        P(None, "narrow"),
        P("narrow", None),
        P(),
        P(),
        P(),
        P(),
    )
    return jax.shard_map(
        body,
        mesh=mesh,
        in_specs=placed,
        out_specs=(
            P("wide", None),
            P("wide", None),
            P(None, None, "narrow"),
            P("narrow"),
            P("narrow"),
            P("narrow", None),
            P(None, "narrow"),
            P("narrow", None),
            P(),
            P(),
            P(),
            P(),
        ),
        check_vma=False,
    )
```

time: 126 us -> 97.8 us (0.78)
  Pallas kernels: 117 us -> 96 us
  local copies, waits for them, and re-layouts: 7.36 us -> 0 us
    pallas_call x1, Pallas kernels: 111 us -> 88.3 us  [body(): pl.pallas_call(kernel, out_shape=(jax.ShapeDtypeStruct((T, D), BF), jax.S...]
    unnamed x12 -> x0, local copies, waits for them, and re-layouts: 7.36 us -> none
    pallas_call x1, Pallas kernels: 5.43 us -> 7.69 us  [body(): pl.pallas_call(finish, out_shape=(jax.ShapeDtypeStruct((T, D), BF), jax.S...]
where the time goes in v3:
time: 97.8 us; the launch traced here: 97.5 us
  Pallas kernels  96 us (98%)
  between operations  1.48 us (2%)
    pallas_call x1, Pallas kernels, body(): pl.pallas_call(kernel, out_shape=(jax.ShapeDtypeStruct((T, D), BF), jax.S...  88.3 us
    pallas_call x1, Pallas kernels, body(): pl.pallas_call(finish, out_shape=(jax.ShapeDtypeStruct((T, D), BF), jax.S...  7.69 us

profile of v3, /device:TPU:0, one launch (start us, length us, event | category | flops | bytes accessed | tf_op | source)
XLA Modules:
  0.0 97.5 jit_solution(11200801253471733451)
XLA Ops:
  1.3 88.3 %shard_map.229 = (bf16[1024,768]{1,0:T(8,128)(2,1)}, bf16[1024,768]{1,0:T(8,128)(2,1)}, bf16[768,768]{1,0:T(8,128)(2,1)}, bf16[768,768]{1,0:T(8,128)(2,1)}, bf16[768,768]{1,0:T(8,128)(2,1)}, /*index=5*/f32[8,768]{1,0:T(8,128)}) custom-call(bf16[1024,768]{1,0:T(8,128)(2,1)} %x_in.1, bf16[1024,768]{1,0:T(8,128)(2,1)} %dy_in.1, s32[1,1024]{1,0:T(1,128)} %seg_in.1, ...), custom_call_target="tpu_custom_call" | custom-call | flops 14000000000 | bytes 20971520 | tf_op jit(solution)/shard_map/pallas_call | solution.py:923
  89.6 7.7 %shard_map.230 = (bf16[1024,768]{1,0:T(8,128)(2,1)}, bf16[1024,768]{1,0:T(8,128)(2,1)}, f32[3,192,768]{2,1,0:T(8,128)}, f32[192]{0:T(256)}, f32[192]{0:T(256)}, ...) custom-call(bf16[1024,768]{1,0:T(8,128)(2,1)} %get-tuple-element.30., ...), custom_call_target="tpu_custom_call" | custom-call | bytes 17825792 | tf_op jit(solution)/shard_map/pallas_call | solution.py:950

commit v4 on v3

--- a/solution.py
+++ b/solution.py
@@ -62,6 +62,13 @@
 
 
 SCRATCH = dict(
+    seg=((1, T), jnp.int32),
+    qg=((W,), F32),
+    kg=((W,), F32),
+    ag=((D,), F32),
+    ash=((D,), F32),
+    mg=((D,), F32),
+    msh=((D,), F32),
     x=((T, D), BF),
     dy=((T, D), BF),
     wt=((3 * W, D), BF),
@@ -130,8 +137,8 @@
     if _s in RELAYED:
         SCRATCH["nb" + _s] = ((2, 192, _w), BF)
 
-NSEM = 192
-NLOC = 48
+NSEM = 224
+NLOC = 56
 
 
 class Wide:
@@ -140,7 +147,7 @@
         self.name = name
         self.first, self.second = first, second
         self.u, self.t = k.coord(first), k.coord(second)
-        self.base = k.sems(3 + 3 + 1 + 3 + 3 + 2)
+        self.base = k.sems(3 + 3 + 1 + 3 + 12)
         self.local = k.locals(3)
         self.relayed = name in RELAYED
 
@@ -178,11 +185,17 @@
         return self.out.at[at(lax.rem(u + 4, 4) * 192 + start, size, 96), self.cols]
 
     def ag1(self, d):
-        if self.relayed:
-            dst = self.ref("nb").at[0 if d == 1 else 1]
-        else:
-            dst = self.rows_out(self.u)
+        dst = self.ref("nb").at[0 if d == 1 else 1]
         return self.k.remote(self.ref("rr"), dst, self.base + 10 + d - 1, self.k.along(self.first, d))
+
+    def piece(self, d, e):
+        start = lax.rem(self.t + 4 - e, 4) * 48
+        return self.k.remote(
+            self.ref("rr").at[at(start, 48, 48)],
+            self.out.at[at(self.u * 192 + start, 48, 48), self.cols],
+            self.base + 10 + 3 * e + d - 1,
+            self.k.along(self.first, d),
+        )
 
     def forward(self, d):
         u, start = (self.u - 1, 0) if d == 1 else (self.u + 1, 96)
@@ -233,10 +246,16 @@
         self.ref("rr")[at(self.t * 48, 48, 48), :] = total.astype(BF)
         for d in (2, 1, 3):
             self.ag2(d).start()
+        if not self.relayed:
+            for d in (2, 1, 3):
+                self.piece(d, 0).start()
 
     def step5(self):
-        for d in (1, 2, 3):
-            self.ag2(d).wait_recv()
+        for e in (1, 3, 2):
+            self.ag2(e).wait_recv()
+            if not self.relayed:
+                for d in (2, 1, 3):
+                    self.piece(d, e).start()
         self.own().start()
 
     def step6(self, d):
@@ -259,8 +278,9 @@
                 self.own(1 + d // 2).wait()
         else:
             for d in (1, 2, 3):
-                self.ag1(d).wait_recv()
-                self.ag1(d).wait_send()
+                for e in range(4):
+                    self.piece(d, e).wait_recv()
+                    self.piece(d, e).wait_send()
         for d in (1, 2, 3):
             self.rs1(d).wait_send()
             self.rs2(d).wait_send()
@@ -408,7 +428,19 @@
     ]
     load_sem = k.locals(len(loads))
     loads = [k.copy(src, dst, load_sem + i) for i, (src, dst) in enumerate(loads)]
-    for load in loads[:6]:
+    smalls = [
+        (ag_in, s.ag),
+        (as_in, s.ash),
+        (qg_in, s.qg),
+        (kg_in, s.kg),
+        (seg_in, s.seg),
+        (mg_in, s.mg),
+        (ms_in, s.msh),
+    ]
+    small_sem = k.locals(len(smalls))
+    smalls = [k.copy(src, dst, small_sem + i) for i, (src, dst) in enumerate(smalls)]
+    loads[0].start()
+    for load in smalls + loads[1:6]:
         load.start()
     load_x, load_w, load_wo, *load_rest, load_up, load_dn, load_dy = loads
 
@@ -469,13 +501,16 @@
         return k.copy(s.r24.at[b], gt_out.at[ar4.mine(b)], out_sem + CH + b)
 
 
-    ag = ag_in[...].reshape(1, D)
-    ash = as_in[...].reshape(1, D)
-    mg = mg_in[...].reshape(1, D)
-    msh = ms_in[...].reshape(1, D)
     limit = T - pad_in[0]
 
+    for load in smalls:
+        load.wait()
     load_x.wait()
+
+    ag = s.ag[...].reshape(1, D)
+    ash = s.ash[...].reshape(1, D)
+    mg = s.mg[...].reshape(1, D)
+    msh = s.msh[...].reshape(1, D)
 
     def gain_col(c, h):
         col = s.gcol[c * W + h * HD : c * W + (h + 1) * HD, :]
@@ -498,7 +533,7 @@
         raw = nt(s.wt[...], s.normed[chunk(b), :])
         if b + 1 < CH:
             first_norm(b + 1)
-        same = jnp.where(subs == seg_in[:, chunk(b)], 1.0, 0.0)
+        same = jnp.where(subs == s.seg[:, chunk(b)], 1.0, 0.0)
         same_valid = same * (1.0 - padded(b))
         query_rows = jnp.where(subs == MINUS, -BIG, BIG * same)
         key_rows = jnp.where(subs == MINUS, 1.0, same_valid)
@@ -526,22 +561,14 @@
             s.vn[h, chunk(b), :] = jnp.transpose(jnp.concatenate([value, ones], axis=0)).astype(BF)
 
     first_norm(0)
-    s.vec[...] = jnp.zeros_like(s.vec)
-    s.gacc[...] = jnp.zeros_like(s.gacc)
-    s.gcol[0:W, :] = jnp.transpose(jnp.broadcast_to(qg_in[...].reshape(1, W), (128, W)))
-    s.gcol[W:, :] = jnp.transpose(jnp.broadcast_to(kg_in[...].reshape(1, W), (128, W)))
-    load_w.wait()
     load_wo.wait()
-    for load in loads[3:6]:
-        load.wait()
-    for load in loads[6:]:
-        load.start()
     pl.semaphore_wait(barrier, len(peers))
     for copy in wo_sends:
         copy.start()
-    for b in range(CH):
-        project(b)
-
+    s.vec[...] = jnp.zeros_like(s.vec)
+    s.gacc[...] = jnp.zeros_like(s.gacc)
+    s.gcol[0:W, :] = jnp.transpose(jnp.broadcast_to(s.qg[...].reshape(1, W), (128, W)))
+    s.gcol[W:, :] = jnp.transpose(jnp.broadcast_to(s.kg[...].reshape(1, W), (128, W)))
     def window(b):
         return range(max(b - 1, 0), min(b + 2, CH))
 
@@ -578,6 +605,13 @@
         mix_z(b).start()
         mix_mate(b).start()
 
+    load_w.wait()
+    for load in load_rest:
+        load.wait()
+    for load in loads[6:]:
+        load.start()
+    for b in range(CH):
+        project(b)
     for b in range(CH):
         attend(b)
         send_mixed(b)
@@ -629,31 +663,40 @@
         rows = slice(b * BLK, (b + 1) * BLK)
         s.p2[rows, :] = nn(s.active[rows, :], s.dn[...]).astype(BF)
 
+    def up_product(b):
+        s.big1[...] = nn(s.normed2[b * BLK : (b + 1) * BLK, :], s.up[...])
+
     wait_mixed(0)
     out_product(0)
     pass_mixed(1)
     second_norm(0)
-    s.big1[...] = nn(s.normed2[0:BLK, :], s.up[...])
+    up_product(0)
     for b in range(CH):
         rows = slice(b * BLK, (b + 1) * BLK)
-        if b + 1 < CH:
-            wait_mixed(b + 1)
         gelu(b)
-        if b + 1 < CH:
-            out_product(b + 1)
         if b >= 1:
-            ar3.s2(b - 1)
             ar2.s1(b - 1)
-        if b + 2 < CH:
-            pass_mixed(b + 2)
         s.p3[rows, :] = nt(s.gpre[rows, :], s.up[...]).astype(BF)
-        if b + 1 < CH:
+        if b >= 1 and b + 1 < CH:
             second_norm(b + 1)
         ar3.s1(b)
+        if b == 0:
+            wait_mixed(1)
+            out_product(1)
+            second_norm(1)
+            pass_mixed(2)
+            ar3.s2(0)
+        if b + 2 < CH:
+            wait_mixed(b + 2)
+        if b + 3 < CH:
+            pass_mixed(b + 3)
         if b + 1 < CH:
-            after = slice((b + 1) * BLK, (b + 2) * BLK)
-            s.big1[...] = nn(s.normed2[after, :], s.up[...])
+            up_product(b + 1)
             mlp_part(b)
+        if 1 <= b < CH - 1:
+            ar3.s2(b)
+        if b + 2 < CH:
+            out_product(b + 2)
 
     left, right = slice(0, D // 2), slice(D // 2, D)
     s.m1[:, left] = tn(s.active[...], s.dy[:, left]).astype(BF)
@@ -757,35 +800,33 @@
         ar4.s1(b)
 
     second_back(0)
-    s.m0[...] = tn(s.normed2[...], s.gpre[...]).astype(BF)
-    wide(wide_2, "step1", (2,))
+    s.m0[:, left] = tn(s.normed2[...], s.gpre[:, left]).astype(BF)
+    wide(wide_2[:1], "step1")
     attend_back(0)
     second_back(1)
-    mlp_part(CH - 1)
-    ar2.s1(CH - 1)
+    s.m0[:, right] = tn(s.normed2[...], s.gpre[:, right]).astype(BF)
+    wide(wide_2[1:], "step1")
     ar2.s2(0)
     attend_back(1)
     keys_back(0)
     second_back(2)
     first_part(0)
-    wide(wide_1, "step2")
-    wide(wide_2, "step1", (1, 3))
+    ar2.s2(1)
     attend_back(2)
     keys_back(1)
+    wide(wide_1, "step2")
     second_back(3)
     first_part(1)
-    wide(wide_1, "step3")
-    ar2.s2(1)
     attend_back(3)
     keys_back(2)
     keys_back(3)
+    ar4.s2(0)
     wide(wide_2, "step2")
     s.m2[0 : 3 * W, left] = nn(s.gproj[...], s.normed[:, left]).astype(BF)
     wide(wide_3[:1], "step1")
     s.m2[0 : 3 * W, right] = nn(s.gproj[...], s.normed[:, right]).astype(BF)
     wide(wide_3[1:], "step1")
-    ar4.s2(0)
-    wide(wide_1, "step4")
+    wide(wide_1, "step3")
     first_part(2)
     first_part(3)
     for which in range(2):
@@ -794,6 +835,10 @@
         s.vec[4 + which : 5 + which, 0:W] = jnp.sum(jnp.transpose(both), axis=0, keepdims=True)
     s.vecs[...] = s.vec[...]
     vec_c.start()
+    wide(wide_2, "step3")
+    ar4.s2(1)
+    mlp_part(CH - 1)
+    ar2.s1(CH - 1)
 
     def layer_out(b):
         ar2.d2(b).wait_recv()
@@ -808,9 +853,6 @@
         ar4.d3(b).start()
         gt_copy(b).start()
 
-    wide(wide_2, "step3")
-    ar2.s2(2)
-    ar4.s2(1)
     upper = lax.broadcasted_iota(jnp.int32, (8, D), 0) < 4
     vec_c.wait_recv()
     s.v1[...] = s.vec[...] + jnp.where(upper, s.rvz[0], 0.0)
@@ -818,41 +860,41 @@
     for copy in vec_x:
         copy.start()
     layer_out(0)
+    wide(wide_1, "step4")
+    wide(wide_2, "step4")
+    layer_out(1)
+    ar2.s2(2)
     wide(wide_3, "step2")
-    wide(wide_2, "step4")
-    wide(wide_1, "step5")
-    for d in (1, 3):
-        wide(wide_1, "step6", d)
     for copy in vec_x:
         copy.wait_recv()
     s.v2[...] = (s.rvx[0] + s.rvx[1]) + (s.rvx[2] + s.rvx[3])
     s.rvy[k.y] = s.v2[...]
     for copy in vec_y:
         copy.start()
-    layer_out(1)
+    wide(wide_1, "step5")
+    for d in (1, 3):
+        wide(wide_1, "step6", d)
+    wide(wide_2, "step5")
+    for d in (1, 3):
+        wide(wide_2, "step6", d)
     wide(wide_3, "step3")
-    ar4.s2(2)
-    wide(wide_2, "step5")
     for copy in vec_y:
         copy.wait_recv()
     s.v3[...] = (s.rvy[0] + s.rvy[1]) + (s.rvy[2] + s.rvy[3])
     vec_z.start()
+    ar4.s2(2)
     ar2.s2(3)
     grad_tokens(0)
     wide(wide_3, "step4")
     wide(wide_1, "step7")
-    for d in (1, 3):
-        wide(wide_2, "step6", d)
+    wide(wide_2, "step7")
     vec_z.wait_recv()
     s.v4[...] = s.v3[...] + s.rvz[1]
     vec_l.start()
     ar4.s2(3)
+    grad_tokens(1)
     layer_out(2)
-    grad_tokens(1)
     wide(wide_3, "step5")
-    for d in (2, 1, 3):
-        wide(wide_3, "step6", d)
-    wide(wide_2, "step7")
     vec_l.wait_recv()
     vec_out[...] = s.v4[...] + jnp.where(upper, s.rvz[2], 0.0)
     grad_tokens(2)
@@ -888,12 +930,10 @@
                 to = dst.at[rows]
             load = pltpu.make_async_copy(src.at[rows], low.at[i, rows], sem_in.at[i, p])
             pieces.append((load, (i, rows), pltpu.make_async_copy(high.at[i, rows], to, sem_out.at[i, p])))
-    size = T // PARTS
-    for i, (src, dst) in enumerate(((lo, lo_o), (gt, gt_o))):
-        for p in range(PARTS):
-            rows = pl.ds(p * size, size)
-            load = pltpu.make_async_copy(src.at[rows], same.at[i, rows], sem_in.at[3 + i, p])
-            pieces.append((load, None, pltpu.make_async_copy(same.at[i, rows], dst.at[rows], sem_out.at[3 + i, p])))
+    for i, (src, dst) in enumerate(((gt, gt_o), (lo, lo_o))):
+        load = pltpu.make_async_copy(src, same.at[i], sem_in.at[3 + i, 0])
+        store = pltpu.make_async_copy(same.at[i], dst, sem_out.at[3 + i, 0])
+        pieces.insert(0, (load, None, store))
     for load, _, _ in pieces:
         load.start()
     for ref, row, count in (
@@ -930,9 +970,7 @@
             jax.ShapeDtypeStruct((4 * W, D), BF),
             jax.ShapeDtypeStruct((8, D), F32),
         ),
-        in_specs=[any_spec, any_spec, vmem, smem, any_spec, vmem, vmem]
-        + [any_spec] * 3
-        + [vmem] * 4,
+        in_specs=[any_spec] * 3 + [smem] + [any_spec] * 10,
         out_specs=(any_spec, any_spec, any_spec, any_spec, any_spec, vmem),
         scratch_shapes=[pltpu.VMEM(shape, dtype) for shape, dtype in SCRATCH.values()]
         + [

time: 97.8 us -> 92.9 us (0.950)
  Pallas kernels: 96 us -> 90.7 us
    pallas_call x1, Pallas kernels: 88.3 us -> 83.7 us  [body(): pl.pallas_call(kernel, out_shape=(jax.ShapeDtypeStruct((T, D), BF), jax.S...]
where the time goes in v4:
time: 92.9 us; the launch traced here: 92.2 us
  Pallas kernels  90.7 us (98%)
  between operations  1.48 us (2%)
    pallas_call x1, Pallas kernels, body(): pl.pallas_call(kernel, out_shape=(jax.ShapeDtypeStruct((T, D), BF), jax.S...  83.7 us
    pallas_call x1, Pallas kernels, body(): pl.pallas_call(finish, out_shape=(jax.ShapeDtypeStruct((T, D), BF), jax.S...  7.02 us

profile of v4, /device:TPU:0, one launch (start us, length us, event | category | flops | bytes accessed | tf_op | source)
XLA Modules:
  0.0 92.2 jit_solution(1838269369806584409)
XLA Ops:
  1.3 83.7 %shard_map.229 = (bf16[1024,768]{1,0:T(8,128)(2,1)}, bf16[1024,768]{1,0:T(8,128)(2,1)}, bf16[768,768]{1,0:T(8,128)(2,1)}, bf16[768,768]{1,0:T(8,128)(2,1)}, bf16[768,768]{1,0:T(8,128)(2,1)}, /*index=5*/f32[8,768]{1,0:T(8,128)}) custom-call(bf16[1024,768]{1,0:T(8,128)(2,1)} %x_in.1, bf16[1024,768]{1,0:T(8,128)(2,1)} %dy_in.1, s32[1,1024]{1,0:T(1,128)} %seg_in.1, ...), custom_call_target="tpu_custom_call" | custom-call | flops 14000000000 | bytes 20971520 | tf_op jit(solution)/shard_map/pallas_call | solution.py:963
  85.0 7.0 %shard_map.230 = (bf16[1024,768]{1,0:T(8,128)(2,1)}, bf16[1024,768]{1,0:T(8,128)(2,1)}, f32[3,192,768]{2,1,0:T(8,128)}, f32[192]{0:T(256)}, f32[192]{0:T(256)}, ...) custom-call(bf16[1024,768]{1,0:T(8,128)(2,1)} %get-tuple-element.30., ...), custom_call_target="tpu_custom_call" | custom-call | bytes 17825792 | tf_op jit(solution)/shard_map/pallas_call | solution.py:988

commit v5 on v4

--- a/solution.py
+++ b/solution.py
@@ -96,6 +96,8 @@
     gpre=((T, F), BF),
     big0=((BLK, D), F32),
     gact=((T, F), F32),
+    n2s=((T, D), BF),
+    r12s=((CH, HALF, D), BF),
     big1=((BLK, D), F32),
     p2=((T, D), BF),
     p3=((T, D), BF),
@@ -106,9 +108,7 @@
     r22=((CH, HALF, D), BF),
     r23=((CH, HALF, D), BF),
     r24=((CH, HALF, D), BF),
-    gm=((CH, HALF, D), F32),
     gattn=((T, D), BF),
-    dkv=((HEADS, T, 2 * HD), F32),
     dkx=((W, T), F32),
     dvx=((W, T), F32),
     gproj=((3 * W, T), BF),
@@ -126,9 +126,12 @@
     v3=((8, D), F32),
     v4=((8, D), F32),
 )
+SIDE = 2
 RELAYED = "abcd"
 for _s, _w in ((_c, D // 2) for _c in "abcdef"):
-    SCRATCH["rs1" + _s] = ((3, 192, _w), BF)
+    SCRATCH["rs1" + _s] = ((4, 96, _w), BF)
+    SCRATCH["ra" + _s] = ((2, 96, _w), BF)
+    SCRATCH["rb" + _s] = ((2, 96, _w), BF)
     SCRATCH["s1" + _s] = ((192, _w), BF)
     SCRATCH["rs2" + _s] = ((3, 48, _w), BF)
     SCRATCH["s2" + _s] = ((48, _w), BF)
@@ -137,8 +140,7 @@
     if _s in RELAYED:
         SCRATCH["nb" + _s] = ((2, 192, _w), BF)
 
-NSEM = 224
-NLOC = 56
+NSEND, NRECV, NLOC = 29, 101, 24
 
 
 class Wide:
@@ -147,21 +149,31 @@
         self.name = name
         self.first, self.second = first, second
         self.u, self.t = k.coord(first), k.coord(second)
-        self.base = k.sems(3 + 3 + 1 + 3 + 12)
-        self.local = k.locals(3)
         self.relayed = name in RELAYED
+        self.send = k.sends(3)
+        self.recv = k.recvs(7 if self.relayed else 8)
+        self.local = k.locals(1)
 
     def ref(self, what):
         return getattr(self.s, what + self.name)
 
-    def rs1(self, d):
+    def half(self, q, i):
+        return at(lax.rem(self.u + q + 4, 4) * 192 + i * 96, 96, 96)
+
+    def rs1(self, i):
         k = self.k
-        q = lax.rem(self.u + d, 4)
+        if i < 4:
+            q, part = ((2, 0), (2, 1), (1, 1), (-1, 0))[i]
+            src = self.mat.at[self.half(q, part), self.cols]
+        else:
+            src = self.ref("rb").at[i - 4]
+        dst = self.ref("ra").at[i] if i < 2 else self.ref("rs1").at[i - 2]
         return k.remote(
-            self.mat.at[at(q * 192, 192, 192), self.cols],
-            self.ref("rs1").at[d - 1],
-            self.base + d - 1,
-            k.along(self.first, d),
+            src,
+            dst,
+            self.send,
+            self.recv + (0 if i < 2 else 1),
+            k.along(self.first, 1 if i % 2 == 0 else 3),
         )
 
     def rs2(self, d):
@@ -170,30 +182,35 @@
         return k.remote(
             self.ref("s1").at[at(q * 48, 48, 48)],
             self.ref("rs2").at[d - 1],
-            self.base + 3 + d - 1,
+            self.send + 1,
+            self.recv + 2,
             k.along(self.second, d),
         )
 
     def zz(self):
-        return self.k.remote(self.ref("s2"), self.ref("rz"), self.base + 6, self.k.zhi)
+        return self.k.remote(self.ref("s2"), self.ref("rz"), self.send + 1, self.recv + 3, self.k.zhi)
 
     def ag2(self, d):
         piece = self.ref("rr").at[at(self.t * 48, 48, 48)]
-        return self.k.remote(piece, piece, self.base + 7 + d - 1, self.k.along(self.second, d))
+        recv = self.recv + 4 + (0 if self.relayed else d - 1)
+        return self.k.remote(piece, piece, self.send + 1, recv, self.k.along(self.second, d))
 
     def rows_out(self, u, start=0, size=192):
         return self.out.at[at(lax.rem(u + 4, 4) * 192 + start, size, 96), self.cols]
 
     def ag1(self, d):
         dst = self.ref("nb").at[0 if d == 1 else 1]
-        return self.k.remote(self.ref("rr"), dst, self.base + 10 + d - 1, self.k.along(self.first, d))
+        return self.k.remote(
+            self.ref("rr"), dst, self.send + 2, self.recv + 5, self.k.along(self.first, d)
+        )
 
     def piece(self, d, e):
         start = lax.rem(self.t + 4 - e, 4) * 48
         return self.k.remote(
             self.ref("rr").at[at(start, 48, 48)],
             self.out.at[at(self.u * 192 + start, 48, 48), self.cols],
-            self.base + 10 + 3 * e + d - 1,
+            self.send + 2,
+            self.recv + 7,
             self.k.along(self.first, d),
         )
 
@@ -201,39 +218,42 @@
         u, start = (self.u - 1, 0) if d == 1 else (self.u + 1, 96)
         src = self.ref("nb").at[0 if d == 1 else 1, pl.ds(start, 96)]
         return self.k.remote(
-            src, self.rows_out(u, start, 96), self.base + 13 + d // 2, self.k.along(self.first, d)
+            src,
+            self.rows_out(u, start, 96),
+            self.send + 2,
+            self.recv + 6,
+            self.k.along(self.first, d),
         )
 
     def own(self, i=0):
         if i == 0:
             return self.k.copy(self.ref("rr"), self.rows_out(self.u), self.local)
         u = self.u - 1 if i == 1 else self.u + 1
-        return self.k.copy(self.ref("nb").at[i - 1], self.rows_out(u), self.local + i)
-
-    def step1(self, which=(2, 1, 3)):
-        for d in which:
-            self.rs1(d).start()
+        return self.k.copy(self.ref("nb").at[i - 1], self.rows_out(u), self.local)
+
+    def step1(self):
+        for i in range(4):
+            self.rs1(i).start()
+
+    def step1b(self):
+        self.k.await_recvs(self.ref("ra"), self.recv)
+        for i, (q, part) in enumerate(((1, 0), (-1, 1))):
+            own = self.mat[self.half(q, part), self.cols].astype(F32)
+            self.ref("rb")[i] = (own + self.ref("ra")[i].astype(F32)).astype(BF)
+            self.rs1(4 + i).start()
 
     def step2(self):
-        for d in (1, 2, 3):
-            self.rs1(d).wait_recv()
+        self.k.await_recvs(self.ref("rs1"), self.recv + 1)
         rs1, s1 = self.ref("rs1"), self.ref("s1")
-
-        def strip(i, c):
-            rows = at(i * 48, 48, 48)
-            total = self.mat[at(self.u * 192 + i * 48, 48, 48), self.cols].astype(F32)
-            for d in range(3):
-                total = total + rs1[d, rows, :].astype(F32)
-            s1[rows, :] = total.astype(BF)
-            return c
-
-        lax.fori_loop(0, 4, strip, 0)
+        for i, (one, two) in enumerate(((1, 2), (0, 3))):
+            total = self.mat[self.half(0, i), self.cols].astype(F32)
+            total = total + (rs1[one].astype(F32) + rs1[two].astype(F32))
+            s1[i * 96 : (i + 1) * 96, :] = total.astype(BF)
         for d in (2, 1, 3):
             self.rs2(d).start()
 
     def step3(self):
-        for d in (1, 2, 3):
-            self.rs2(d).wait_recv()
+        self.k.await_recvs(self.ref("rs2"), self.recv + 2)
         total = self.ref("s1")[at(self.t * 48, 48, 48), :].astype(F32)
         for d in range(3):
             total = total + self.ref("rs2")[d].astype(F32)
@@ -251,9 +271,11 @@
                 self.piece(d, 0).start()
 
     def step5(self):
-        for e in (1, 3, 2):
-            self.ag2(e).wait_recv()
-            if not self.relayed:
+        if self.relayed:
+            self.k.await_recvs(self.ref("rr").at[pl.ds(0, 144)], self.recv + 4)
+        else:
+            for e in (1, 3, 2):
+                self.ag2(e).wait_recv()
                 for d in (2, 1, 3):
                     self.piece(d, e).start()
         self.own().start()
@@ -262,36 +284,33 @@
         self.ag1(d).start()
 
     def step7(self):
+        self.k.await_recvs(self.ref("nb"), self.recv + 5)
         for d in (1, 3):
-            self.ag1(d).wait_recv()
             self.forward(d).start()
         for i in (1, 2):
             self.own(i).start()
 
     def finish(self):
-        self.own().wait()
+        k = self.k
+        some, most = (pl.ds(0, 336), self.cols), (pl.ds(0, 576), self.cols)
         if self.relayed:
-            for d in (1, 3):
-                self.forward(d).wait_recv()
-                self.forward(d).wait_send()
-                self.ag1(d).wait_send()
-                self.own(1 + d // 2).wait()
+            k.await_recvs(self.out.at[pl.ds(0, 192), self.cols], self.recv + 6)
+            k.copy(self.mat.at[most], self.out.at[most], self.local).wait()
         else:
-            for d in (1, 2, 3):
-                for e in range(4):
-                    self.piece(d, e).wait_recv()
-                    self.piece(d, e).wait_send()
-        for d in (1, 2, 3):
-            self.rs1(d).wait_send()
-            self.rs2(d).wait_send()
-            self.ag2(d).wait_send()
-        self.zz().wait_send()
+            k.await_recvs(self.out.at[most], self.recv + 7)
+            self.own().wait()
+        k.await_sends(self.mat.at[most], self.send)
+        k.await_sends(self.mat.at[some], self.send + 1)
+        k.await_sends(self.mat.at[most], self.send + 2)
 
 
 class Narrow:
-    def __init__(self, k, part, r1, r2, result):
+    def __init__(self, k, part, r1, r2, result, joint=True, side=None):
         self.k, self.part, self.r1, self.r2, self.result = k, part, r1, r2, result
-        self.base = k.sems(3 * CH)
+        self.side = side
+        self.joint = joint
+        self.send = k.sends(2 if side is None else 3)
+        self.recv = k.recvs((2 * CH + 1 if joint else 3 * CH) + (0 if side is None else CH - SIDE))
 
     def mine(self, b):
         return at(b * BLK + self.k.core * HALF, HALF, HALF)
@@ -301,17 +320,22 @@
 
     def d1(self, b):
         return self.k.remote(
-            self.part.at[self.theirs(b)], self.r1.at[b], self.base + b, self.k.mate
+            self.part.at[self.theirs(b)], self.r1.at[b], self.send, self.recv + b, self.k.mate
         )
 
     def d2(self, b):
+        if self.side is None or b < SIDE:
+            src, device = self.part, self.k.zlo
+        else:
+            src, device = self.side[0], self.k.side
         return self.k.remote(
-            self.part.at[self.mine(b)], self.r2.at[b], self.base + CH + b, self.k.zlo
+            src.at[self.mine(b)], self.r2.at[b], self.send, self.recv + CH + b, device
         )
 
     def d3(self, b):
         src, dst = self.result(b, self.mine(b))
-        return self.k.remote(src, dst, self.base + 2 * CH + b, self.k.mate)
+        recv = self.recv + 2 * CH + (0 if self.joint else b)
+        return self.k.remote(src, dst, self.send + 1, recv, self.k.mate)
 
     def s1(self, b):
         self.d1(b).start()
@@ -320,16 +344,37 @@
         self.d1(b).wait_recv()
         total = self.part[self.mine(b), :].astype(F32) + self.r1[b].astype(F32)
         self.part[self.mine(b), :] = total.astype(BF)
+        if self.side is None or b < SIDE:
+            self.d2(b).start()
+
+    def d1_side(self, b):
+        part, r1 = self.side
+        return self.k.remote(
+            part.at[self.theirs(b)],
+            r1.at[b],
+            self.send + 2,
+            self.recv + 2 * CH + 1 + b - SIDE,
+            self.k.mate,
+        )
+
+    def s2_side(self, b):
+        part, r1 = self.side
+        self.d1_side(b).wait_recv()
+        total = part[self.mine(b), :].astype(F32) + r1[b].astype(F32)
+        part[self.mine(b), :] = total.astype(BF)
         self.d2(b).start()
 
     def total(self, b):
         return self.part[self.mine(b), :].astype(F32) + self.r2[b].astype(F32)
 
-    def finish(self, last=True):
-        for b in range(CH):
-            self.d1(b).wait_send()
-            self.d2(b).wait_send()
-            self.d3(b).wait_send()
+    def finish(self):
+        k, half = self.k, self.part.at[pl.ds(0, T // 2)]
+        if self.joint:
+            k.await_recvs(half, self.recv + 2 * CH)
+        k.await_sends(self.part, self.send)
+        k.await_sends(half, self.send + 1)
+        if self.side is not None:
+            k.await_sends(self.part.at[pl.ds(0, (CH - SIDE) * HALF)], self.send + 2)
 
 
 class Names:
@@ -339,7 +384,7 @@
 class Kernel:
     def __init__(self, s, send, recv, loc):
         self.s, self.send, self.recv, self.loc = s, send, recv, loc
-        self.nsem = self.nloc = 0
+        self.taken = {}
         w = lax.axis_index("wide")
         n = lax.axis_index("narrow")
         self.w, self.n = w, n
@@ -362,25 +407,36 @@
             return (self.w - self.x + lax.rem(self.x + d, 4), self.n)
         return (self.w - 4 * self.y + 4 * lax.rem(self.y + d, 4), self.n)
 
-    def sems(self, count):
-        self.nsem += count
-        assert self.nsem <= NSEM
-        return self.nsem - count
+    def take(self, kind, count, most):
+        start = self.taken.get(kind, 0)
+        self.taken[kind] = start + count
+        assert start + count <= most, (kind, start + count, most)
+        return start
+
+    def sends(self, count):
+        return self.take("send", count, NSEND)
+
+    def recvs(self, count):
+        return self.take("recv", count, NRECV)
 
     def locals(self, count):
-        self.nloc += count
-        assert self.nloc <= NLOC
-        return self.nloc - count
-
-    def remote(self, src, dst, sem, device):
+        return self.take("local", count, NLOC)
+
+    def remote(self, src, dst, send, recv, device):
         return pltpu.make_async_remote_copy(
             src_ref=src,
             dst_ref=dst,
-            send_sem=self.send.at[sem],
-            recv_sem=self.recv.at[sem],
+            send_sem=self.send.at[send],
+            recv_sem=self.recv.at[recv],
             device_id=device,
             device_id_type=MESH,
         )
+
+    def await_sends(self, ref, send):
+        self.remote(ref, ref, send, 0, self.mate).wait_send()
+
+    def await_recvs(self, ref, recv):
+        self.remote(ref, ref, 0, recv, self.mate).wait_recv()
 
     def copy(self, src, dst, sem):
         return pltpu.make_async_copy(src, dst, self.loc.at[sem])
@@ -450,32 +506,32 @@
     for peer in peers:
         pl.semaphore_signal(barrier, inc=1, device_id=peer, device_id_type=MESH)
 
-    sem = k.sems(4)
+    wo_send, wo_recv = k.sends(1), k.recvs(4)
     own_low = s.wo.at[at(n * W, W // 3, W // 3)]
     own_high = s.wo.at[at(n * W + W // 3, 2 * W // 3, W // 3)]
     other_wo = s.wo.at[at(k.n2 * W, W, W)]
     wo_sends = [
-        k.remote(own_wo, own_wo, sem, k.mate),
-        k.remote(own_low, own_low, sem + 1, k.zlo),
-        k.remote(own_high, own_high, sem + 2, k.side),
+        k.remote(own_wo, own_wo, wo_send, wo_recv, k.mate),
+        k.remote(own_low, own_low, wo_send, wo_recv + 1, k.zlo),
+        k.remote(own_high, own_high, wo_send, wo_recv + 2, k.side),
     ]
-    wo_pass = k.remote(other_wo, other_wo, sem + 3, k.mate)
-    mix_sem = k.sems(3 * CH)
+    wo_pass = k.remote(other_wo, other_wo, wo_send, wo_recv + 3, k.mate)
+    mix_send, mix_sem = k.sends(1), k.recvs(3 * CH)
 
     def mix_mate(b):
         ref = s.mixed.at[at(n * W, W, W), chunk(b)]
-        return k.remote(ref, ref, mix_sem + b, k.mate)
+        return k.remote(ref, ref, mix_send, mix_sem + b, k.mate)
 
     def mix_z(b):
         ref = s.mixed.at[at(n * W, W, W), chunk(b)]
-        return k.remote(ref, ref, mix_sem + CH + b, k.zlo)
+        return k.remote(ref, ref, mix_send, mix_sem + CH + b, k.zlo)
 
     def mix_pass(b):
         ref = s.mixed.at[at(k.n2 * W, W, W), chunk(b)]
-        return k.remote(ref, ref, mix_sem + 2 * CH + b, k.mate)
-
-    ar2 = Narrow(k, s.p2, s.r12, s.r22, lambda b, rows: (s.r22.at[b], lo_out.at[rows]))
-    ar3 = Narrow(k, s.p3, s.r13, s.r23, lambda b, rows: (s.gattn.at[rows], s.gattn.at[rows]))
+        return k.remote(ref, ref, mix_send, mix_sem + 2 * CH + b, k.mate)
+
+    ar2 = Narrow(k, s.p2, s.r12, s.r22, lambda b, rows: (s.r22.at[b], lo_out.at[rows]), side=(s.gpre, s.r12s))
+    ar3 = Narrow(k, s.p3, s.r13, s.r23, lambda b, rows: (s.gattn.at[rows], s.gattn.at[rows]), joint=False)
     ar4 = Narrow(k, s.p4, s.r14, s.r24, lambda b, rows: (s.r24.at[b], gt_out.at[rows]))
     low_cols, high_cols = pl.ds(0, D // 2), pl.ds(D // 2, D // 2)
     wide_1 = Wide(k, "a", s.m1, low_cols, gdn_out, "x", "y"), Wide(k, "b", s.m1, high_cols, gdn_out, "y", "x")
@@ -486,19 +542,33 @@
         for item in pair:
             getattr(item, step)(*args)
 
-    vec_sem = k.sems(3 + 3 + 3)
-    vec_c = k.remote(s.vecs, s.rvz.at[0], vec_sem, k.mate)
-    vec_x = [k.remote(s.v1, s.rvx.at[k.x], vec_sem + d, k.along("x", d)) for d in (1, 2, 3)]
-    vec_y = [k.remote(s.v2, s.rvy.at[k.y], vec_sem + 3 + d, k.along("y", d)) for d in (1, 2, 3)]
-    vec_z = k.remote(s.v3, s.rvz.at[1], vec_sem + 7, k.zhi)
-    vec_l = k.remote(s.v4, s.rvz.at[2], vec_sem + 8, k.zlo)
-    out_sem = k.locals(2 * CH)
+    vec_send, vec_sem = k.sends(1), k.recvs(5)
+    vec_c = k.remote(s.vecs, s.rvz.at[0], vec_send, vec_sem, k.mate)
+    vec_x = [
+        k.remote(s.v1, s.rvx.at[k.x], vec_send, vec_sem + 1, k.along("x", d)) for d in (1, 2, 3)
+    ]
+    vec_y = [
+        k.remote(s.v2, s.rvy.at[k.y], vec_send, vec_sem + 2, k.along("y", d)) for d in (1, 2, 3)
+    ]
+    vec_z = k.remote(s.v3, s.rvz.at[1], vec_send, vec_sem + 3, k.zhi)
+    vec_l = k.remote(s.v4, s.rvz.at[2], vec_send, vec_sem + 4, k.zlo)
+    out_sem = k.locals(2)
+
+    side_send, side_sem = k.sends(1), k.recvs(2 * (CH - SIDE))
+
+    def side_norm(b):
+        rows = ar2.mine(b)
+        return k.remote(s.normed2.at[rows], s.n2s.at[rows], side_send, side_sem + b - SIDE, k.side)
+
+    def side_pass(b):
+        rows = ar2.mine(b)
+        return k.remote(s.n2s.at[rows], s.n2s.at[rows], side_send, side_sem + CH - SIDE + b - SIDE, k.mate)
 
     def lo_copy(b):
-        return k.copy(s.r22.at[b], lo_out.at[ar2.mine(b)], out_sem + b)
+        return k.copy(s.r22.at[b], lo_out.at[ar2.mine(b)], out_sem)
 
     def gt_copy(b):
-        return k.copy(s.r24.at[b], gt_out.at[ar4.mine(b)], out_sem + CH + b)
+        return k.copy(s.r24.at[b], gt_out.at[ar4.mine(b)], out_sem + 1)
 
 
     limit = T - pad_in[0]
@@ -676,9 +746,13 @@
         gelu(b)
         if b >= 1:
             ar2.s1(b - 1)
+        if b == 3:
+            ar3.s2(2)
         s.p3[rows, :] = nt(s.gpre[rows, :], s.up[...]).astype(BF)
         if b >= 1 and b + 1 < CH:
             second_norm(b + 1)
+            if b + 1 >= SIDE:
+                side_norm(b + 1).start()
         ar3.s1(b)
         if b == 0:
             wait_mixed(1)
@@ -686,17 +760,16 @@
             second_norm(1)
             pass_mixed(2)
             ar3.s2(0)
-        if b + 2 < CH:
-            wait_mixed(b + 2)
-        if b + 3 < CH:
-            pass_mixed(b + 3)
         if b + 1 < CH:
             up_product(b + 1)
             mlp_part(b)
-        if 1 <= b < CH - 1:
-            ar3.s2(b)
         if b + 2 < CH:
+            wait_mixed(b + 2)
             out_product(b + 2)
+        if b + 3 < CH:
+            pass_mixed(b + 3)
+        if b == 1:
+            ar3.s2(1)
 
     left, right = slice(0, D // 2), slice(D // 2, D)
     s.m1[:, left] = tn(s.active[...], s.dy[:, left]).astype(BF)
@@ -712,9 +785,13 @@
         s.vec[2:3, :] += 0.5 * jnp.sum(total * hat, axis=0, keepdims=True)
         s.vec[3:4, :] += 0.5 * jnp.sum(total, axis=0, keepdims=True)
         grad = s.dy[ar3.mine(b), :].astype(F32) + norm_back(total * mg, hat, rstd)
-        s.gm[b] = grad
+        s.gact[b * HALF : (b + 1) * HALF, :] = grad
         s.gattn[ar3.mine(b), :] = grad.astype(BF)
         ar3.d3(b).start()
+
+    def key_sums(h, b):
+        col = (b // 2 * HEADS + h) * 2 * HD
+        return slice(T // 2 + b % 2 * BLK, T // 2 + (b % 2 + 1) * BLK), slice(col, col + 2 * HD)
 
     def head_back(grad, which, h, b):
         rows = slice(which * W + h * HD, which * W + (h + 1) * HD)
@@ -770,9 +847,9 @@
             grad_scores[h].append(grad_score)
             both = nn(jnp.concatenate([grad_score, weight], axis=1), pairs[h])
             if b == max(i - 1, 0):
-                s.dkv[h, chunk(i), :] = both
+                s.gact[key_sums(h, i)] = both
             else:
-                s.dkv[h, chunk(i), :] += both
+                s.gact[key_sums(h, i)] += both
             if i == window(b)[-1]:
                 keys = s.kta[h, 0:HD, window(b)[0] * BLK : (i + 1) * BLK]
                 grad_queries[h] = grad_queries[h] + nn(
@@ -784,7 +861,7 @@
     def keys_back(b):
         for h in range(HEADS):
             rows = slice(h * HD, (h + 1) * HD)
-            both = jnp.transpose(s.dkv[h, chunk(b), :])
+            both = jnp.transpose(s.gact[key_sums(h, b)])
             head_back((both[0:HD] + s.dkx[rows, chunk(b)]) * 0.125, 1, h, b)
             grad_value = both[HD:] + s.dvx[rows, chunk(b)]
             s.gproj[2 * W + h * HD : 2 * W + (h + 1) * HD, chunk(b)] = grad_value.astype(BF)
@@ -799,12 +876,29 @@
             s.vec[1:2, :] += jnp.sum(part, axis=0, keepdims=True)
         ar4.s1(b)
 
+    def side_mlp(b):
+        side_pass(b).wait_recv()
+        rows = slice(b * BLK, (b + 1) * BLK)
+        s.big0[...] = nn(s.n2s[rows, :], s.up[...])
+        for i in range(BLK // 8):
+            out = slice(b * BLK + i * 8, b * BLK + (i + 1) * 8)
+            pre = s.big0[i * 8 : (i + 1) * 8, :]
+            half = 0.5 + 0.5 * jnp.tanh(pre * (GELU_A + GELU_B * (pre * pre)))
+            s.active[out, :] = (pre * half).astype(BF)
+        s.gpre[rows, :] = nn(s.active[rows, :], s.dn[...]).astype(BF)
+        ar2.d1_side(b).start()
+
+    def pass_side(b):
+        side_norm(b).wait_recv()
+        side_pass(b).start()
+
     second_back(0)
     s.m0[:, left] = tn(s.normed2[...], s.gpre[:, left]).astype(BF)
     wide(wide_2[:1], "step1")
     attend_back(0)
     second_back(1)
     s.m0[:, right] = tn(s.normed2[...], s.gpre[:, right]).astype(BF)
+    wide(wide_1, "step1b")
     wide(wide_2[1:], "step1")
     ar2.s2(0)
     attend_back(1)
@@ -814,16 +908,17 @@
     ar2.s2(1)
     attend_back(2)
     keys_back(1)
+    second_back(3)
+    wide(wide_2, "step1b")
     wide(wide_1, "step2")
-    second_back(3)
     first_part(1)
     attend_back(3)
     keys_back(2)
     keys_back(3)
     ar4.s2(0)
-    wide(wide_2, "step2")
     s.m2[0 : 3 * W, left] = nn(s.gproj[...], s.normed[:, left]).astype(BF)
     wide(wide_3[:1], "step1")
+    wide(wide_2, "step2")
     s.m2[0 : 3 * W, right] = nn(s.gproj[...], s.normed[:, right]).astype(BF)
     wide(wide_3[1:], "step1")
     wide(wide_1, "step3")
@@ -837,8 +932,11 @@
     vec_c.start()
     wide(wide_2, "step3")
     ar4.s2(1)
+    wide(wide_3, "step1b")
     mlp_part(CH - 1)
     ar2.s1(CH - 1)
+    for b in range(SIDE, CH):
+        pass_side(b)
 
     def layer_out(b):
         ar2.d2(b).wait_recv()
@@ -849,7 +947,7 @@
     def grad_tokens(b):
         ar4.d2(b).wait_recv()
         hat, rstd = moments(s.x[ar4.mine(b), :].astype(F32))
-        s.r24[b] = (s.gm[b] + norm_back(ar4.total(b) * ag, hat, rstd)).astype(BF)
+        s.r24[b] = (s.gact[b * HALF : (b + 1) * HALF, :] + norm_back(ar4.total(b) * ag, hat, rstd)).astype(BF)
         ar4.d3(b).start()
         gt_copy(b).start()
 
@@ -859,14 +957,14 @@
     s.rvx[k.x] = s.v1[...]
     for copy in vec_x:
         copy.start()
-    layer_out(0)
+    ar4.s2(2)
     wide(wide_1, "step4")
+    side_mlp(2)
     wide(wide_2, "step4")
-    layer_out(1)
-    ar2.s2(2)
+    side_mlp(3)
+    ar2.s2_side(2)
     wide(wide_3, "step2")
-    for copy in vec_x:
-        copy.wait_recv()
+    k.await_recvs(s.rvx.at[pl.ds(0, 3)], vec_sem + 1)
     s.v2[...] = (s.rvx[0] + s.rvx[1]) + (s.rvx[2] + s.rvx[3])
     s.rvy[k.y] = s.v2[...]
     for copy in vec_y:
@@ -874,45 +972,44 @@
     wide(wide_1, "step5")
     for d in (1, 3):
         wide(wide_1, "step6", d)
+    ar2.s2_side(3)
+    ar2.s2(2)
+    ar2.s2(3)
+    layer_out(0)
     wide(wide_2, "step5")
     for d in (1, 3):
         wide(wide_2, "step6", d)
+    layer_out(1)
     wide(wide_3, "step3")
-    for copy in vec_y:
-        copy.wait_recv()
+    k.await_recvs(s.rvy.at[pl.ds(0, 3)], vec_sem + 2)
     s.v3[...] = (s.rvy[0] + s.rvy[1]) + (s.rvy[2] + s.rvy[3])
     vec_z.start()
-    ar4.s2(2)
-    ar2.s2(3)
+    ar4.s2(3)
     grad_tokens(0)
+    wide(wide_1, "step7")
     wide(wide_3, "step4")
-    wide(wide_1, "step7")
     wide(wide_2, "step7")
     vec_z.wait_recv()
     s.v4[...] = s.v3[...] + s.rvz[1]
     vec_l.start()
-    ar4.s2(3)
     grad_tokens(1)
+    wide(wide_3, "step5")
     layer_out(2)
-    wide(wide_3, "step5")
+    grad_tokens(2)
+    layer_out(3)
     vec_l.wait_recv()
     vec_out[...] = s.v4[...] + jnp.where(upper, s.rvz[2], 0.0)
-    grad_tokens(2)
-    layer_out(3)
     grad_tokens(3)
 
-    for b in range(CH):
-        ar2.d3(b).wait_recv()
-        ar4.d3(b).wait_recv()
-        lo_copy(b).wait()
-        gt_copy(b).wait()
-        mix_mate(b).wait_send()
-        mix_z(b).wait_send()
-        mix_pass(b).wait_send()
+    half = pl.ds(0, T // 2)
+    k.copy(s.p2.at[half], lo_out.at[half], out_sem).wait()
+    k.copy(s.p4.at[half], gt_out.at[half], out_sem + 1).wait()
     for item in (ar2, ar3, ar4, *wide_1, *wide_2, *wide_3):
         item.finish()
-    for copy in [*wo_sends, wo_pass, *vec_x, *vec_y, vec_z, vec_c, vec_l]:
-        copy.wait_send()
+    k.await_sends(s.wo.at[pl.ds(0, 3 * W)], wo_send)
+    k.await_sends(s.mixed.at[pl.ds(0, 3 * W)], mix_send)
+    k.await_sends(s.n2s.at[pl.ds(0, (CH - SIDE) * BLK)], side_send)
+    k.await_sends(s.big0.at[pl.ds(0, 72)], vec_send)
 
 
 PARTS = 4
@@ -974,8 +1071,8 @@
         out_specs=(any_spec, any_spec, any_spec, any_spec, any_spec, vmem),
         scratch_shapes=[pltpu.VMEM(shape, dtype) for shape, dtype in SCRATCH.values()]
         + [
-            pltpu.SemaphoreType.DMA((NSEM,)),
-            pltpu.SemaphoreType.DMA((NSEM,)),
+            pltpu.SemaphoreType.DMA((NSEND,)),
+            pltpu.SemaphoreType.DMA((NRECV,)),
             pltpu.SemaphoreType.DMA((NLOC,)),
         ],
         compiler_params=pltpu.CompilerParams(

time: 92.9 us -> 89.3 us (0.961)
  Pallas kernels: 90.7 us -> 87.6 us
    pallas_call x1, Pallas kernels: 83.7 us -> 80.6 us  [body(): pl.pallas_call(kernel, out_shape=(jax.ShapeDtypeStruct((T, D), BF), jax.S...]
where the time goes in v5:
time: 89.3 us; the launch traced here: 89.1 us
  Pallas kernels  87.6 us (98%)
  between operations  1.48 us (2%)
    pallas_call x1, Pallas kernels, body(): pl.pallas_call(kernel, out_shape=(jax.ShapeDtypeStruct((T, D), BF), jax.S...  80.6 us
    pallas_call x1, Pallas kernels, body(): pl.pallas_call(finish, out_shape=(jax.ShapeDtypeStruct((T, D), BF), jax.S...  7.02 us

profile of v5, /device:TPU:0, one launch (start us, length us, event | category | flops | bytes accessed | tf_op | source)
XLA Modules:
  0.0 89.1 jit_solution(3163935359583721879)
XLA Ops:
  1.3 80.6 %shard_map.229 = (bf16[1024,768]{1,0:T(8,128)(2,1)}, bf16[1024,768]{1,0:T(8,128)(2,1)}, bf16[768,768]{1,0:T(8,128)(2,1)}, bf16[768,768]{1,0:T(8,128)(2,1)}, bf16[768,768]{1,0:T(8,128)(2,1)}, /*index=5*/f32[8,768]{1,0:T(8,128)}) custom-call(bf16[1024,768]{1,0:T(8,128)(2,1)} %x_in.1, bf16[1024,768]{1,0:T(8,128)(2,1)} %dy_in.1, s32[1,1024]{1,0:T(1,128)} %seg_in.1, ...), custom_call_target="tpu_custom_call" | custom-call | flops 14000000000 | bytes 20971520 | tf_op jit(solution)/shard_map/pallas_call | solution.py:1060
  81.9 7.0 %shard_map.230 = (bf16[1024,768]{1,0:T(8,128)(2,1)}, bf16[1024,768]{1,0:T(8,128)(2,1)}, f32[3,192,768]{2,1,0:T(8,128)}, f32[192]{0:T(256)}, f32[192]{0:T(256)}, ...) custom-call(bf16[1024,768]{1,0:T(8,128)(2,1)} %get-tuple-element.30., ...), custom_call_target="tpu_custom_call" | custom-call | bytes 17825792 | tf_op jit(solution)/shard_map/pallas_call | solution.py:1085

commit v6 on v5

--- a/solution.py
+++ b/solution.py
@@ -140,17 +140,17 @@
     if _s in RELAYED:
         SCRATCH["nb" + _s] = ((2, 192, _w), BF)
 
-NSEND, NRECV, NLOC = 29, 101, 24
+NSEND, NRECV, NLOC = 20, 95, 25
 
 
 class Wide:
-    def __init__(self, k, name, mat, cols, out, first, second):
+    def __init__(self, k, send, name, mat, cols, out, first, second):
         self.k, self.s, self.mat, self.cols, self.out = k, k.s, mat, cols, out
         self.name = name
         self.first, self.second = first, second
         self.u, self.t = k.coord(first), k.coord(second)
         self.relayed = name in RELAYED
-        self.send = k.sends(3)
+        self.send = send
         self.recv = k.recvs(7 if self.relayed else 8)
         self.local = k.locals(1)
 
@@ -292,16 +292,17 @@
 
     def finish(self):
         k = self.k
-        some, most = (pl.ds(0, 336), self.cols), (pl.ds(0, 576), self.cols)
+        most = (pl.ds(0, 576), self.cols)
         if self.relayed:
             k.await_recvs(self.out.at[pl.ds(0, 192), self.cols], self.recv + 6)
             k.copy(self.mat.at[most], self.out.at[most], self.local).wait()
         else:
             k.await_recvs(self.out.at[most], self.recv + 7)
             self.own().wait()
-        k.await_sends(self.mat.at[most], self.send)
-        k.await_sends(self.mat.at[some], self.send + 1)
-        k.await_sends(self.mat.at[most], self.send + 2)
+        if self.first == "x":
+            k.await_sends(self.mat.at[pl.ds(0, 576)], self.send)
+            k.await_sends(self.mat.at[pl.ds(0, 336)], self.send + 1)
+            k.await_sends(self.mat.at[pl.ds(0, 576)], self.send + 2)
 
 
 class Narrow:
@@ -468,7 +469,8 @@
     s = Names()
     for name, ref in zip(SCRATCH, scratch):
         setattr(s, name, ref)
-    k = Kernel(s, *scratch[len(SCRATCH) :])
+    pad_smem, *semaphores = scratch[len(SCRATCH) :]
+    k = Kernel(s, *semaphores)
     n, core = k.n, k.core
 
     own_wo = s.wo.at[at(n * W, W, W)]
@@ -490,6 +492,7 @@
         (qg_in, s.qg),
         (kg_in, s.kg),
         (seg_in, s.seg),
+        (pad_in, pad_smem),
         (mg_in, s.mg),
         (ms_in, s.msh),
     ]
@@ -506,17 +509,17 @@
     for peer in peers:
         pl.semaphore_signal(barrier, inc=1, device_id=peer, device_id_type=MESH)
 
-    wo_send, wo_recv = k.sends(1), k.recvs(4)
+    wo_send, wo_recv = k.sends(1), k.recvs(2)
     own_low = s.wo.at[at(n * W, W // 3, W // 3)]
     own_high = s.wo.at[at(n * W + W // 3, 2 * W // 3, W // 3)]
     other_wo = s.wo.at[at(k.n2 * W, W, W)]
     wo_sends = [
         k.remote(own_wo, own_wo, wo_send, wo_recv, k.mate),
         k.remote(own_low, own_low, wo_send, wo_recv + 1, k.zlo),
-        k.remote(own_high, own_high, wo_send, wo_recv + 2, k.side),
+        k.remote(own_high, own_high, wo_send, wo_recv + 1, k.side),
     ]
-    wo_pass = k.remote(other_wo, other_wo, wo_send, wo_recv + 3, k.mate)
-    mix_send, mix_sem = k.sends(1), k.recvs(3 * CH)
+    wo_pass = k.remote(other_wo, other_wo, wo_send, wo_recv, k.mate)
+    mix_send, mix_sem = k.sends(1), k.recvs(2 * CH)
 
     def mix_mate(b):
         ref = s.mixed.at[at(n * W, W, W), chunk(b)]
@@ -528,15 +531,16 @@
 
     def mix_pass(b):
         ref = s.mixed.at[at(k.n2 * W, W, W), chunk(b)]
-        return k.remote(ref, ref, mix_send, mix_sem + 2 * CH + b, k.mate)
+        return k.remote(ref, ref, mix_send, mix_sem + b, k.mate)
 
     ar2 = Narrow(k, s.p2, s.r12, s.r22, lambda b, rows: (s.r22.at[b], lo_out.at[rows]), side=(s.gpre, s.r12s))
     ar3 = Narrow(k, s.p3, s.r13, s.r23, lambda b, rows: (s.gattn.at[rows], s.gattn.at[rows]), joint=False)
     ar4 = Narrow(k, s.p4, s.r14, s.r24, lambda b, rows: (s.r24.at[b], gt_out.at[rows]))
     low_cols, high_cols = pl.ds(0, D // 2), pl.ds(D // 2, D // 2)
-    wide_1 = Wide(k, "a", s.m1, low_cols, gdn_out, "x", "y"), Wide(k, "b", s.m1, high_cols, gdn_out, "y", "x")
-    wide_2 = Wide(k, "c", s.m0, low_cols, gup_out, "x", "y"), Wide(k, "d", s.m0, high_cols, gup_out, "y", "x")
-    wide_3 = Wide(k, "e", s.m2, low_cols, g2_out, "x", "y"), Wide(k, "f", s.m2, high_cols, g2_out, "y", "x")
+    wide_sends = [k.sends(3) for _ in range(3)]
+    wide_1 = Wide(k, wide_sends[0], "a", s.m1, low_cols, gdn_out, "x", "y"), Wide(k, wide_sends[0], "b", s.m1, high_cols, gdn_out, "y", "x")
+    wide_2 = Wide(k, wide_sends[1], "c", s.m0, low_cols, gup_out, "x", "y"), Wide(k, wide_sends[1], "d", s.m0, high_cols, gup_out, "y", "x")
+    wide_3 = Wide(k, wide_sends[2], "e", s.m2, low_cols, g2_out, "x", "y"), Wide(k, wide_sends[2], "f", s.m2, high_cols, g2_out, "y", "x")
 
     def wide(pair, step, *args):
         for item in pair:
@@ -571,8 +575,6 @@
         return k.copy(s.r24.at[b], gt_out.at[ar4.mine(b)], out_sem + 1)
 
 
-    limit = T - pad_in[0]
-
     for load in smalls:
         load.wait()
     load_x.wait()
@@ -588,6 +590,8 @@
 
     lanes = lax.broadcasted_iota(jnp.int32, (1, BLK), 1)
     subs = lax.broadcasted_iota(jnp.int32, (HD, BLK), 0)
+
+    limit = T - pad_smem[0]
 
     def padded(b):
         return jnp.where(lanes + b * BLK >= limit, 1.0, 0.0)
@@ -680,28 +684,29 @@
         load.wait()
     for load in loads[6:]:
         load.start()
-    for b in range(CH):
-        project(b)
-    for b in range(CH):
+    project(0)
+    project(1)
+    attend(0)
+    send_mixed(0)
+    project(2)
+    project(3)
+    for b in range(1, CH):
         attend(b)
         send_mixed(b)
 
     load_dy.wait()
     load_dn.wait()
     s.gact[0 : T // 2, :] = nt(s.dy[0 : T // 2, :], s.dn[...])
-    for copy in wo_sends[1:]:
-        copy.wait_recv()
+    k.await_recvs(other_wo, wo_recv + 1)
     wo_pass.start()
     s.gact[T // 2 :, :] = nt(s.dy[T // 2 :, :], s.dn[...])
     load_up.wait()
     mix_z(0).wait_recv()
     mix_pass(0).start()
-    wo_sends[0].wait_recv()
-    wo_pass.wait_recv()
+    k.await_recvs(s.wo.at[pl.ds(0, 2 * W)], wo_recv)
 
     def wait_mixed(b):
-        mix_mate(b).wait_recv()
-        mix_pass(b).wait_recv()
+        k.await_recvs(s.mixed.at[pl.ds(0, 2 * W), chunk(b)], mix_sem + b)
 
     def out_product(b):
         s.big0[...] = tn(s.mixed[:, chunk(b)], s.wo[...])
@@ -736,6 +741,7 @@
     def up_product(b):
         s.big1[...] = nn(s.normed2[b * BLK : (b + 1) * BLK, :], s.up[...])
 
+    left, right = slice(0, D // 2), slice(D // 2, D)
     wait_mixed(0)
     out_product(0)
     pass_mixed(1)
@@ -744,10 +750,15 @@
     for b in range(CH):
         rows = slice(b * BLK, (b + 1) * BLK)
         gelu(b)
-        if b >= 1:
+        if 1 <= b <= SIDE:
             ar2.s1(b - 1)
         if b == 3:
             ar3.s2(2)
+        if b == CH - 1:
+            s.m1[:, left] = tn(s.active[...], s.dy[:, left]).astype(BF)
+            wide(wide_1[:1], "step1")
+            s.m1[:, right] = tn(s.active[...], s.dy[:, right]).astype(BF)
+            wide(wide_1[1:], "step1")
         s.p3[rows, :] = nt(s.gpre[rows, :], s.up[...]).astype(BF)
         if b >= 1 and b + 1 < CH:
             second_norm(b + 1)
@@ -762,7 +773,8 @@
             ar3.s2(0)
         if b + 1 < CH:
             up_product(b + 1)
-            mlp_part(b)
+            if b < SIDE:
+                mlp_part(b)
         if b + 2 < CH:
             wait_mixed(b + 2)
             out_product(b + 2)
@@ -770,13 +782,6 @@
             pass_mixed(b + 3)
         if b == 1:
             ar3.s2(1)
-
-    left, right = slice(0, D // 2), slice(D // 2, D)
-    s.m1[:, left] = tn(s.active[...], s.dy[:, left]).astype(BF)
-    ar3.s2(CH - 1)
-    wide(wide_1[:1], "step1")
-    s.m1[:, right] = tn(s.active[...], s.dy[:, right]).astype(BF)
-    wide(wide_1[1:], "step1")
 
     def second_back(b):
         ar3.d2(b).wait_recv()
@@ -893,35 +898,37 @@
         side_pass(b).start()
 
     second_back(0)
+    ar3.s2(CH - 1)
     s.m0[:, left] = tn(s.normed2[...], s.gpre[:, left]).astype(BF)
     wide(wide_2[:1], "step1")
+    s.m0[:, right] = tn(s.normed2[...], s.gpre[:, right]).astype(BF)
+    wide(wide_2[1:], "step1")
     attend_back(0)
     second_back(1)
-    s.m0[:, right] = tn(s.normed2[...], s.gpre[:, right]).astype(BF)
     wide(wide_1, "step1b")
-    wide(wide_2[1:], "step1")
     ar2.s2(0)
+    mlp_part(2)
     attend_back(1)
     keys_back(0)
     second_back(2)
+    wide(wide_2, "step1b")
     first_part(0)
     ar2.s2(1)
     attend_back(2)
     keys_back(1)
     second_back(3)
-    wide(wide_2, "step1b")
     wide(wide_1, "step2")
     first_part(1)
     attend_back(3)
     keys_back(2)
     keys_back(3)
-    ar4.s2(0)
+    wide(wide_2, "step2")
     s.m2[0 : 3 * W, left] = nn(s.gproj[...], s.normed[:, left]).astype(BF)
     wide(wide_3[:1], "step1")
-    wide(wide_2, "step2")
+    wide(wide_1, "step3")
     s.m2[0 : 3 * W, right] = nn(s.gproj[...], s.normed[:, right]).astype(BF)
     wide(wide_3[1:], "step1")
-    wide(wide_1, "step3")
+    ar2.s1(2)
     first_part(2)
     first_part(3)
     for which in range(2):
@@ -930,13 +937,15 @@
         s.vec[4 + which : 5 + which, 0:W] = jnp.sum(jnp.transpose(both), axis=0, keepdims=True)
     s.vecs[...] = s.vec[...]
     vec_c.start()
+    for b in range(SIDE, CH):
+        pass_side(b)
     wide(wide_2, "step3")
+    ar4.s2(0)
+    wide(wide_1, "step4")
+    wide(wide_3, "step1b")
     ar4.s2(1)
-    wide(wide_3, "step1b")
     mlp_part(CH - 1)
     ar2.s1(CH - 1)
-    for b in range(SIDE, CH):
-        pass_side(b)
 
     def layer_out(b):
         ar2.d2(b).wait_recv()
@@ -957,12 +966,8 @@
     s.rvx[k.x] = s.v1[...]
     for copy in vec_x:
         copy.start()
-    ar4.s2(2)
-    wide(wide_1, "step4")
     side_mlp(2)
     wide(wide_2, "step4")
-    side_mlp(3)
-    ar2.s2_side(2)
     wide(wide_3, "step2")
     k.await_recvs(s.rvx.at[pl.ds(0, 3)], vec_sem + 1)
     s.v2[...] = (s.rvx[0] + s.rvx[1]) + (s.rvx[2] + s.rvx[3])
@@ -972,26 +977,29 @@
     wide(wide_1, "step5")
     for d in (1, 3):
         wide(wide_1, "step6", d)
-    ar2.s2_side(3)
-    ar2.s2(2)
-    ar2.s2(3)
-    layer_out(0)
+    side_mlp(3)
+    ar2.s2_side(2)
     wide(wide_2, "step5")
     for d in (1, 3):
         wide(wide_2, "step6", d)
-    layer_out(1)
+    ar2.s2_side(3)
     wide(wide_3, "step3")
     k.await_recvs(s.rvy.at[pl.ds(0, 3)], vec_sem + 2)
     s.v3[...] = (s.rvy[0] + s.rvy[1]) + (s.rvy[2] + s.rvy[3])
     vec_z.start()
-    ar4.s2(3)
+    ar4.s2(2)
+    ar2.s2(2)
+    ar2.s2(3)
+    layer_out(0)
+    layer_out(1)
     grad_tokens(0)
+    wide(wide_3, "step4")
     wide(wide_1, "step7")
-    wide(wide_3, "step4")
-    wide(wide_2, "step7")
     vec_z.wait_recv()
     s.v4[...] = s.v3[...] + s.rvz[1]
     vec_l.start()
+    ar4.s2(3)
+    wide(wide_2, "step7")
     grad_tokens(1)
     wide(wide_3, "step5")
     layer_out(2)
@@ -1054,7 +1062,6 @@
 def body(*args):
     any_spec = pl.BlockSpec(memory_space=pl.ANY)
     vmem = pl.BlockSpec(memory_space=pltpu.VMEM)
-    smem = pl.BlockSpec(memory_space=pltpu.SMEM)
     args = list(args)
     args[4] = jnp.swapaxes(args[4], 1, 2).reshape(3 * W, D)
     out = pl.pallas_call(
@@ -1067,10 +1074,11 @@
             jax.ShapeDtypeStruct((4 * W, D), BF),
             jax.ShapeDtypeStruct((8, D), F32),
         ),
-        in_specs=[any_spec] * 3 + [smem] + [any_spec] * 10,
+        in_specs=[any_spec] * 14,
         out_specs=(any_spec, any_spec, any_spec, any_spec, any_spec, vmem),
         scratch_shapes=[pltpu.VMEM(shape, dtype) for shape, dtype in SCRATCH.values()]
         + [
+            pltpu.SMEM((1,), jnp.int32),
             pltpu.SemaphoreType.DMA((NSEND,)),
             pltpu.SemaphoreType.DMA((NRECV,)),
             pltpu.SemaphoreType.DMA((NLOC,)),

time: 89.3 us -> 86.2 us (0.965)
  Pallas kernels: 87.6 us -> 84.5 us
    pallas_call x1, Pallas kernels: 80.6 us -> 77.5 us  [body(): pl.pallas_call(kernel, out_shape=(jax.ShapeDtypeStruct((T, D), BF), jax.S...]
where the time goes in v6:
time: 86.2 us; the launch traced here: 86 us
  Pallas kernels  84.5 us (98%)
  between operations  1.48 us (2%)
    pallas_call x1, Pallas kernels, body(): pl.pallas_call(kernel, out_shape=(jax.ShapeDtypeStruct((T, D), BF), jax.S...  77.5 us
    pallas_call x1, Pallas kernels, body(): pl.pallas_call(finish, out_shape=(jax.ShapeDtypeStruct((T, D), BF), jax.S...  7.02 us

profile of v6, /device:TPU:0, one launch (start us, length us, event | category | flops | bytes accessed | tf_op | source)
XLA Modules:
  0.0 86.0 jit_solution(27199581120520855)
XLA Ops:
  1.3 77.5 %shard_map.229 = (bf16[1024,768]{1,0:T(8,128)(2,1)}, bf16[1024,768]{1,0:T(8,128)(2,1)}, bf16[768,768]{1,0:T(8,128)(2,1)}, bf16[768,768]{1,0:T(8,128)(2,1)}, bf16[768,768]{1,0:T(8,128)(2,1)}, /*index=5*/f32[8,768]{1,0:T(8,128)}) custom-call(bf16[1024,768]{1,0:T(8,128)(2,1)} %x_in.1, bf16[1024,768]{1,0:T(8,128)(2,1)} %dy_in.1, s32[1,1024]{1,0:T(1,128)} %seg_in.1, ...), custom_call_target="tpu_custom_call" | custom-call | flops 14000000000 | bytes 20971520 | tf_op jit(solution)/shard_map/pallas_call | solution.py:1067
  78.8 7.0 %shard_map.230 = (bf16[1024,768]{1,0:T(8,128)(2,1)}, bf16[1024,768]{1,0:T(8,128)(2,1)}, f32[3,192,768]{2,1,0:T(8,128)}, f32[192]{0:T(256)}, f32[192]{0:T(256)}, ...) custom-call(bf16[1024,768]{1,0:T(8,128)(2,1)} %get-tuple-element.30., ...), custom_call_target="tpu_custom_call" | custom-call | bytes 17825792 | tf_op jit(solution)/shard_map/pallas_call | solution.py:1093

commit v7 on v6

--- a/solution.py
+++ b/solution.py
@@ -699,10 +699,10 @@
     s.gact[0 : T // 2, :] = nt(s.dy[0 : T // 2, :], s.dn[...])
     k.await_recvs(other_wo, wo_recv + 1)
     wo_pass.start()
+    mix_z(0).wait_recv()
+    mix_pass(0).start()
     s.gact[T // 2 :, :] = nt(s.dy[T // 2 :, :], s.dn[...])
     load_up.wait()
-    mix_z(0).wait_recv()
-    mix_pass(0).start()
     k.await_recvs(s.wo.at[pl.ds(0, 2 * W)], wo_recv)
 
     def wait_mixed(b):
@@ -898,9 +898,9 @@
         side_pass(b).start()
 
     second_back(0)
-    ar3.s2(CH - 1)
     s.m0[:, left] = tn(s.normed2[...], s.gpre[:, left]).astype(BF)
     wide(wide_2[:1], "step1")
+    ar3.s2(CH - 1)
     s.m0[:, right] = tn(s.normed2[...], s.gpre[:, right]).astype(BF)
     wide(wide_2[1:], "step1")
     attend_back(0)
@@ -941,8 +941,8 @@
         pass_side(b)
     wide(wide_2, "step3")
     ar4.s2(0)
+    wide(wide_3, "step1b")
     wide(wide_1, "step4")
-    wide(wide_3, "step1b")
     ar4.s2(1)
     mlp_part(CH - 1)
     ar2.s1(CH - 1)
@@ -967,26 +967,23 @@
     for copy in vec_x:
         copy.start()
     side_mlp(2)
+    wide(wide_3, "step2")
     wide(wide_2, "step4")
-    wide(wide_3, "step2")
+    wide(wide_1, "step5")
+    for d in (1, 3):
+        wide(wide_1, "step6", d)
+    side_mlp(3)
+    ar2.s2_side(2)
     k.await_recvs(s.rvx.at[pl.ds(0, 3)], vec_sem + 1)
     s.v2[...] = (s.rvx[0] + s.rvx[1]) + (s.rvx[2] + s.rvx[3])
     s.rvy[k.y] = s.v2[...]
     for copy in vec_y:
         copy.start()
-    wide(wide_1, "step5")
-    for d in (1, 3):
-        wide(wide_1, "step6", d)
-    side_mlp(3)
-    ar2.s2_side(2)
     wide(wide_2, "step5")
     for d in (1, 3):
         wide(wide_2, "step6", d)
     ar2.s2_side(3)
     wide(wide_3, "step3")
-    k.await_recvs(s.rvy.at[pl.ds(0, 3)], vec_sem + 2)
-    s.v3[...] = (s.rvy[0] + s.rvy[1]) + (s.rvy[2] + s.rvy[3])
-    vec_z.start()
     ar4.s2(2)
     ar2.s2(2)
     ar2.s2(3)
@@ -995,13 +992,16 @@
     grad_tokens(0)
     wide(wide_3, "step4")
     wide(wide_1, "step7")
-    vec_z.wait_recv()
-    s.v4[...] = s.v3[...] + s.rvz[1]
-    vec_l.start()
+    k.await_recvs(s.rvy.at[pl.ds(0, 3)], vec_sem + 2)
+    s.v3[...] = (s.rvy[0] + s.rvy[1]) + (s.rvy[2] + s.rvy[3])
+    vec_z.start()
     ar4.s2(3)
     wide(wide_2, "step7")
     grad_tokens(1)
     wide(wide_3, "step5")
+    vec_z.wait_recv()
+    s.v4[...] = s.v3[...] + s.rvz[1]
+    vec_l.start()
     layer_out(2)
     grad_tokens(2)
     layer_out(3)

time: 86.2 us -> 85.1 us (0.987)
  Pallas kernels: 84.5 us -> 83.4 us
    pallas_call x1, Pallas kernels: 77.5 us -> 76.4 us  [body(): pl.pallas_call(kernel, out_shape=(jax.ShapeDtypeStruct((T, D), BF), jax.S...]
where the time goes in v7:
time: 85.1 us; the launch traced here: 84.9 us
  Pallas kernels  83.4 us (98%)
  between operations  1.48 us (2%)
    pallas_call x1, Pallas kernels, body(): pl.pallas_call(kernel, out_shape=(jax.ShapeDtypeStruct((T, D), BF), jax.S...  76.4 us
    pallas_call x1, Pallas kernels, body(): pl.pallas_call(finish, out_shape=(jax.ShapeDtypeStruct((T, D), BF), jax.S...  7.02 us

profile of v7, /device:TPU:0, one launch (start us, length us, event | category | flops | bytes accessed | tf_op | source)
XLA Modules:
  0.0 84.9 jit_solution(16322774872104811207)
XLA Ops:
  1.3 76.4 %shard_map.229 = (bf16[1024,768]{1,0:T(8,128)(2,1)}, bf16[1024,768]{1,0:T(8,128)(2,1)}, bf16[768,768]{1,0:T(8,128)(2,1)}, bf16[768,768]{1,0:T(8,128)(2,1)}, bf16[768,768]{1,0:T(8,128)(2,1)}, /*index=5*/f32[8,768]{1,0:T(8,128)}) custom-call(bf16[1024,768]{1,0:T(8,128)(2,1)} %x_in.1, bf16[1024,768]{1,0:T(8,128)(2,1)} %dy_in.1, s32[1,1024]{1,0:T(1,128)} %seg_in.1, ...), custom_call_target="tpu_custom_call" | custom-call | flops 14000000000 | bytes 20971520 | tf_op jit(solution)/shard_map/pallas_call | solution.py:1067
  77.7 7.0 %shard_map.230 = (bf16[1024,768]{1,0:T(8,128)(2,1)}, bf16[1024,768]{1,0:T(8,128)(2,1)}, f32[3,192,768]{2,1,0:T(8,128)}, f32[192]{0:T(256)}, f32[192]{0:T(256)}, ...) custom-call(bf16[1024,768]{1,0:T(8,128)(2,1)} %get-tuple-element.30., ...), custom_call_target="tpu_custom_call" | custom-call | bytes 17825792 | tf_op jit(solution)/shard_map/pallas_call | solution.py:1093

commit v8 on v7

--- a/solution.py
+++ b/solution.py
@@ -140,19 +140,24 @@
     if _s in RELAYED:
         SCRATCH["nb" + _s] = ((2, 192, _w), BF)
 
-NSEND, NRECV, NLOC = 20, 95, 25
+NSEND, NRECV, NLOC = 20, 78, 17
 
 
 class Wide:
-    def __init__(self, k, send, name, mat, cols, out, first, second):
+    def __init__(self, k, send, recv, local, name, mat, cols, out, first, second):
         self.k, self.s, self.mat, self.cols, self.out = k, k.s, mat, cols, out
         self.name = name
         self.first, self.second = first, second
         self.u, self.t = k.coord(first), k.coord(second)
         self.relayed = name in RELAYED
         self.send = send
-        self.recv = k.recvs(7 if self.relayed else 8)
-        self.local = k.locals(1)
+        self.lead = first == "x"
+        self.recv, self.own_recv = recv, None if self.relayed else k.recvs(3)
+        self.local = local
+
+    def await_both(self, rows, recv):
+        if self.lead:
+            self.k.await_recvs(self.mat.at[pl.ds(0, rows)], self.recv + recv)
 
     def ref(self, what):
         return getattr(self.s, what + self.name)
@@ -192,7 +197,7 @@
 
     def ag2(self, d):
         piece = self.ref("rr").at[at(self.t * 48, 48, 48)]
-        recv = self.recv + 4 + (0 if self.relayed else d - 1)
+        recv = self.recv + 4 if self.relayed else self.own_recv + d - 1
         return self.k.remote(piece, piece, self.send + 1, recv, self.k.along(self.second, d))
 
     def rows_out(self, u, start=0, size=192):
@@ -210,7 +215,7 @@
             self.ref("rr").at[at(start, 48, 48)],
             self.out.at[at(self.u * 192 + start, 48, 48), self.cols],
             self.send + 2,
-            self.recv + 7,
+            self.recv + 6,
             self.k.along(self.first, d),
         )
 
@@ -236,14 +241,14 @@
             self.rs1(i).start()
 
     def step1b(self):
-        self.k.await_recvs(self.ref("ra"), self.recv)
+        self.await_both(192, 0)
         for i, (q, part) in enumerate(((1, 0), (-1, 1))):
             own = self.mat[self.half(q, part), self.cols].astype(F32)
             self.ref("rb")[i] = (own + self.ref("ra")[i].astype(F32)).astype(BF)
             self.rs1(4 + i).start()
 
     def step2(self):
-        self.k.await_recvs(self.ref("rs1"), self.recv + 1)
+        self.await_both(384, 1)
         rs1, s1 = self.ref("rs1"), self.ref("s1")
         for i, (one, two) in enumerate(((1, 2), (0, 3))):
             total = self.mat[self.half(0, i), self.cols].astype(F32)
@@ -253,7 +258,7 @@
             self.rs2(d).start()
 
     def step3(self):
-        self.k.await_recvs(self.ref("rs2"), self.recv + 2)
+        self.await_both(144, 2)
         total = self.ref("s1")[at(self.t * 48, 48, 48), :].astype(F32)
         for d in range(3):
             total = total + self.ref("rs2")[d].astype(F32)
@@ -261,7 +266,7 @@
         self.zz().start()
 
     def step4(self):
-        self.zz().wait_recv()
+        self.await_both(48, 3)
         total = self.ref("s2")[...].astype(F32) + self.ref("rz")[...].astype(F32)
         self.ref("rr")[at(self.t * 48, 48, 48), :] = total.astype(BF)
         for d in (2, 1, 3):
@@ -272,7 +277,7 @@
 
     def step5(self):
         if self.relayed:
-            self.k.await_recvs(self.ref("rr").at[pl.ds(0, 144)], self.recv + 4)
+            self.await_both(144, 4)
         else:
             for e in (1, 3, 2):
                 self.ag2(e).wait_recv()
@@ -284,7 +289,7 @@
         self.ag1(d).start()
 
     def step7(self):
-        self.k.await_recvs(self.ref("nb"), self.recv + 5)
+        self.await_both(384, 5)
         for d in (1, 3):
             self.forward(d).start()
         for i in (1, 2):
@@ -294,10 +299,10 @@
         k = self.k
         most = (pl.ds(0, 576), self.cols)
         if self.relayed:
-            k.await_recvs(self.out.at[pl.ds(0, 192), self.cols], self.recv + 6)
+            self.await_both(192, 6)
             k.copy(self.mat.at[most], self.out.at[most], self.local).wait()
         else:
-            k.await_recvs(self.out.at[most], self.recv + 7)
+            self.await_both(576, 6)
             self.own().wait()
         if self.first == "x":
             k.await_sends(self.mat.at[pl.ds(0, 576)], self.send)
@@ -537,10 +542,10 @@
     ar3 = Narrow(k, s.p3, s.r13, s.r23, lambda b, rows: (s.gattn.at[rows], s.gattn.at[rows]), joint=False)
     ar4 = Narrow(k, s.p4, s.r14, s.r24, lambda b, rows: (s.r24.at[b], gt_out.at[rows]))
     low_cols, high_cols = pl.ds(0, D // 2), pl.ds(D // 2, D // 2)
-    wide_sends = [k.sends(3) for _ in range(3)]
-    wide_1 = Wide(k, wide_sends[0], "a", s.m1, low_cols, gdn_out, "x", "y"), Wide(k, wide_sends[0], "b", s.m1, high_cols, gdn_out, "y", "x")
-    wide_2 = Wide(k, wide_sends[1], "c", s.m0, low_cols, gup_out, "x", "y"), Wide(k, wide_sends[1], "d", s.m0, high_cols, gup_out, "y", "x")
-    wide_3 = Wide(k, wide_sends[2], "e", s.m2, low_cols, g2_out, "x", "y"), Wide(k, wide_sends[2], "f", s.m2, high_cols, g2_out, "y", "x")
+    wide_sems = [(k.sends(3), k.recvs(7)) for _ in range(3)]
+    wide_1 = Wide(k, *wide_sems[0], 2, "a", s.m1, low_cols, gdn_out, "x", "y"), Wide(k, *wide_sems[0], 3, "b", s.m1, high_cols, gdn_out, "y", "x")
+    wide_2 = Wide(k, *wide_sems[1], 4, "c", s.m0, low_cols, gup_out, "x", "y"), Wide(k, *wide_sems[1], 5, "d", s.m0, high_cols, gup_out, "y", "x")
+    wide_3 = Wide(k, *wide_sems[2], 6, "e", s.m2, low_cols, g2_out, "x", "y"), Wide(k, *wide_sems[2], 7, "f", s.m2, high_cols, g2_out, "y", "x")
 
     def wide(pair, step, *args):
         for item in pair:
@@ -556,7 +561,7 @@
     ]
     vec_z = k.remote(s.v3, s.rvz.at[1], vec_send, vec_sem + 3, k.zhi)
     vec_l = k.remote(s.v4, s.rvz.at[2], vec_send, vec_sem + 4, k.zlo)
-    out_sem = k.locals(2)
+    out_sem = 0
 
     side_send, side_sem = k.sends(1), k.recvs(2 * (CH - SIDE))
 
@@ -925,9 +930,9 @@
     wide(wide_2, "step2")
     s.m2[0 : 3 * W, left] = nn(s.gproj[...], s.normed[:, left]).astype(BF)
     wide(wide_3[:1], "step1")
-    wide(wide_1, "step3")
     s.m2[0 : 3 * W, right] = nn(s.gproj[...], s.normed[:, right]).astype(BF)
     wide(wide_3[1:], "step1")
+    wide(wide_1, "step3")
     ar2.s1(2)
     first_part(2)
     first_part(3)
@@ -979,11 +984,11 @@
     s.rvy[k.y] = s.v2[...]
     for copy in vec_y:
         copy.start()
+    ar2.s2_side(3)
+    wide(wide_3, "step3")
     wide(wide_2, "step5")
     for d in (1, 3):
         wide(wide_2, "step6", d)
-    ar2.s2_side(3)
-    wide(wide_3, "step3")
     ar4.s2(2)
     ar2.s2(2)
     ar2.s2(3)

time: 85.1 us -> 85 us (level)
  no operation moved by 1% of the time
where the time goes in v8:
time: 85 us; the launch traced here: 84.8 us
  Pallas kernels  83.3 us (98%)
  between operations  1.48 us (2%)
    pallas_call x1, Pallas kernels, body(): pl.pallas_call(kernel, out_shape=(jax.ShapeDtypeStruct((T, D), BF), jax.S...  76.3 us
    pallas_call x1, Pallas kernels, body(): pl.pallas_call(finish, out_shape=(jax.ShapeDtypeStruct((T, D), BF), jax.S...  7.02 us

profile of v8, /device:TPU:0, one launch (start us, length us, event | category | flops | bytes accessed | tf_op | source)
XLA Modules:
  0.0 84.8 jit_solution(9028094183311404973)
XLA Ops:
  1.3 76.3 %shard_map.229 = (bf16[1024,768]{1,0:T(8,128)(2,1)}, bf16[1024,768]{1,0:T(8,128)(2,1)}, bf16[768,768]{1,0:T(8,128)(2,1)}, bf16[768,768]{1,0:T(8,128)(2,1)}, bf16[768,768]{1,0:T(8,128)(2,1)}, /*index=5*/f32[8,768]{1,0:T(8,128)}) custom-call(bf16[1024,768]{1,0:T(8,128)(2,1)} %x_in.1, bf16[1024,768]{1,0:T(8,128)(2,1)} %dy_in.1, s32[1,1024]{1,0:T(1,128)} %seg_in.1, ...), custom_call_target="tpu_custom_call" | custom-call | flops 14000000000 | bytes 20971520 | tf_op jit(solution)/shard_map/pallas_call | solution.py:1072
  77.6 7.0 %shard_map.230 = (bf16[1024,768]{1,0:T(8,128)(2,1)}, bf16[1024,768]{1,0:T(8,128)(2,1)}, f32[3,192,768]{2,1,0:T(8,128)}, f32[192]{0:T(256)}, f32[192]{0:T(256)}, ...) custom-call(bf16[1024,768]{1,0:T(8,128)(2,1)} %get-tuple-element.30., ...), custom_call_target="tpu_custom_call" | custom-call | bytes 17825792 | tf_op jit(solution)/shard_map/pallas_call | solution.py:1098
